TPU v7x, 512 devices: a whole 4x8x8 slice. The times are simulated.
512 devices in a mesh: loop: 16 (over x, z_lo), bulk: 32 (over z_hi, y, core).
Axes of the slice: x: 4, y: 8, z: 8 (z_hi: 2, z_lo: 4; z = z_hi * 4 + z_lo), core: 2. Of those that a mesh axis runs over, the one named last changes fastest.
Arguments:
- series: float32 [16896, 3072], P('loop', 'bulk'), may hold values from -64 to 64
Outputs:
- correlation: float32 [16, 1056, 16896], P(None, 'bulk', 'loop')
All inputs are finite; a program needn't handle non-finite values.
Results may differ from a plain program's by a relative error of at most 0.0011.
Values may be sent and summed in bfloat16 or wider, within the bound.
No kernel may reach another device: no remote copies, remote signals or barrier semaphores. Data moves between devices by JAX's collectives and lax.ppermute only.
A program may use at most 64 MiB of HBM per device.

v0:
```python
import jax
import jax.numpy as jnp
from jax import lax
from jax.sharding import PartitionSpec as P

TIME = 3072


epsilon = 1e-06


def normalize(centered, square_total):
    return (centered * lax.rsqrt(square_total / TIME + epsilon)).astype(jnp.bfloat16)


def contract(first_operand, second_operand):
    product = lax.dot_general(
        first_operand, second_operand, (((1,), (1,)), ((), ())), preferred_element_type=jnp.float32
    )
    return product / TIME


def cycle_gather(own_rows):
    return lax.all_gather(own_rows, "loop", axis=0, tiled=True)


def on_device(series):
    share_rows = series.shape[0] // lax.axis_size("bulk")
    average = lax.psum(jnp.sum(series, axis=1, keepdims=True), "bulk") / TIME
    centered = series - average
    squares = lax.psum(jnp.sum(centered * centered, axis=1, keepdims=True), "bulk")
    zscore = normalize(centered, squares)
    row_series = lax.all_gather(zscore, "bulk", axis=1, tiled=True)
    own_rows = lax.dynamic_slice_in_dim(
        row_series, lax.axis_index("bulk") * share_rows, share_rows, 0
    )
    gathered = contract(cycle_gather(own_rows), row_series)
    return gathered.reshape(lax.axis_size("loop"), share_rows, series.shape[0])


def solution(mesh):
    placed = (P("loop", "bulk"),)
    return jax.shard_map(
        on_device, mesh=mesh, in_specs=placed, out_specs=P(None, "bulk", "loop"), check_vma=False
    )
```

profile of v0, /device:TPU:6, one launch (start us, length us, event | category | flops | bytes accessed | tf_op | source)
XLA Modules:
  0.0 430.0 jit_solution(14525923785989103205)
XLA Ops:
  6.5 0.0 all-gather.4.cloned.1.call-start
  6.5 1.0 reduce_sum.18
  7.6 97.6 %psum.14 = f32[1056,1]{0,1:T(1,128)S(1)} all-reduce(f32[1056,1]{0,1:T(1,128)S(1)} %broadcast_in_dim.6), channel_id=1, replica_groups=mesh['loop'=16,'bulk'=32] {'bulk'}, use_global_device_ids=true, to_apply=%region_1.0 | all-reduce | flops 1056 | bytes 8448 | tf_op jit(solution)/shard_map/psum | solution.py:29
  105.2 1.1 multiply_reduce_fusion
  106.3 86.1 %psum.15 = f32[1056,1]{0,1:T(1,128)S(1)} all-reduce(f32[1056,1]{0,1:T(1,128)S(1)} %broadcast_in_dim.7), channel_id=1, replica_groups=mesh['loop'=16,'bulk'=32] {'bulk'}, use_global_device_ids=true, to_apply=%region_3.0 | all-reduce | flops 1056 | bytes 8448 | tf_op jit(solution)/shard_map/psum | solution.py:31
  192.4 1.7 multiply_convert_fusion
  194.2 0.0 all-gather.4.cloned.1.call-update
  194.2 0.0 all-gather.6.cloned.1.call-start
  194.3 119.1 %all-gather.4.cloned.1.call-done = bf16[1056,3072]{0,1:T(8,128)(2,1)} async-done(((bf16[1056,96]{0,1:T(8,128)(2,1)}), bf16[1056,3072]{0,1:T(8,128)(2,1)}) %all-gather.4.cloned.1.call-update) | async-done | bytes 6488080 | tf_op jit(solution)/shard_map/all_gather | solution.py:33
  313.4 1.7 constant_dynamic-slice_fusion
  315.1 1.0 copy.8
  316.1 0.0 all-gather.6.cloned.1.call-update
  316.2 91.9 %all-gather.6.cloned.1.call-done = bf16[16,33,3072]{2,1,0:T(8,128)(2,1)} async-done(((bf16[1,33,3072]{2,1,0:T(8,128)(2,1)}), bf16[16,33,3072]{2,1,0:T(8,128)(2,1)}) %all-gather.6.cloned.1.call-update) | async-done | bytes 3244048 | tf_op jit(solution)/shard_map/all_gather | solution.py:24
  408.0 2.7 reshape.5
  410.7 8.8 %convolution_multiply_fusion = f32[528,1056]{1,0:T(8,128)} fusion(bf16[528,3072]{1,0:T(8,128)(2,1)S(1)} %reshape.5, bf16[1056,3072]{0,1:T(8,128)(2,1)} %all-gather.4.cloned.1.call-done), kind=kOutput, calls=%fused_computation | convolution fusion | flops 3426255360 | bytes 11962368 | tf_op jit(solution)/shard_map/dot_general | solution.py:17
  419.5 1.8 reshape.3
  421.3 1.9 copy.7
  (4 shorter events, 0.1 us)
Async XLA Ops:
  6.5 306.9 %all-gather.4.cloned.1.call-start = ((), (), s32[]{:S(2)}) async-start(), calls=%async_computation | async-start | bytes 7299072 | tf_op jit(solution)/shard_map/all_gather | solution.py:33
  194.2 213.8 %all-gather.6.cloned.1.call-start = ((), (), s32[]{:S(2)}) async-start(), calls=%async_computation.1 | async-start | bytes 4177920 | tf_op jit(solution)/shard_map/all_gather | solution.py:24
Sparse Core Ops, SparseCore 0:
  194.3 119.0 all-gather.3
  316.3 91.6 all-gather.5
where the time goes:
time: 434 us; the launch traced here: 430 us
  waiting for transfers between devices  211 us (49%)
  blocking collectives  184 us (42%)
  between operations  13.5 us (3%)
  local copies, waits for them, and re-layouts  9.12 us (2%)
  matrix products  8.79 us (2%)
    all_gather x1, waiting for transfers between devices, on_device(): row_series = lax.all_gather(zscore, 'bulk', axis=1, tiled=True)  119 us
    psum x1, blocking collectives, on_device(): average = lax.psum(jnp.sum(series, axis=1, keepdims=True), 'bulk') / TIME  97.6 us
    all_gather x1, waiting for transfers between devices, cycle_gather(): return lax.all_gather(own_rows, 'loop', axis=0, tiled=True)  91.9 us
    psum x1, blocking collectives, on_device(): lax.psum(jnp.sum(centered * centered, axis=1, keepdims=True), 'bulk')  86.1 us
    dot_general x1, matrix products, contract(): lax.dot_general(first_operand, second_operand, (((1,), (1,)), ((), ())),...  8.79 us
  transfers between devices with their start and end apart: 2, of which 2 were waited for; matrix products, arithmetic and copies ran while one was open for 0% of the time, Pallas kernels for 0%

commit v1 on v0

v1 whole, which is shorter than its diff:
```python
import jax
import jax.numpy as jnp
from jax import lax
from jax.sharding import PartitionSpec as P

TIME = 3072

epsilon = 1e-06


def standardize(rows):
    average = jnp.sum(rows, axis=1, keepdims=True) / TIME
    centered = rows - average
    variance = jnp.sum(centered * centered, axis=1, keepdims=True) / TIME
    return (centered * lax.rsqrt(variance + epsilon)).astype(jnp.bfloat16)


def on_device(series):
    n_bulk = lax.axis_size("bulk")
    rows, steps = series.shape
    share = rows // n_bulk
    pieces = lax.all_to_all(series.reshape(n_bulk, share, steps), "bulk", 0, 0, tiled=True)
    own = standardize(pieces.transpose(1, 0, 2).reshape(share, n_bulk * steps))
    block = lax.all_gather(own, "bulk", axis=0, tiled=True)
    others = lax.all_gather(own, "loop", axis=0, tiled=True)
    product = lax.dot_general(
        others, block, (((1,), (1,)), ((), ())), preferred_element_type=jnp.float32
    )
    return (product / TIME).reshape(lax.axis_size("loop"), share, rows)


def solution(mesh):
    placed = (P("loop", "bulk"),)
    return jax.shard_map(
        on_device, mesh=mesh, in_specs=placed, out_specs=P(None, "bulk", "loop"), check_vma=False
    )
```

time: 434 us -> 306 us (0.71)
  blocking collectives: 184 us -> 40.4 us
  waiting for transfers between devices: 211 us -> 225 us
  local copies, waits for them, and re-layouts: 9.12 us -> 15.2 us
    psum x2 -> x0, blocking collectives: 184 us -> none  [the longest x1 97.6 us: on_device(): average = lax.psum(jnp.sum(series, axis=1, keepdims=True), 'bulk') / TIME]
    all_to_all x0 -> x1, blocking collectives: none -> 40.4 us  [on_device(): lax.all_to_all(series.reshape(n_bulk, share, steps), 'bulk', 0, 0, tiled=...]
    all_gather x2, waiting for transfers between devices: 211 us -> 225 us  [the longest x1 133 us: on_device(): block = lax.all_gather(own, 'bulk', axis=0, tiled=True)]
    unnamed x2 -> x3, local copies, waits for them, and re-layouts: 3.71 us -> 11 us
  transfers between devices with their start and end apart: 2 -> 2, of which waited for: 2 -> 2; matrix products, arithmetic and copies ran while one was open for 0% -> 1% of each run, Pallas kernels for 0% -> 0%
where the time goes in v1:
time: 306 us; the launch traced here: 304 us
  waiting for transfers between devices  225 us (74%)
  blocking collectives  40.4 us (13%)
  local copies, waits for them, and re-layouts  15.2 us (5%)
  between operations  13.4 us (4%)
  matrix products  8.65 us (3%)
    all_gather x1, waiting for transfers between devices, on_device(): block = lax.all_gather(own, 'bulk', axis=0, tiled=True)  133 us
    all_gather x1, waiting for transfers between devices, on_device(): others = lax.all_gather(own, 'loop', axis=0, tiled=True)  92 us
    all_to_all x1, blocking collectives, on_device(): lax.all_to_all(series.reshape(n_bulk, share, steps), 'bulk', 0, 0, tiled=...  40.4 us
    unnamed x3, local copies, waits for them, and re-layouts  11 us
    dot_general x1, matrix products, on_device(): lax.dot_general(others, block, (((1,), (1,)), ((), ())), preferred_elemen...  8.65 us
  transfers between devices with their start and end apart: 2, of which 2 were waited for; matrix products, arithmetic and copies ran while one was open for 1% of the time, Pallas kernels for 0%

profile of v1, /device:TPU:6, one launch (start us, length us, event | category | flops | bytes accessed | tf_op | source)
XLA Modules:
  0.0 304.3 jit_solution(10203501590802974913)
XLA Ops:
  6.5 0.0 all-gather.5.cloned.1.call-start
  6.5 1.2 copy.6
  7.8 40.4 %all_to_all.5 = f32[32,33,96]{2,1,0:T(8,128)S(1)} all-to-all(f32[32,33,96]{2,1,0:T(8,128)S(1)} %reshape.26), channel_id=1, replica_groups=mesh['loop'=16,'bulk'=32] {'bulk'}, dimensions={0} | all-to-all | bytes 811008 | tf_op jit(solution)/shard_map/all_to_all | solution.py:22
  48.2 0.2 reduce_sum.18
  48.4 0.3 multiply_reduce_fusion
  48.7 0.1 copy.7
  48.8 0.3 reshape.27
  49.1 0.8 fusion
  49.9 0.0 all-gather.5.cloned.1.call-update
  49.9 0.0 all-gather.7.cloned.1.call-start
  50.0 0.7 all-gather.7.cloned.1.call-update
  50.7 92.0 %all-gather.5.cloned.1.call-done = bf16[16,33,3072]{2,1,0:T(8,128)(2,1)} async-done(((bf16[1,33,3072]{2,1,0:T(8,128)(2,1)}), bf16[16,33,3072]{2,1,0:T(8,128)(2,1)}) %all-gather.5.cloned.1.call-update) | async-done | bytes 3244048 | tf_op jit(solution)/shard_map/all_gather | solution.py:25
  142.7 2.7 reshape.30
  145.4 132.7 %all-gather.7.cloned.1.call-done = bf16[32,33,3072]{2,1,0:T(8,128)(2,1)} async-done(((bf16[1,33,3072]{2,1,0:T(8,128)(2,1)}), bf16[32,33,3072]{2,1,0:T(8,128)(2,1)}) %all-gather.7.cloned.1.call-update) | async-done | bytes 6488080 | tf_op jit(solution)/shard_map/all_gather | solution.py:24
  278.0 7.1 %reshape.32 = bf16[1056,3072]{1,0:T(8,128)(2,1)} reshape(bf16[32,33,3072]{2,1,0:T(8,128)(2,1)} %all-gather.7.cloned.1.call-done) | data formatting | bytes 12976128
  285.1 8.7 %convolution_multiply_fusion = f32[528,1056]{1,0:T(8,128)} fusion(bf16[528,3072]{1,0:T(8,128)(2,1)S(1)} %reshape.30, bf16[1056,3072]{1,0:T(8,128)(2,1)} %reshape.32), kind=kOutput, calls=%fused_computation | convolution fusion | flops 3426255360 | bytes 11962368 | tf_op jit(solution)/shard_map/dot_general | solution.py:26
  293.8 1.8 reshape.28
  295.6 1.9 copy.8
  (3 shorter events, 0.1 us)
Async XLA Ops:
  6.5 136.1 %all-gather.5.cloned.1.call-start = ((), (), s32[]{:S(2)}) async-start(), calls=%async_computation.1 | async-start | bytes 4177920 | tf_op jit(solution)/shard_map/all_gather | solution.py:25
  49.9 228.1 %all-gather.7.cloned.1.call-start = ((), (), s32[]{:S(2)}) async-start(), calls=%async_computation.2 | async-start | bytes 8110080 | tf_op jit(solution)/shard_map/all_gather | solution.py:24
Sparse Core Ops, SparseCore 0:
  50.1 92.5 all-gather.4
  146.0 131.9 all-gather.6

commit v2 on v1

v2 whole, which is shorter than its diff:
```python
import jax
import jax.numpy as jnp
from jax import lax
from jax.sharding import Mesh, PartitionSpec as P

TIME = 3072
AXES = ("x", "zl", "zh", "y", "core")
SIZES = (4, 4, 2, 8, 2)

epsilon = 1e-06


def standardize(rows):
    average = jnp.sum(rows, axis=1, keepdims=True) / TIME
    centered = rows - average
    variance = jnp.sum(centered * centered, axis=1, keepdims=True) / TIME
    return (centered * lax.rsqrt(variance + epsilon)).astype(jnp.bfloat16)


def shift(array, axis, by):
    size = lax.axis_size(axis)
    return lax.ppermute(array, axis, [(i, (i + by) % size) for i in range(size)])


def gather_x(part):
    after = shift(part, "x", 1)
    before = shift(part, "x", -1)
    half = part.shape[0] // 2
    far = jnp.concatenate([shift(after[:half], "x", 1), shift(before[half:], "x", -1)])
    here = lax.axis_index("x")
    whole = jnp.zeros((4,) + part.shape, part.dtype)
    for piece, offset in ((part, 0), (after, -1), (far, 2), (before, 1)):
        whole = lax.dynamic_update_slice_in_dim(whole, piece[None], (here + offset) % 4, 0)
    return whole.reshape((4 * part.shape[0],) + part.shape[1:])


def on_device(series):
    rows, steps = series.shape
    share = rows // 32
    bulk = ("zh", "y", "core")
    pieces = lax.all_to_all(series.reshape(32, share, steps), bulk, 0, 0, tiled=True)
    own = standardize(pieces.transpose(1, 0, 2).reshape(share, TIME))
    pair = lax.all_gather(own, "zh")
    block = lax.all_gather(pair, ("y", "core"))
    block = block.transpose(1, 0, 2, 3).reshape(rows, TIME)
    others = gather_x(lax.all_gather(own, "zl"))
    product = lax.dot_general(
        others, block, (((2,), (1,)), ((), ())), preferred_element_type=jnp.float32
    )
    return product / TIME


def solution(mesh):
    split = Mesh(mesh.devices.reshape(SIZES), AXES)
    return jax.shard_map(
        on_device,
        mesh=split,
        in_specs=(P(("x", "zl"), ("zh", "y", "core")),),
        out_specs=P(None, ("zh", "y", "core"), ("x", "zl")),
        check_vma=False,
    )
```

time: 306 us -> 175 us (0.57)
  the two profiles are of different devices: /device:TPU:6 before, /device:TPU:8 now
where the time goes in v2:
time: 175 us
  blocking collectives  77.8 us (44%)
  local copies, waits for them, and re-layouts  38.5 us (22%)
  waiting for transfers between devices  19.6 us (11%)
  starting transfers between devices  14.3 us (8%)
  between operations  13.6 us (8%)
  matrix products  9.33 us (5%)
    all_to_all x1, blocking collectives, on_device(): lax.all_to_all(series.reshape(32, share, steps), bulk, 0, 0, tiled=True)  40.7 us
    all_gather x1, blocking collectives, on_device(): others = gather_x(lax.all_gather(own, 'zl'))  25.7 us
    ppermute x4, waiting for transfers between devices, shift(): lax.ppermute(array, axis, [(i, (i + by) % size) for i in range(size)])  19.6 us
    ppermute x4, starting transfers between devices, shift(): lax.ppermute(array, axis, [(i, (i + by) % size) for i in range(size)])  14.3 us
    all_gather x1, local copies, waits for them, and re-layouts, on_device(): block = lax.all_gather(pair, ('y', 'core'))  12.5 us
    all_gather x1, blocking collectives, on_device(): pair = lax.all_gather(own, 'zh')  11.4 us
    dot_general x1, matrix products, on_device(): lax.dot_general(others, block, (((2,), (1,)), ((), ())), preferred_elemen...  9.33 us
    reshape x1, local copies, waits for them, and re-layouts, on_device(): block = block.transpose(1, 0, 2, 3).reshape(rows, TIME)  7.12 us
  transfers between devices with their start and end apart: 5, of which 3 were waited for; matrix products, arithmetic and copies ran while one was open for 5% of the time, Pallas kernels for 0%

profile of v2, /device:TPU:8, one launch (start us, length us, event | category | flops | bytes accessed | tf_op | source)
XLA Modules:
  0.0 174.5 jit_solution(9964336477880110053)
XLA Ops:
  6.5 0.0 all-gather.3.cloned.1.call-start
  6.5 1.2 copy.8
  7.8 40.7 %all_to_all.5 = f32[32,33,96]{2,1,0:T(8,128)S(1)} all-to-all(f32[32,33,96]{2,1,0:T(8,128)S(1)} %reshape.83), channel_id=1, replica_groups=mesh['x'=4,'zl'=4,'zh'=2,'y'=8,'core'=2] {'zh','y','core'}, dimensions={0} | all-to-all | bytes 811008 | tf_op jit(solution)/shard_map/all_to_all | solution.py:41
  48.5 0.2 reduce_sum.18
  48.6 0.3 multiply_reduce_fusion
  48.9 0.1 copy.9
  49.0 0.3 reshape.84
  49.3 0.1 multiply_convert_fusion
  49.5 11.4 %all_gather.15 = bf16[2,33,3072]{2,1,0:T(8,128)(2,1)} all-gather(bf16[1,33,3072]{2,1,0:T(8,128)(2,1)S(1)} %multiply_convert_fusion), channel_id=1, replica_groups=mesh['x'=4,'zl'=4,'zh'=2,'y'=8,'core'=2] {'zh'}, dimensions={0}, use_global_device_ids=true | all-gather | bytes 608256 | tf_op jit(solution)/shard_map/all_gather | solution.py:43
  60.9 0.0 all-gather.3.cloned.1.call-update
  60.9 25.7 %all_gather.14 = bf16[4,33,3072]{2,1,0:T(8,128)(2,1)S(1)} all-gather(bf16[1,33,3072]{2,1,0:T(8,128)(2,1)S(1)} %multiply_convert_fusion), channel_id=1, replica_groups=mesh['x'=4,'zl'=4,'zh'=2,'y'=8,'core'=2] {'zl'}, dimensions={0}, use_global_device_ids=true | all-gather | bytes 1013760 | tf_op jit(solution)/shard_map/all_gather | solution.py:46
  86.6 0.6 copy.10
  87.3 4.7 %collective-permute-start.2 = (bf16[4,33,3072]{2,0,1:T(4,128)(2,1)S(1)}, bf16[4,33,3072]{2,0,1:T(4,128)(2,1)S(1)}, u32[]{:S(2)}, u32[]{:S(2)}) collective-permute-start(bf16[4,33,3072]{2,0,1:T(4,128)(2,1)S(1)} %copy.10), channel_id=1, source_target_pairs={{0,384},{128,0},{256,128},{384,256},{1,385},{129,1},{257,129},{385... | collective-permute-start | bytes 2433032 | tf_op jit(solution)/shard_map/ppermute | solution.py:22
  91.9 1.9 %collective-permute-start = (bf16[4,33,3072]{2,0,1:T(4,128)(2,1)S(1)}, bf16[4,33,3072]{2,0,1:T(4,128)(2,1)S(1)}, u32[]{:S(2)}, u32[]{:S(2)}) collective-permute-start(bf16[4,33,3072]{2,0,1:T(4,128)(2,1)S(1)} %copy.10), channel_id=1, source_target_pairs={{0,128},{128,256},{256,384},{384,0},{1,129},{129,257},{257,385},{3... | collective-permute-start | bytes 2433032 | tf_op jit(solution)/shard_map/ppermute | solution.py:22
  93.9 2.4 %broadcast_in_dim.17 = bf16[4,4,33,3072]{3,2,1,0:T(8,128)(2,1)} broadcast(bf16[]{:T(256)} %constant.38.clone.1), dimensions={} | broadcast | bytes 3244034 | tf_op jit(solution)/shard_map/broadcast_in_dim | solution.py:31
  96.3 1.0 bitcast_dynamic-update-slice_fusion
  97.3 10.9 %collective-permute-done.2 = bf16[4,33,3072]{2,0,1:T(4,128)(2,1)S(1)} collective-permute-done((bf16[4,33,3072]{2,0,1:T(4,128)(2,1)S(1)}, bf16[4,33,3072]{2,0,1:T(4,128)(2,1)S(1)}, u32[]{:S(2)}, u32[]{:S(2)}) %collective-permute-start.2) | collective-permute-done | bytes 811040 | tf_op jit(solution)/shard_map/ppermute | solution.py:22
  108.2 0.5 slice.9
  108.7 5.6 %collective-permute-start.3 = (bf16[2,33,3072]{2,0,1:T(2,128)(2,1)S(1)}, bf16[2,33,3072]{2,0,1:T(2,128)(2,1)S(1)}, u32[]{:S(2)}, u32[]{:S(2)}) collective-permute-start(bf16[2,33,3072]{2,0,1:T(2,128)(2,1)S(1)} %slice.9), channel_id=1, source_target_pairs={{0,384},{128,0},{256,128},{384,256},{1,385},{129,1},{257,129},{385... | collective-permute-start | bytes 1216520 | tf_op jit(solution)/shard_map/ppermute | solution.py:22
  114.3 0.0 collective-permute-done
  114.3 0.3 slice.8
  114.6 2.1 %collective-permute-start.1 = (bf16[2,33,3072]{2,0,1:T(2,128)(2,1)S(1)}, bf16[2,33,3072]{2,0,1:T(2,128)(2,1)S(1)}, u32[]{:S(2)}, u32[]{:S(2)}) collective-permute-start(bf16[2,33,3072]{2,0,1:T(2,128)(2,1)S(1)} %slice.8), channel_id=1, source_target_pairs={{0,128},{128,256},{256,384},{384,0},{1,129},{129,257},{257,385},{3... | collective-permute-start | bytes 1216520 | tf_op jit(solution)/shard_map/ppermute | solution.py:22
  116.7 1.2 copy_dynamic-update-slice_fusion.2
  118.0 3.1 %collective-permute-done.3 = bf16[2,33,3072]{2,0,1:T(2,128)(2,1)S(1)} collective-permute-done((bf16[2,33,3072]{2,0,1:T(2,128)(2,1)S(1)}, bf16[2,33,3072]{2,0,1:T(2,128)(2,1)S(1)}, u32[]{:S(2)}, u32[]{:S(2)}) %collective-permute-start.3) | collective-permute-done | bytes 405536 | tf_op jit(solution)/shard_map/ppermute | solution.py:22
  121.0 5.6 %collective-permute-done.1 = bf16[2,33,3072]{2,0,1:T(2,128)(2,1)S(1)} collective-permute-done((bf16[2,33,3072]{2,0,1:T(2,128)(2,1)S(1)}, bf16[2,33,3072]{2,0,1:T(2,128)(2,1)S(1)}, u32[]{:S(2)}, u32[]{:S(2)}) %collective-permute-start.1) | collective-permute-done | bytes 405536 | tf_op jit(solution)/shard_map/ppermute | solution.py:22
  126.6 0.9 maximum_bitcast_fusion
  127.5 1.2 copy_dynamic-update-slice_fusion.1
  128.8 1.2 copy_dynamic-update-slice_fusion
  130.0 0.0 all-gather.3.cloned.1.call-done
  130.0 12.5 %copy.23 = bf16[16,2,33,3072]{3,1,0,2:T(2,128)(2,1)S(1)} copy(bf16[16,2,33,3072]{3,2,1,0:T(8,128)(2,1)} %bitcast.17) | data formatting | bytes 12976128 | tf_op jit(solution)/shard_map/all_gather | solution.py:44
  142.5 6.8 %copy.16 = bf16[2,16,33,3072]{3,2,1,0:T(8,128)(2,1)} copy(bf16[2,16,33,3072]{3,0,1,2:T(2,128)(2,1)S(1)} %bitcast.15) | data formatting | bytes 12976128 | tf_op jit(solution)/shard_map/transpose | solution.py:45
  149.3 7.1 %reshape.88 = bf16[1056,3072,1]{1,0,2:T(8,128)(2,1)} reshape(bf16[2,16,33,3072]{3,2,1,0:T(8,128)(2,1)} %copy.16) | data formatting | bytes 12976128 | tf_op jit(solution)/shard_map/reshape | solution.py:45
  156.5 9.3 %convolution_multiply_fusion = f32[16,33,1056]{2,1,0:T(8,128)S(1)} fusion(bf16[16,33,3072]{2,1,0:T(8,128)(2,1)} %bitcast.5, bf16[1056,3072,1]{1,0,2:T(8,128)(2,1)} %reshape.88), kind=kOutput, calls=%fused_computation.1 | convolution fusion | flops 3426255360 | bytes 11962368 | tf_op jit(solution)/shard_map/dot_general | solution.py:47
  165.8 1.9 %copy.17 = f32[16,33,1056]{2,0,1:T(8,128)} copy(f32[16,33,1056]{2,1,0:T(8,128)S(1)} %convolution_multiply_fusion) | data formatting | bytes 4460544 | tf_op jit(solution)/shard_map/div | solution.py:50
  (3 shorter events, 0.1 us)
Async XLA Ops:
  6.5 123.5 %all-gather.3.cloned.1.call-start = ((), (), s32[]{:S(2)}) async-start(), calls=%async_computation.1 | async-start | bytes 8355840 | tf_op jit(solution)/shard_map/all_gather | solution.py:44
  87.3 21.0 %collective-permute-start.2 = (bf16[4,33,3072]{2,0,1:T(4,128)(2,1)S(1)}, bf16[4,33,3072]{2,0,1:T(4,128)(2,1)S(1)}, u32[]{:S(2)}, u32[]{:S(2)}) collective-permute-start(bf16[4,33,3072]{2,0,1:T(4,128)(2,1)S(1)} %copy.10), channel_id=1, source_target_pairs={{0,384},{128,0},{256,128},{384,256},{1,385},{129,1},{257,129},{385... | collective-permute-start | bytes 2433032 | tf_op jit(solution)/shard_map/ppermute | solution.py:22
  91.9 22.4 %collective-permute-start = (bf16[4,33,3072]{2,0,1:T(4,128)(2,1)S(1)}, bf16[4,33,3072]{2,0,1:T(4,128)(2,1)S(1)}, u32[]{:S(2)}, u32[]{:S(2)}) collective-permute-start(bf16[4,33,3072]{2,0,1:T(4,128)(2,1)S(1)} %copy.10), channel_id=1, source_target_pairs={{0,128},{128,256},{256,384},{384,0},{1,129},{129,257},{257,385},{3... | collective-permute-start | bytes 2433032 | tf_op jit(solution)/shard_map/ppermute | solution.py:22
  108.7 12.3 %collective-permute-start.3 = (bf16[2,33,3072]{2,0,1:T(2,128)(2,1)S(1)}, bf16[2,33,3072]{2,0,1:T(2,128)(2,1)S(1)}, u32[]{:S(2)}, u32[]{:S(2)}) collective-permute-start(bf16[2,33,3072]{2,0,1:T(2,128)(2,1)S(1)} %slice.9), channel_id=1, source_target_pairs={{0,384},{128,0},{256,128},{384,256},{1,385},{129,1},{257,129},{385... | collective-permute-start | bytes 1216520 | tf_op jit(solution)/shard_map/ppermute | solution.py:22
  114.6 12.0 %collective-permute-start.1 = (bf16[2,33,3072]{2,0,1:T(2,128)(2,1)S(1)}, bf16[2,33,3072]{2,0,1:T(2,128)(2,1)S(1)}, u32[]{:S(2)}, u32[]{:S(2)}) collective-permute-start(bf16[2,33,3072]{2,0,1:T(2,128)(2,1)S(1)} %slice.8), channel_id=1, source_target_pairs={{0,128},{128,256},{256,384},{384,0},{1,129},{129,257},{257,385},{3... | collective-permute-start | bytes 1216520 | tf_op jit(solution)/shard_map/ppermute | solution.py:22
Sparse Core Ops, SparseCore 0:
  61.0 53.7 all-gather.2

commit v3 on v2

v3 whole, which is shorter than its diff:
```python
import jax
import jax.numpy as jnp
from jax import lax
from jax.experimental import pallas as pl
from jax.experimental.pallas import tpu as pltpu
from jax.sharding import Mesh, PartitionSpec as P

TIME = 3072
AXES = ("x", "zl", "zh", "y", "core")
SIZES = (4, 4, 2, 8, 2)
BULK = ("zh", "y", "core")
SHARE = 33
WINDOW = 40
ROWS = 1056
GROUP = 8 * SHARE

epsilon = 1e-06


def standardize(rows):
    average = jnp.sum(rows, axis=1, keepdims=True) / TIME
    centered = rows - average
    variance = jnp.sum(centered * centered, axis=1, keepdims=True) / TIME
    return (centered * lax.rsqrt(variance + epsilon)).astype(jnp.bfloat16)


def shift(array, axis, by):
    size = lax.axis_size(axis)
    return lax.ppermute(array, axis, [(i, (i + by) % size) for i in range(size)])


def gather_x(part):
    after = shift(part, "x", 1)
    before = shift(part, "x", -1)
    far = [shift(after[:, :2], "x", 1), shift(before[:, 2:], "x", -1)]
    return jnp.concatenate([part, before, *far, after], axis=1)


def product_kernel(place, others, windows, out, held, block, arrived):
    copies = []
    for group in range(4):
        half, parity = divmod(group, 2)
        copy = pltpu.make_async_copy(
            windows.at[pl.ds(8 * parity, 8), half], held.at[group], arrived.at[group]
        )
        copy.start()
        copies.append(copy)
    edges = [0, 256, 512, 768, ROWS]
    for group in range(4):
        copies[group].wait()
        for i in range(8):
            start = GROUP * group + 32 * i
            size = 32 if i < 7 else 40
            block[start : start + size, :] = held[group, i, :size, :]
        low, high = edges[group], edges[group + 1]
        product = lax.dot_general(
            others[...],
            block[low:high, :],
            (((1,), (1,)), ((), ())),
            preferred_element_type=jnp.float32,
        ) * (1.0 / TIME)
        product = product.reshape(SHARE, 16, high - low)
        for x in range(4):

            @pl.when(place[0] == x)
            def _():
                for k in range(4):
                    to = 4 * ((x + k) % 4)
                    out[:, to : to + 4, low:high] = product[:, 4 * k : 4 * k + 4, :]


def multiply(others, windows):
    place = lax.axis_index("x").astype(jnp.int32).reshape(1)
    return pl.pallas_call(
        product_kernel,
        out_shape=jax.ShapeDtypeStruct((SHARE, 16, ROWS), jnp.float32),
        in_specs=[
            pl.BlockSpec(memory_space=pltpu.SMEM),
            pl.BlockSpec(memory_space=pltpu.VMEM),
            pl.BlockSpec(memory_space=pl.ANY),
        ],
        out_specs=pl.BlockSpec(memory_space=pltpu.VMEM),
        scratch_shapes=[
            pltpu.VMEM((4, 8, WINDOW, TIME), jnp.bfloat16),
            pltpu.VMEM((ROWS, TIME), jnp.bfloat16),
            pltpu.SemaphoreType.DMA((4,)),
        ],
        compiler_params=pltpu.CompilerParams(vmem_limit_bytes=48 * 1024 * 1024),
        cost_estimate=pl.CostEstimate(
            flops=2 * 528 * ROWS * TIME, bytes_accessed=14_000_000, transcendentals=0
        ),
    )(place, others, windows)


def on_device(series):
    groups = series.reshape(4, GROUP, -1)
    windows = jnp.stack([groups[:, 32 * i : 32 * i + WINDOW] for i in range(8)], axis=1)
    windows = windows.reshape(32, WINDOW, -1)
    pieces = lax.all_to_all(windows, BULK, 0, 0, tiled=True)
    window = standardize(pieces.transpose(1, 0, 2).reshape(WINDOW, TIME))
    own = lax.dynamic_slice_in_dim(window, lax.rem(lax.axis_index(BULK), 8), SHARE, 0)
    pair = lax.all_gather(window, "zh")
    gathered = lax.all_gather(pair, ("y", "core"))
    others = gather_x(lax.all_gather(own, "zl").transpose(1, 0, 2))
    product = multiply(others.reshape(SHARE * 16, TIME), gathered)
    return product.transpose(1, 0, 2)


def solution(mesh):
    split = Mesh(mesh.devices.reshape(SIZES), AXES)
    return jax.shard_map(
        on_device,
        mesh=split,
        in_specs=(P(("x", "zl"), BULK),),
        out_specs=P(None, BULK, ("x", "zl")),
        check_vma=False,
    )
```

time: 175 us -> 146 us (0.83)
  the two profiles are of different devices: /device:TPU:8 before, /device:TPU:6 now
where the time goes in v3:
time: 146 us
  blocking collectives  77.2 us (53%)
  waiting for transfers between devices  25.9 us (18%)
  between operations  13.6 us (9%)
  starting transfers between devices  11.7 us (8%)
  Pallas kernels  10 us (7%)
  local copies, waits for them, and re-layouts  6.32 us (4%)
    all_to_all x1, blocking collectives, on_device(): pieces = lax.all_to_all(windows, BULK, 0, 0, tiled=True)  40.4 us
    ppermute x4, waiting for transfers between devices, shift(): lax.ppermute(array, axis, [(i, (i + by) % size) for i in range(size)])  25.9 us
    all_gather x1, blocking collectives, on_device(): others = gather_x(lax.all_gather(own, 'zl').transpose(1, 0, 2))  25.7 us
    ppermute x4, starting transfers between devices, shift(): lax.ppermute(array, axis, [(i, (i + by) % size) for i in range(size)])  11.7 us
    all_gather x1, blocking collectives, on_device(): pair = lax.all_gather(window, 'zh')  11.1 us
    pallas_call x1, Pallas kernels, multiply(): pl.pallas_call(product_kernel, out_shape=jax.ShapeDtypeStruct((SHARE, 16,...  10 us
  transfers between devices with their start and end apart: 5, of which 3 were waited for; matrix products, arithmetic and copies ran while one was open for 3% of the time, Pallas kernels for 0%

profile of v3, /device:TPU:6, one launch (start us, length us, event | category | flops | bytes accessed | tf_op | source)
XLA Modules:
  0.0 145.5 jit_solution(5302739710995180871)
XLA Ops:
  6.5 0.0 all-gather.5.cloned.1.call-start
  6.5 1.2 copy.10
  7.9 40.4 %all_to_all.5 = f32[32,40,96]{2,1,0:T(8,128)S(1)} all-to-all(f32[32,40,96]{2,1,0:T(8,128)S(1)} %bitcast.56), channel_id=1, replica_groups=mesh['x'=4,'zl'=4,'zh'=2,'y'=8,'core'=2] {'zh','y','core'}, dimensions={0} | all-to-all | bytes 983040 | tf_op jit(solution)/shard_map/all_to_all | solution.py:99
  48.4 0.2 reduce_sum.18
  48.5 0.3 multiply_reduce_fusion
  48.8 0.1 copy.12
  48.9 0.3 reshape.93
  49.3 0.1 multiply_convert_fusion
  49.4 11.1 %all_gather.18 = bf16[2,40,3072]{2,1,0:T(8,128)(2,1)} all-gather(bf16[1,40,3072]{2,1,0:T(8,128)(2,1)S(1)} %multiply_convert_fusion), channel_id=1, replica_groups=mesh['x'=4,'zl'=4,'zh'=2,'y'=8,'core'=2] {'zh'}, dimensions={0}, use_global_device_ids=true | all-gather | bytes 737280 | tf_op jit(solution)/shard_map/all_gather | solution.py:102
  60.5 0.0 all-gather.5.cloned.1.call-update
  60.6 0.1 dynamic-slice.1
  60.7 0.1 dynamic-slice
  60.7 0.3 reshape.91
  61.1 0.1 fusion.2
  61.2 25.7 %all-gather.2 = bf16[4,33,3072]{2,1,0:T(8,128)(2,1)S(1)} all-gather(bf16[1,33,3072]{2,1,0:T(8,128)(2,1)S(1)} %fusion.2), channel_id=2, replica_groups=mesh['x'=4,'zl'=4,'zh'=2,'y'=8,'core'=2] {'zl'}, dimensions={0}, use_global_device_ids=true | all-gather | bytes 1013760 | tf_op jit(solution)/shard_map/all_gather | solution.py:104
  86.9 0.6 copy.13
  87.5 2.4 %collective-permute-start.1 = (bf16[33,4,3072]{2,1,0:T(4,128)(2,1)S(1)}, bf16[33,4,3072]{2,1,0:T(4,128)(2,1)S(1)}, u32[]{:S(2)}, u32[]{:S(2)}) collective-permute-start(bf16[33,4,3072]{2,1,0:T(4,128)(2,1)S(1)} %copy.13), channel_id=1, source_target_pairs={{0,128},{128,256},{256,384},{384,0},{1,129},{129,257},{257,385},{3... | collective-permute-start | bytes 2433032 | tf_op jit(solution)/shard_map/ppermute | solution.py:29
  89.9 3.5 %collective-permute-start = (bf16[33,4,3072]{2,1,0:T(4,128)(2,1)S(1)}, bf16[33,4,3072]{2,1,0:T(4,128)(2,1)S(1)}, u32[]{:S(2)}, u32[]{:S(2)}) collective-permute-start(bf16[33,4,3072]{2,1,0:T(4,128)(2,1)S(1)} %copy.13), channel_id=1, source_target_pairs={{0,384},{128,0},{256,128},{384,256},{1,385},{129,1},{257,129},{385... | collective-permute-start | bytes 2433032 | tf_op jit(solution)/shard_map/ppermute | solution.py:29
  93.4 0.1 constant_dynamic-update-slice_fusion.4
  93.5 14.6 %collective-permute-done.1 = bf16[33,4,3072]{2,1,0:T(4,128)(2,1)S(1)} collective-permute-done((bf16[33,4,3072]{2,1,0:T(4,128)(2,1)S(1)}, bf16[33,4,3072]{2,1,0:T(4,128)(2,1)S(1)}, u32[]{:S(2)}, u32[]{:S(2)}) %collective-permute-start.1) | collective-permute-done | bytes 811040 | tf_op jit(solution)/shard_map/ppermute | solution.py:29
  108.1 0.3 slice.48
  108.4 0.1 copy.23
  108.5 3.6 %collective-permute-start.2 = (bf16[33,2,3072]{2,0,1:T(8,128)(2,1)S(1)}, bf16[33,2,3072]{2,0,1:T(8,128)(2,1)S(1)}, u32[]{:S(2)}, u32[]{:S(2)}) collective-permute-start(bf16[33,2,3072]{2,0,1:T(8,128)(2,1)S(1)} %copy.23), channel_id=1, source_target_pairs={{0,128},{128,256},{256,384},{384,0},{1,129},{129,257},{257,385},{3... | collective-permute-start | bytes 1216520 | tf_op jit(solution)/shard_map/ppermute | solution.py:29
  112.1 0.0 collective-permute-done
  112.1 0.5 slice.49
  112.5 0.1 copy.24
  112.6 2.2 %collective-permute-start.3 = (bf16[33,2,3072]{2,0,1:T(8,128)(2,1)S(1)}, bf16[33,2,3072]{2,0,1:T(8,128)(2,1)S(1)}, u32[]{:S(2)}, u32[]{:S(2)}) collective-permute-start(bf16[33,2,3072]{2,0,1:T(8,128)(2,1)S(1)} %copy.24), channel_id=1, source_target_pairs={{0,384},{128,0},{256,128},{384,256},{1,385},{129,1},{257,129},{385... | collective-permute-start | bytes 1216520 | tf_op jit(solution)/shard_map/ppermute | solution.py:29
  114.9 0.3 constant_dynamic-update-slice_fusion.3
  115.2 6.2 %collective-permute-done.2 = bf16[33,2,3072]{2,0,1:T(8,128)(2,1)S(1)} collective-permute-done((bf16[33,2,3072]{2,0,1:T(8,128)(2,1)S(1)}, bf16[33,2,3072]{2,0,1:T(8,128)(2,1)S(1)}, u32[]{:S(2)}, u32[]{:S(2)}) %collective-permute-start.2) | collective-permute-done | bytes 405536 | tf_op jit(solution)/shard_map/ppermute | solution.py:29
  121.4 5.1 %collective-permute-done.3 = bf16[33,2,3072]{2,0,1:T(8,128)(2,1)S(1)} collective-permute-done((bf16[33,2,3072]{2,0,1:T(8,128)(2,1)S(1)}, bf16[33,2,3072]{2,0,1:T(8,128)(2,1)S(1)}, u32[]{:S(2)}, u32[]{:S(2)}) %collective-permute-start.3) | collective-permute-done | bytes 405536 | tf_op jit(solution)/shard_map/ppermute | solution.py:29
  126.5 0.3 constant_dynamic-update-slice_fusion
  126.8 1.8 %copy.19 = bf16[33,16,3072]{2,1,0:T(8,128)(2,1)S(1)} copy(bf16[33,16,3072]{2,0,1:T(8,128)(2,1)S(1)} %constant_dynamic-update-slice_fusion) | data formatting | bytes 6488064 | tf_op jit(solution)/shard_map/concatenate | solution.py:36
  128.6 0.0 all-gather.5.cloned.1.call-done
  128.7 10.0 %shard_map.17 = f32[33,16,1056]{2,1,0:T(8,128)} custom-call(s32[1]{0:T(128)} %bitcast.place, bf16[528,3072]{1,0:T(8,128)(2,1)S(1)} %bitcast.44, bf16[16,2,40,3072]{3,2,1,0:T(8,128)(2,1)} %bitcast.47), custom_call_target="tpu_custom_call" | custom-call | flops 3425697792 | bytes 14000000 | tf_op jit(solution)/shard_map/pallas_call | solution.py:74
  (13 shorter events, 0.2 us)
Async XLA Ops:
  6.5 122.1 %all-gather.5.cloned.1.call-start = ((), (), s32[]{:S(2)}) async-start(), calls=%async_computation.1 | async-start | bytes 8355840 | tf_op jit(solution)/shard_map/all_gather | solution.py:103
  87.5 20.6 %collective-permute-start.1 = (bf16[33,4,3072]{2,1,0:T(4,128)(2,1)S(1)}, bf16[33,4,3072]{2,1,0:T(4,128)(2,1)S(1)}, u32[]{:S(2)}, u32[]{:S(2)}) collective-permute-start(bf16[33,4,3072]{2,1,0:T(4,128)(2,1)S(1)} %copy.13), channel_id=1, source_target_pairs={{0,128},{128,256},{256,384},{384,0},{1,129},{129,257},{257,385},{3... | collective-permute-start | bytes 2433032 | tf_op jit(solution)/shard_map/ppermute | solution.py:29
  89.9 22.2 %collective-permute-start = (bf16[33,4,3072]{2,1,0:T(4,128)(2,1)S(1)}, bf16[33,4,3072]{2,1,0:T(4,128)(2,1)S(1)}, u32[]{:S(2)}, u32[]{:S(2)}) collective-permute-start(bf16[33,4,3072]{2,1,0:T(4,128)(2,1)S(1)} %copy.13), channel_id=1, source_target_pairs={{0,384},{128,0},{256,128},{384,256},{1,385},{129,1},{257,129},{385... | collective-permute-start | bytes 2433032 | tf_op jit(solution)/shard_map/ppermute | solution.py:29
  108.5 12.9 %collective-permute-start.2 = (bf16[33,2,3072]{2,0,1:T(8,128)(2,1)S(1)}, bf16[33,2,3072]{2,0,1:T(8,128)(2,1)S(1)}, u32[]{:S(2)}, u32[]{:S(2)}) collective-permute-start(bf16[33,2,3072]{2,0,1:T(8,128)(2,1)S(1)} %copy.23), channel_id=1, source_target_pairs={{0,128},{128,256},{256,384},{384,0},{1,129},{129,257},{257,385},{3... | collective-permute-start | bytes 1216520 | tf_op jit(solution)/shard_map/ppermute | solution.py:29
  112.6 13.8 %collective-permute-start.3 = (bf16[33,2,3072]{2,0,1:T(8,128)(2,1)S(1)}, bf16[33,2,3072]{2,0,1:T(8,128)(2,1)S(1)}, u32[]{:S(2)}, u32[]{:S(2)}) collective-permute-start(bf16[33,2,3072]{2,0,1:T(8,128)(2,1)S(1)} %copy.24), channel_id=1, source_target_pairs={{0,384},{128,0},{256,128},{384,256},{1,385},{129,1},{257,129},{385... | collective-permute-start | bytes 1216520 | tf_op jit(solution)/shard_map/ppermute | solution.py:29
Sparse Core Ops, SparseCore 0:
  60.7 55.7 all-gather.4

commit v4 on v3

v4 whole, which is shorter than its diff:
```python
import jax
import jax.numpy as jnp
from jax import lax
from jax.experimental import pallas as pl
from jax.experimental.pallas import tpu as pltpu
from jax.sharding import Mesh, PartitionSpec as P

TIME = 3072
HALF = TIME // 2
AXES = ("x", "zl", "zh", "y", "core")
SIZES = (4, 4, 2, 8, 2)
BULK = ("zh", "y", "core")
SHARE = 33
WINDOW = 40
ROWS = 1056
GROUP = 8 * SHARE

epsilon = 1e-06


def shift(array, axis, by):
    size = lax.axis_size(axis)
    return lax.ppermute(array, axis, [(i, (i + by) % size) for i in range(size)])


def standardize(half):
    mean = jnp.sum(half, axis=1) / HALF
    from_mean = half - mean[:, None]
    deviation = jnp.sum(from_mean * from_mean, axis=1)
    both = lax.all_gather(jnp.stack([mean, deviation]), "zh")
    average = (both[0, 0] + both[1, 0]) * 0.5
    between = both[0, 0] - both[1, 0]
    squares = both[0, 1] + both[1, 1] + (HALF * 0.5) * (between * between)
    scale = lax.rsqrt(squares / TIME + epsilon)
    return ((half - average[:, None]) * scale[:, None]).astype(jnp.bfloat16)


def gather_x(part):
    after = shift(part, "x", 1)
    before = shift(part, "x", -1)
    far = [shift(after[:, :2], "x", 1), shift(before[:, 2:], "x", -1)]
    return jnp.concatenate([part, before, *far, after], axis=1)


def product_kernel(place, others, near, far, out, held_near, held_far, block, arrived):
    copies = []
    for h in range(2):
        for n, (source, held) in enumerate(((near, held_near), (far, held_far))):
            yc = pl.ds(8 * h, 8)
            copy = pltpu.make_async_copy(source.at[yc], held.at[yc], arrived.at[2 * h + n])
            copy.start()
            copies.append(copy)
    for h in range(2):
        copies[2 * h].wait()
        copies[2 * h + 1].wait()
        for w in range(2):
            for i in range(8):
                start = GROUP * (2 * w + h) + 32 * i
                size = 32 if i < 7 else 40
                rows = slice(WINDOW * w, WINDOW * w + size)
                block[start : start + size, :HALF] = held_near[8 * h + i, rows, :]
                block[start : start + size, HALF:] = held_far[8 * h + i, rows, :]
    edges = [0, 256, 512, 768, ROWS]
    for low, high in zip(edges[:-1], edges[1:]):
        product = lax.dot_general(
            others[...],
            block[low:high, :],
            (((1,), (1,)), ((), ())),
            preferred_element_type=jnp.float32,
        ) * (1.0 / TIME)
        product = product.reshape(SHARE, 16, high - low)
        for x in range(4):

            @pl.when(place[0] == x)
            def _():
                for k in range(4):
                    to = 4 * ((x + k) % 4)
                    out[:, to : to + 4, low:high] = product[:, 4 * k : 4 * k + 4, :]


def multiply(others, near, far):
    place = lax.axis_index("x").astype(jnp.int32).reshape(1)
    return pl.pallas_call(
        product_kernel,
        out_shape=jax.ShapeDtypeStruct((SHARE, 16, ROWS), jnp.float32),
        in_specs=[
            pl.BlockSpec(memory_space=pltpu.SMEM),
            pl.BlockSpec(memory_space=pltpu.VMEM),
            pl.BlockSpec(memory_space=pl.ANY),
            pl.BlockSpec(memory_space=pl.ANY),
        ],
        out_specs=pl.BlockSpec(memory_space=pltpu.VMEM),
        scratch_shapes=[
            pltpu.VMEM((16, 2 * WINDOW, HALF), jnp.bfloat16),
            pltpu.VMEM((16, 2 * WINDOW, HALF), jnp.bfloat16),
            pltpu.VMEM((ROWS, TIME), jnp.bfloat16),
            pltpu.SemaphoreType.DMA((4,)),
        ],
        compiler_params=pltpu.CompilerParams(vmem_limit_bytes=48 * 1024 * 1024),
        cost_estimate=pl.CostEstimate(
            flops=2 * 528 * ROWS * TIME, bytes_accessed=14_000_000, transcendentals=0
        ),
    )(place, others, near, far)


def on_device(series):
    steps = series.shape[1]
    groups = series.reshape(2, 2, GROUP, steps)
    windows = jnp.stack([groups[:, :, 32 * i : 32 * i + WINDOW] for i in range(8)], axis=2)
    windows = windows.transpose(1, 2, 0, 3, 4).reshape(16, 2 * WINDOW, steps)
    pieces = lax.all_to_all(windows, ("y", "core"), 0, 0, tiled=True)
    zscore = standardize(pieces.transpose(1, 0, 2).reshape(2 * WINDOW, HALF))
    near = lax.all_gather(zscore, ("y", "core"))

    zh, zl = lax.axis_index("zh"), lax.axis_index("zl")
    column = [
        lax.all_gather(zscore[WINDOW * w : WINDOW * w + WINDOW], ("zh", "zl")) for w in range(2)
    ]
    partner = jnp.concatenate(
        [lax.dynamic_index_in_dim(c, (1 - zh) * 4 + zl, 0, False) for c in column]
    )
    far = lax.all_gather(partner, ("y", "core"))

    mine = jnp.where(zh == 0, column[0], column[1]).reshape(2, 4, WINDOW, HALF)
    mine = lax.dynamic_slice_in_dim(mine, lax.rem(lax.axis_index(BULK), 8), SHARE, 2)
    mine = jnp.where(zh == 0, mine, mine[::-1])
    mine = mine.transpose(2, 1, 0, 3).reshape(SHARE, 4, TIME)
    others = gather_x(mine)
    product = multiply(others.reshape(SHARE * 16, TIME), near, far)
    return product.transpose(1, 0, 2)


def solution(mesh):
    split = Mesh(mesh.devices.reshape(SIZES), AXES)
    return jax.shard_map(
        on_device,
        mesh=split,
        in_specs=(P(("x", "zl"), BULK),),
        out_specs=P(None, BULK, ("x", "zl")),
        check_vma=False,
    )
```

time: 146 us -> 184 us (1.26)
  local copies, waits for them, and re-layouts: 6.32 us -> 26.5 us
  blocking collectives: 77.2 us -> 94.7 us
  waiting for transfers between devices: 25.9 us -> 20.8 us
  other arithmetic: 0.68 us -> 3.36 us
  Pallas kernels: 10 us -> 11.9 us
    all_gather x2 -> x3, blocking collectives: 36.8 us -> 67.8 us  [the longest x2 56.6 us: on_device(): lax.all_gather(zscore[WINDOW * w:WINDOW * w + WINDOW], ('zh', 'zl'))]
    all_to_all x1, blocking collectives: 40.4 us -> 26.9 us  [on_device(): pieces = lax.all_to_all(windows, ('y', 'core'), 0, 0, tiled=True)]
    concatenate x2 -> x1, local copies, waits for them, and re-layouts: 2.11 us -> 14.3 us  [gather_x(): return jnp.concatenate([part, before, *far, after], axis=1)]
    rev x0 -> x1, local copies, waits for them, and re-layouts: none -> 6.47 us  [on_device(): mine = jnp.where(zh == 0, mine, mine[::-1])]
    ppermute x4, waiting for transfers between devices: 25.9 us -> 20.7 us  [shift(): lax.ppermute(array, axis, [(i, (i + by) % size) for i in range(size)])]
    pallas_call x1, Pallas kernels: 10 us -> 11.9 us  [multiply(): pl.pallas_call(product_kernel, out_shape=jax.ShapeDtypeStruct((SHARE, 16,...]
  transfers between devices with their start and end apart: 5 -> 6, of which waited for: 3 -> 3; matrix products, arithmetic and copies ran while one was open for 3% -> 14% of each run, Pallas kernels for 0% -> 0%
where the time goes in v4:
time: 184 us; the launch traced here: 183 us
  blocking collectives  94.7 us (51%)
  local copies, waits for them, and re-layouts  26.5 us (14%)
  waiting for transfers between devices  20.8 us (11%)
  between operations  13.7 us (7%)
  Pallas kernels  11.9 us (6%)
  starting transfers between devices  11.7 us (6%)
  other arithmetic  3.36 us (2%)
    all_gather x2, blocking collectives, on_device(): lax.all_gather(zscore[WINDOW * w:WINDOW * w + WINDOW], ('zh', 'zl'))  56.6 us
    all_to_all x1, blocking collectives, on_device(): pieces = lax.all_to_all(windows, ('y', 'core'), 0, 0, tiled=True)  26.9 us
    ppermute x4, waiting for transfers between devices, shift(): lax.ppermute(array, axis, [(i, (i + by) % size) for i in range(size)])  20.7 us
    concatenate x1, local copies, waits for them, and re-layouts, gather_x(): return jnp.concatenate([part, before, *far, after], axis=1)  14.3 us
    pallas_call x1, Pallas kernels, multiply(): pl.pallas_call(product_kernel, out_shape=jax.ShapeDtypeStruct((SHARE, 16,...  11.9 us
    ppermute x4, starting transfers between devices, shift(): lax.ppermute(array, axis, [(i, (i + by) % size) for i in range(size)])  11.7 us
    all_gather x1, blocking collectives, standardize(): both = lax.all_gather(jnp.stack([mean, deviation]), 'zh')  11.2 us
    rev x1, local copies, waits for them, and re-layouts, on_device(): mine = jnp.where(zh == 0, mine, mine[::-1])  6.47 us
  transfers between devices with their start and end apart: 6, of which 3 were waited for; matrix products, arithmetic and copies ran while one was open for 14% of the time, Pallas kernels for 0%

profile of v4, /device:TPU:6, one launch (start us, length us, event | category | flops | bytes accessed | tf_op | source)
XLA Modules:
  0.0 182.7 jit_solution(17028950216737700087)
XLA Ops:
  6.5 0.0 all-gather.8.cloned.1.call-start
  6.5 1.2 copy.19
  7.9 26.9 %all_to_all.5 = f32[16,80,96]{2,1,0:T(8,128)S(1)} all-to-all(f32[16,80,96]{2,1,0:T(8,128)S(1)} %bitcast.75), channel_id=1, replica_groups=mesh['x'=4,'zl'=4,'zh'=2,'y'=8,'core'=2] {'y','core'}, dimensions={0} | all-to-all | bytes 983040 | tf_op jit(solution)/shard_map/all_to_all | solution.py:111
  34.9 0.1 reduce_sum.18
  35.0 0.3 multiply_reduce_fusion
  35.3 11.2 %all-gather.4 = f32[2,2,80]{2,1,0:T(2,128)S(1)} all-gather(f32[1,2,80]{2,1,0:T(2,128)S(1)} %maximum_bitcast_fusion), channel_id=2, replica_groups=mesh['x'=4,'zl'=4,'zh'=2,'y'=8,'core'=2] {'zh'}, dimensions={0}, use_global_device_ids=true | all-gather | bytes 1920 | tf_op jit(solution)/shard_map/all_gather | solution.py:30
  46.5 0.2 copy.21
  46.7 0.3 reshape.144
  47.0 0.8 multiply_convert_fusion
  47.9 0.0 all-gather.8.cloned.1.call-update
  47.9 0.0 all-gather.10.cloned.1.call-start
  47.9 0.3 reshape.140
  48.2 0.1 multiply_convert_fusion.1
  48.4 30.2 %all-gather.2 = bf16[320,1536]{1,0:T(8,128)(2,1)S(1)} all-gather(bf16[40,1536]{1,0:T(8,128)(2,1)S(1)} %get-tuple-element.5), channel_id=4, replica_groups=mesh['x'=4,'zl'=4,'zh'=2,'y'=8,'core'=2] {'zh','zl'}, dimensions={0}, use_global_device_ids=true | all-gather | bytes 1105920 | tf_op jit(solution)/shard_map/all_gather | solution.py:117
  78.6 26.3 %all-gather.1 = bf16[320,1536]{1,0:T(8,128)(2,1)S(1)} all-gather(bf16[40,1536]{1,0:T(8,128)(2,1)S(1)} %get-tuple-element.6), channel_id=3, replica_groups=mesh['x'=4,'zl'=4,'zh'=2,'y'=8,'core'=2] {'zh','zl'}, dimensions={0}, use_global_device_ids=true | all-gather | bytes 1105920 | tf_op jit(solution)/shard_map/all_gather | solution.py:117
  105.0 0.7 pad_maximum_fusion
  105.7 0.0 all-gather.10.cloned.1.call-update
  105.7 0.1 broadcast_select_fusion.1
  105.9 0.2 constant_dynamic-slice_fusion
  106.1 0.8 copy.24
  107.0 6.5 %rev.3 = bf16[2,4,33,1536]{3,0,1,2:T(2,128)(2,1)S(1)} reverse(bf16[2,4,33,1536]{3,0,1,2:T(2,128)(2,1)S(1)} %copy.24), dimensions={0} | reverse | bytes 1622016 | tf_op jit(solution)/shard_map/rev | solution.py:126
  113.4 1.1 fusion
  114.6 0.5 reshape.142
  115.1 0.0 copy-start
  115.1 2.5 %collective-permute-start.1 = (bf16[33,4,3072]{2,1,0:T(4,128)(2,1)S(1)}, bf16[33,4,3072]{2,1,0:T(4,128)(2,1)S(1)}, u32[]{:S(2)}, u32[]{:S(2)}) collective-permute-start(bf16[33,4,3072]{2,1,0:T(4,128)(2,1)S(1)} %reshape.142), channel_id=1, source_target_pairs={{0,128},{128,256},{256,384},{384,0},{1,129},{129,257},{257,385},{3... | collective-permute-start | bytes 2433032 | tf_op jit(solution)/shard_map/ppermute | solution.py:23
  117.6 3.3 %collective-permute-start = (bf16[33,4,3072]{2,1,0:T(4,128)(2,1)S(1)}, bf16[33,4,3072]{2,1,0:T(4,128)(2,1)S(1)}, u32[]{:S(2)}, u32[]{:S(2)}) collective-permute-start(bf16[33,4,3072]{2,1,0:T(4,128)(2,1)S(1)} %reshape.142), channel_id=1, source_target_pairs={{0,384},{128,0},{256,128},{384,256},{1,385},{129,1},{257,129},{385... | collective-permute-start | bytes 2433032 | tf_op jit(solution)/shard_map/ppermute | solution.py:23
  121.0 12.6 %collective-permute-done.1 = bf16[33,4,3072]{2,1,0:T(4,128)(2,1)S(1)} collective-permute-done((bf16[33,4,3072]{2,1,0:T(4,128)(2,1)S(1)}, bf16[33,4,3072]{2,1,0:T(4,128)(2,1)S(1)}, u32[]{:S(2)}, u32[]{:S(2)}) %collective-permute-start.1) | collective-permute-done | bytes 811040 | tf_op jit(solution)/shard_map/ppermute | solution.py:23
  133.6 0.0 copy-start.1
  133.6 0.3 slice.80
  133.9 3.5 %collective-permute-start.2 = (bf16[33,2,3072]{2,1,0:T(2,128)(2,1)S(1)}, bf16[33,2,3072]{2,1,0:T(2,128)(2,1)S(1)}, u32[]{:S(2)}, u32[]{:S(2)}) collective-permute-start(bf16[33,2,3072]{2,1,0:T(2,128)(2,1)S(1)} %slice.80), channel_id=1, source_target_pairs={{0,128},{128,256},{256,384},{384,0},{1,129},{129,257},{257,385},{3... | collective-permute-start | bytes 1216520 | tf_op jit(solution)/shard_map/ppermute | solution.py:23
  137.4 0.0 collective-permute-done
  137.4 0.0 copy-done.1
  137.5 0.0 copy-start.2
  137.5 0.5 slice.81
  137.9 0.5 copy-done.2
  138.5 2.3 %collective-permute-start.3 = (bf16[33,2,3072]{2,1,0:T(2,128)(2,1)S(1)}, bf16[33,2,3072]{2,1,0:T(2,128)(2,1)}, u32[]{:S(2)}, u32[]{:S(2)}) collective-permute-start(bf16[33,2,3072]{2,1,0:T(2,128)(2,1)S(1)} %slice.81), channel_id=1, source_target_pairs={{0,384},{128,0},{256,128},{384,256},{1,385},{129,1},{257,129},{385... | collective-permute-start | bytes 1216520 | tf_op jit(solution)/shard_map/ppermute | solution.py:23
  140.8 2.9 %collective-permute-done.2 = bf16[33,2,3072]{2,1,0:T(2,128)(2,1)S(1)} collective-permute-done((bf16[33,2,3072]{2,1,0:T(2,128)(2,1)S(1)}, bf16[33,2,3072]{2,1,0:T(2,128)(2,1)S(1)}, u32[]{:S(2)}, u32[]{:S(2)}) %collective-permute-start.2) | collective-permute-done | bytes 405536 | tf_op jit(solution)/shard_map/ppermute | solution.py:23
  143.7 0.0 copy-done
  143.7 0.0 copy-start.3
  143.7 0.7 copy-done.3
  144.4 5.1 %collective-permute-done.3 = bf16[33,2,3072]{2,1,0:T(2,128)(2,1)} collective-permute-done((bf16[33,2,3072]{2,1,0:T(2,128)(2,1)S(1)}, bf16[33,2,3072]{2,1,0:T(2,128)(2,1)}, u32[]{:S(2)}, u32[]{:S(2)}) %collective-permute-start.3) | collective-permute-done | bytes 405536 | tf_op jit(solution)/shard_map/ppermute | solution.py:23
  149.6 14.3 %concatenate.6 = bf16[33,16,3072]{2,1,0:T(8,128)(2,1)S(1)} concatenate(bf16[33,4,3072]{2,1,0:T(4,128)(2,1)} %copy-done, bf16[33,4,3072]{2,1,0:T(4,128)(2,1)} %copy-done.2, bf16[33,2,3072]{2,1,0:T(2,128)(2,1)} %copy-done.3, bf16[33,2,3072]{2,1,0:T(2,128)(2,1)} %collective-permute-done.3, bf16[33,4,3072]{2,1,0:T(4,128)(2,1)} %copy-done.1), dimensions={1} | concatenate | bytes 6488064 | tf_op jit(solution)/shard_map/concatenate | solution.py:42
  163.8 0.0 all-gather.8.cloned.1.call-done.near
  163.9 0.0 all-gather.10.cloned.1.call-done
  163.9 11.9 %shard_map.17 = f32[33,16,1056]{2,1,0:T(8,128)} custom-call(s32[1]{0:T(128)} %bitcast.place, bf16[528,3072]{1,0:T(8,128)(2,1)S(1)} %bitcast.59, bf16[16,80,1536]{2,1,0:T(8,128)(2,1)} %all-gather.8.cloned.1.call-done.near, bf16[16,80,1536]{2,1,0:T(8,128)(2,1)} %bitcast.65), custom_call_target="tpu_custom_call" | custom-call | flops 3425697792 | bytes 14000000 | tf_op jit(solution)/shard_map/pallas_call | solution.py:83
  (15 shorter events, 0.2 us)
Async XLA Ops:
  6.5 157.3 %all-gather.8.cloned.1.call-start = ((), (), s32[]{:S(2)}) async-start(), calls=%async_computation.1 | async-start | bytes 4177920 | tf_op jit(solution)/shard_map/all_gather | solution.py:113
  47.9 116.0 %all-gather.10.cloned.1.call-start = ((), (), s32[]{:S(2)}) async-start(), calls=%async_computation.2 | async-start | bytes 4177920 | tf_op jit(solution)/shard_map/all_gather | solution.py:122
  115.1 28.6 %copy-start = (bf16[33,4,3072]{2,1,0:T(4,128)(2,1)}, bf16[33,4,3072]{2,1,0:T(4,128)(2,1)S(1)}, u32[]{:S(2)}) copy-start(bf16[33,4,3072]{2,1,0:T(4,128)(2,1)S(1)} %reshape.142) | copy-start | bytes 2433028
  115.1 18.5 %collective-permute-start.1 = (bf16[33,4,3072]{2,1,0:T(4,128)(2,1)S(1)}, bf16[33,4,3072]{2,1,0:T(4,128)(2,1)S(1)}, u32[]{:S(2)}, u32[]{:S(2)}) collective-permute-start(bf16[33,4,3072]{2,1,0:T(4,128)(2,1)S(1)} %reshape.142), channel_id=1, source_target_pairs={{0,128},{128,256},{256,384},{384,0},{1,129},{129,257},{257,385},{3... | collective-permute-start | bytes 2433032 | tf_op jit(solution)/shard_map/ppermute | solution.py:23
  117.6 19.8 %collective-permute-start = (bf16[33,4,3072]{2,1,0:T(4,128)(2,1)S(1)}, bf16[33,4,3072]{2,1,0:T(4,128)(2,1)S(1)}, u32[]{:S(2)}, u32[]{:S(2)}) collective-permute-start(bf16[33,4,3072]{2,1,0:T(4,128)(2,1)S(1)} %reshape.142), channel_id=1, source_target_pairs={{0,384},{128,0},{256,128},{384,256},{1,385},{129,1},{257,129},{385... | collective-permute-start | bytes 2433032 | tf_op jit(solution)/shard_map/ppermute | solution.py:23
  133.6 3.9 %copy-start.1 = (bf16[33,4,3072]{2,1,0:T(4,128)(2,1)}, bf16[33,4,3072]{2,1,0:T(4,128)(2,1)S(1)}, u32[]{:S(2)}) copy-start(bf16[33,4,3072]{2,1,0:T(4,128)(2,1)S(1)} %collective-permute-done.1) | copy-start | bytes 2433028
  133.9 9.8 %collective-permute-start.2 = (bf16[33,2,3072]{2,1,0:T(2,128)(2,1)S(1)}, bf16[33,2,3072]{2,1,0:T(2,128)(2,1)S(1)}, u32[]{:S(2)}, u32[]{:S(2)}) collective-permute-start(bf16[33,2,3072]{2,1,0:T(2,128)(2,1)S(1)} %slice.80), channel_id=1, source_target_pairs={{0,128},{128,256},{256,384},{384,0},{1,129},{129,257},{257,385},{3... | collective-permute-start | bytes 1216520 | tf_op jit(solution)/shard_map/ppermute | solution.py:23
  137.5 1.0 copy-start.2
  138.5 11.1 %collective-permute-start.3 = (bf16[33,2,3072]{2,1,0:T(2,128)(2,1)S(1)}, bf16[33,2,3072]{2,1,0:T(2,128)(2,1)}, u32[]{:S(2)}, u32[]{:S(2)}) collective-permute-start(bf16[33,2,3072]{2,1,0:T(2,128)(2,1)S(1)} %slice.81), channel_id=1, source_target_pairs={{0,384},{128,0},{256,128},{384,256},{1,385},{129,1},{257,129},{385... | collective-permute-start | bytes 1216520 | tf_op jit(solution)/shard_map/ppermute | solution.py:23
  143.7 0.7 copy-start.3
Sparse Core Ops, SparseCore 0:
  48.0 41.5 all-gather.7
  105.8 38.4 all-gather.9

commit v5 on v4

v5 whole, which is shorter than its diff:
```python
import jax
import jax.numpy as jnp
from jax import lax
from jax.experimental import pallas as pl
from jax.experimental.pallas import tpu as pltpu
from jax.sharding import Mesh, PartitionSpec as P

TIME = 3072
HALF = TIME // 2
AXES = ("x", "zl", "zh", "y", "core")
SIZES = (4, 4, 2, 8, 2)
BULK = ("zh", "y", "core")
SHARE = 33
WINDOW = 40
ROWS = 1056
GROUP = 8 * SHARE

epsilon = 1e-06


def shift(array, axis, by):
    size = lax.axis_size(axis)
    return lax.ppermute(array, axis, [(i, (i + by) % size) for i in range(size)])


def pack(windows):
    n = windows.shape[0]
    tail = windows[:, 64:].reshape(n, 16, 3, 32).transpose(0, 2, 1, 3).reshape(n, 48, 32)
    tail = jnp.pad(tail, ((0, 0), (0, 16), (0, 0)))
    return jnp.concatenate([windows[:, :64], tail], axis=2)


def unpack(pieces):
    n = pieces.shape[0]
    tail = pieces[:, :48, 96:].reshape(n, 3, 16, 32).transpose(0, 2, 1, 3).reshape(n, 16, 96)
    return jnp.concatenate([pieces[:, :, :96], tail], axis=1)


def standardize(half):
    mean = jnp.sum(half, axis=1) / HALF
    from_mean = half - mean[:, None]
    deviation = jnp.sum(from_mean * from_mean, axis=1)
    both = lax.all_gather(jnp.stack([mean, deviation]), "zh")
    average = (both[0, 0] + both[1, 0]) * 0.5
    between = both[0, 0] - both[1, 0]
    squares = both[0, 1] + both[1, 1] + (HALF * 0.5) * (between * between)
    scale = lax.rsqrt(squares / TIME + epsilon)
    return ((half - average[:, None]) * scale[:, None]).astype(jnp.bfloat16)


def gather_x(part):
    after = shift(part, "x", 1)
    before = shift(part, "x", -1)
    cut = HALF // 2
    far = [shift(after[:, :cut], "x", 1), shift(before[:, cut:], "x", -1)]
    return jnp.concatenate([part, before, jnp.concatenate(far, axis=1), after], axis=0)


def product_kernel(place, first, second, windows, out, held, block, turned, arrived):
    copies = []
    for h in range(2):
        yc = pl.ds(8 * h, 8)
        copy = pltpu.make_async_copy(windows.at[yc], held.at[yc], arrived.at[h])
        copy.start()
        copies.append(copy)

    def place_rows(h):
        copies[h].wait()
        for w in range(2):
            for i in range(8):
                start = GROUP * (2 * w + h) + 32 * i
                size = 32 if i < 7 else 40
                rows = slice(WINDOW * w, WINDOW * w + size)
                for t in range(2):
                    steps = slice(HALF * t, HALF * t + HALF)
                    block[start : start + size, steps] = held[8 * h + i, t, rows, :]

    def multiply_rows(low, high):
        product = 0.0
        for t, part in enumerate((first, second)):
            product += lax.dot_general(
                part[...],
                block[low:high, HALF * t : HALF * t + HALF],
                (((1,), (1,)), ((), ())),
                preferred_element_type=jnp.float32,
            )
        product = product * (1.0 / TIME)
        for k in range(4):
            turned[k, :, : high - low] = product[132 * k : 132 * k + 132, :]
        for x in range(4):
            rows = turned[lax.rem(x - place[0] + 4, 4), :, : high - low]
            out[:, 4 * x : 4 * x + 4, low:high] = rows.reshape(SHARE, 4, high - low)

    place_rows(0)
    multiply_rows(0, 256)
    place_rows(1)
    multiply_rows(256, 512)
    multiply_rows(512, 768)
    multiply_rows(768, ROWS)


def multiply(first, second, windows):
    place = lax.axis_index("x").astype(jnp.int32).reshape(1)
    return pl.pallas_call(
        product_kernel,
        out_shape=jax.ShapeDtypeStruct((SHARE, 16, ROWS), jnp.float32),
        in_specs=[
            pl.BlockSpec(memory_space=pltpu.SMEM),
            pl.BlockSpec(memory_space=pltpu.VMEM),
            pl.BlockSpec(memory_space=pltpu.VMEM),
            pl.BlockSpec(memory_space=pltpu.HBM),
        ],
        out_specs=pl.BlockSpec(memory_space=pltpu.VMEM),
        scratch_shapes=[
            pltpu.VMEM((16, 2, 2 * WINDOW, HALF), jnp.bfloat16),
            pltpu.VMEM((ROWS, TIME), jnp.bfloat16),
            pltpu.VMEM((4, 4 * SHARE, 384), jnp.float32),
            pltpu.SemaphoreType.DMA((2,)),
        ],
        compiler_params=pltpu.CompilerParams(vmem_limit_bytes=48 * 1024 * 1024),
        cost_estimate=pl.CostEstimate(
            flops=2 * 528 * ROWS * TIME, bytes_accessed=14_000_000, transcendentals=0
        ),
    )(place, first, second, windows)


def on_device(series):
    steps = series.shape[1]
    groups = series.reshape(2, 2, GROUP, steps)
    windows = jnp.stack([groups[:, :, 32 * i : 32 * i + WINDOW] for i in range(8)], axis=2)
    windows = windows.transpose(1, 2, 0, 3, 4).reshape(16, 2 * WINDOW, steps)
    pieces = unpack(lax.all_to_all(pack(windows), ("y", "core"), 0, 0, tiled=True))
    zscore = standardize(pieces.transpose(1, 0, 2).reshape(2 * WINDOW, HALF))

    pair = lax.all_gather(zscore, "zh")
    gathered = lax.all_gather(pair, ("y", "core"))

    offset = WINDOW * lax.axis_index("zh") + lax.rem(lax.axis_index(BULK), 8)
    mine = lax.dynamic_slice_in_dim(pair, offset, SHARE, 1)
    halves = [
        gather_x(lax.all_gather(mine[t], "zl").transpose(1, 0, 2).reshape(SHARE * 4, HALF))
        for t in range(2)
    ]
    return multiply(*halves, gathered).transpose(1, 0, 2)


def solution(mesh):
    split = Mesh(mesh.devices.reshape(SIZES), AXES)
    return jax.shard_map(
        on_device,
        mesh=split,
        in_specs=(P(("x", "zl"), BULK),),
        out_specs=P(None, BULK, ("x", "zl")),
        check_vma=False,
    )
```

time: 184 us -> 146 us (0.79)
  local copies, waits for them, and re-layouts: 26.5 us -> 4.48 us
  waiting for transfers between devices: 20.8 us -> 6.75 us
  starting transfers between devices: 11.7 us -> 25.5 us
  blocking collectives: 94.7 us -> 83.6 us
  other arithmetic: 3.36 us -> 1.19 us
    concatenate x1 -> x0, local copies, waits for them, and re-layouts: 14.3 us -> none  [gather_x(): return jnp.concatenate([part, before, *far, after], axis=1)]
    ppermute x4 -> x8, waiting for transfers between devices: 20.7 us -> 6.71 us  [shift(): lax.ppermute(array, axis, [(i, (i + by) % size) for i in range(size)])]
    ppermute x4 -> x8, starting transfers between devices: 11.7 us -> 25.5 us  [shift(): lax.ppermute(array, axis, [(i, (i + by) % size) for i in range(size)])]
    all_gather x2 -> x3, blocking collectives: 56.6 us -> 49.4 us  [the longest x2 35.9 us: on_device(): lax.all_gather(mine[t], 'zl').transpose(1, 0, 2).reshape(SHARE * 4, HALF)]
    rev x1 -> x0, local copies, waits for them, and re-layouts: 6.47 us -> none  [on_device(): mine = jnp.where(zh == 0, mine, mine[::-1])]
    all_to_all x1, blocking collectives: 26.9 us -> 23 us  [on_device(): lax.all_to_all(pack(windows), ('y', 'core'), 0, 0, tiled=True)]
    unnamed x17 -> x20, local copies, waits for them, and re-layouts: 3.4 us -> 1.3 us
  transfers between devices with their start and end apart: 6 -> 9, of which waited for: 3 -> 3; matrix products, arithmetic and copies ran while one was open for 14% -> 2% of each run, Pallas kernels for 0% -> 0%
where the time goes in v5:
time: 146 us
  blocking collectives  83.6 us (57%)
  starting transfers between devices  25.5 us (17%)
  between operations  13.8 us (9%)
  Pallas kernels  10.3 us (7%)
  waiting for transfers between devices  6.75 us (5%)
  local copies, waits for them, and re-layouts  4.48 us (3%)
    all_gather x2, blocking collectives, on_device(): lax.all_gather(mine[t], 'zl').transpose(1, 0, 2).reshape(SHARE * 4, HALF)  35.9 us
    ppermute x8, starting transfers between devices, shift(): lax.ppermute(array, axis, [(i, (i + by) % size) for i in range(size)])  25.5 us
    all_to_all x1, blocking collectives, on_device(): lax.all_to_all(pack(windows), ('y', 'core'), 0, 0, tiled=True)  23 us
    all_gather x1, blocking collectives, on_device(): pair = lax.all_gather(zscore, 'zh')  13.5 us
    all_gather x1, blocking collectives, standardize(): both = lax.all_gather(jnp.stack([mean, deviation]), 'zh')  11.2 us
    pallas_call x1, Pallas kernels, multiply(): pl.pallas_call(product_kernel, out_shape=jax.ShapeDtypeStruct((SHARE, 16,...  10.3 us
    ppermute x8, waiting for transfers between devices, shift(): lax.ppermute(array, axis, [(i, (i + by) % size) for i in range(size)])  6.71 us
  transfers between devices with their start and end apart: 9, of which 3 were waited for; matrix products, arithmetic and copies ran while one was open for 2% of the time, Pallas kernels for 0%

profile of v5, /device:TPU:6, one launch (start us, length us, event | category | flops | bytes accessed | tf_op | source)
XLA Modules:
  0.0 145.5 jit_solution(6539554003045896487)
XLA Ops:
  6.5 1.2 copy.19
  8.0 0.2 reshape.147
  8.3 0.2 select_maximum_fusion
  8.5 23.0 %all_to_all.5 = f32[16,64,128]{2,1,0:T(8,128)S(1)} all-to-all(f32[16,64,128]{2,1,0:T(8,128)S(1)} %select_maximum_fusion), channel_id=1, replica_groups=mesh['x'=4,'zl'=4,'zh'=2,'y'=8,'core'=2] {'y','core'}, dimensions={0} | all-to-all | bytes 1048576 | tf_op jit(solution)/shard_map/all_to_all | solution.py:132
  31.5 0.2 slice.101
  31.7 0.2 copy.27
  31.9 0.2 reshape.150
  32.1 0.2 fusion
  32.3 0.3 multiply_reduce_fusion
  32.5 11.2 %all-gather.2 = f32[2,2,80]{2,1,0:T(2,128)S(1)} all-gather(f32[1,2,80]{2,1,0:T(2,128)S(1)} %maximum_bitcast_fusion), channel_id=2, replica_groups=mesh['x'=4,'zl'=4,'zh'=2,'y'=8,'core'=2] {'zh'}, dimensions={0}, use_global_device_ids=true | all-gather | bytes 1920 | tf_op jit(solution)/shard_map/all_gather | solution.py:43
  43.8 0.2 copy.23
  44.0 0.3 reshape.151
  44.3 0.1 multiply_convert_fusion
  44.4 13.5 %all_gather.24 = bf16[2,80,1536]{2,1,0:T(8,128)(2,1)} all-gather(bf16[1,80,1536]{2,1,0:T(8,128)(2,1)S(1)} %multiply_convert_fusion), channel_id=1, replica_groups=mesh['x'=4,'zl'=4,'zh'=2,'y'=8,'core'=2] {'zh'}, dimensions={0}, use_global_device_ids=true | all-gather | bytes 737280 | tf_op jit(solution)/shard_map/all_gather | solution.py:135
  57.9 0.0 all-gather.5.cloned.1.call-update
  57.9 1.1 constant_dynamic-slice_fusion.1
  59.0 21.1 %all_gather.26 = bf16[4,33,1536]{2,1,0:T(8,128)(2,1)S(1)} all-gather(bf16[1,33,1536]{2,1,0:T(8,128)(2,1)S(1)} %get-tuple-element.7), channel_id=1, replica_groups=mesh['x'=4,'zl'=4,'zh'=2,'y'=8,'core'=2] {'zl'}, dimensions={0}, use_global_device_ids=true | all-gather | bytes 506880 | tf_op jit(solution)/shard_map/all_gather | solution.py:141
  80.0 0.2 copy.25
  80.3 0.1 reshape.153
  80.4 2.4 %collective-permute-start.5 = (bf16[132,1536]{1,0:T(8,128)(2,1)S(1)}, bf16[132,1536]{1,0:T(8,128)(2,1)S(1)}, u32[]{:S(2)}, u32[]{:S(2)}) collective-permute-start(bf16[132,1536]{1,0:T(8,128)(2,1)S(1)} %reshape.153), channel_id=1, source_target_pairs={{0,128},{128,256},{256,384},{384,0},{1,129},{129,257},{257,385},{3... | collective-permute-start | bytes 1216520 | tf_op jit(solution)/shard_map/ppermute | solution.py:23
  82.8 3.5 %collective-permute-start.4 = (bf16[132,1536]{1,0:T(8,128)(2,1)S(1)}, bf16[132,1536]{1,0:T(8,128)(2,1)S(1)}, u32[]{:S(2)}, u32[]{:S(2)}) collective-permute-start(bf16[132,1536]{1,0:T(8,128)(2,1)S(1)} %reshape.153), channel_id=1, source_target_pairs={{0,384},{128,0},{256,128},{384,256},{1,385},{129,1},{257,129},{385... | collective-permute-start | bytes 1216520 | tf_op jit(solution)/shard_map/ppermute | solution.py:23
  86.2 14.8 %all_gather.25 = bf16[4,33,1536]{2,1,0:T(8,128)(2,1)S(1)} all-gather(bf16[1,33,1536]{2,1,0:T(8,128)(2,1)S(1)} %get-tuple-element.8), channel_id=1, replica_groups=mesh['x'=4,'zl'=4,'zh'=2,'y'=8,'core'=2] {'zl'}, dimensions={0}, use_global_device_ids=true | all-gather | bytes 506880 | tf_op jit(solution)/shard_map/all_gather | solution.py:141
  101.0 0.2 copy.24
  101.2 0.1 reshape.152
  101.3 0.0 copy-start
  101.3 3.6 %collective-permute-start.1 = (bf16[132,1536]{1,0:T(8,128)(2,1)S(1)}, bf16[132,1536]{1,0:T(8,128)(2,1)S(1)}, u32[]{:S(2)}, u32[]{:S(2)}) collective-permute-start(bf16[132,1536]{1,0:T(8,128)(2,1)S(1)} %reshape.152), channel_id=1, source_target_pairs={{0,128},{128,256},{256,384},{384,0},{1,129},{129,257},{257,385},{3... | collective-permute-start | bytes 1216520 | tf_op jit(solution)/shard_map/ppermute | solution.py:23
  105.0 2.2 %collective-permute-start = (bf16[132,1536]{1,0:T(8,128)(2,1)S(1)}, bf16[132,1536]{1,0:T(8,128)(2,1)S(1)}, u32[]{:S(2)}, u32[]{:S(2)}) collective-permute-start(bf16[132,1536]{1,0:T(8,128)(2,1)S(1)} %reshape.152), channel_id=1, source_target_pairs={{0,384},{128,0},{256,128},{384,256},{1,385},{129,1},{257,129},{385... | collective-permute-start | bytes 1216520 | tf_op jit(solution)/shard_map/ppermute | solution.py:23
  107.2 0.0 collective-permute-done.5
  107.2 4.8 %collective-permute-start.6 = (bf16[132,768]{1,0:T(8,128)(2,1)S(1)}, bf16[132,768]{1,0:T(8,128)(2,1)S(1)}, u32[]{:S(2)}, u32[]{:S(2)}) collective-permute-start(bf16[132,768]{1,0:T(8,128)(2,1)S(1)} %slice.108), channel_id=1, source_target_pairs={{0,128},{128,256},{256,384},{384,0},{1,129},{129,257},{257,385},{3... | collective-permute-start | bytes 608264 | tf_op jit(solution)/shard_map/ppermute | solution.py:23
  112.1 0.0 collective-permute-done.4
  112.1 1.9 %collective-permute-start.7 = (bf16[132,768]{1,0:T(8,128)(2,1)S(1)}, bf16[132,768]{1,0:T(8,128)(2,1)S(1)}, u32[]{:S(2)}, u32[]{:S(2)}) collective-permute-start(bf16[132,768]{1,0:T(8,128)(2,1)S(1)} %slice.109), channel_id=1, source_target_pairs={{0,384},{128,0},{256,128},{384,256},{1,385},{129,1},{257,129},{385... | collective-permute-start | bytes 608264 | tf_op jit(solution)/shard_map/ppermute | solution.py:23
  114.0 0.0 collective-permute-done.1
  114.0 0.0 copy-start.2
  114.1 5.1 %collective-permute-start.2 = (bf16[132,768]{1,0:T(8,128)(2,1)S(1)}, bf16[132,768]{1,0:T(8,128)(2,1)S(1)}, u32[]{:S(2)}, u32[]{:S(2)}) collective-permute-start(bf16[132,768]{1,0:T(8,128)(2,1)S(1)} %slice.106), channel_id=1, source_target_pairs={{0,128},{128,256},{256,384},{384,0},{1,129},{129,257},{257,385},{3... | collective-permute-start | bytes 608264 | tf_op jit(solution)/shard_map/ppermute | solution.py:23
  119.2 0.0 collective-permute-done
  119.3 1.9 %collective-permute-start.3 = (bf16[132,768]{1,0:T(8,128)(2,1)S(1)}, bf16[132,768]{1,0:T(8,128)(2,1)S(1)}, u32[]{:S(2)}, u32[]{:S(2)}) collective-permute-start(bf16[132,768]{1,0:T(8,128)(2,1)S(1)} %slice.107), channel_id=1, source_target_pairs={{0,384},{128,0},{256,128},{384,256},{1,385},{129,1},{257,129},{385... | collective-permute-start | bytes 608264 | tf_op jit(solution)/shard_map/ppermute | solution.py:23
  121.2 0.0 collective-permute-done.6
  121.2 0.0 copy-done
  121.2 0.0 copy-done.2
  121.2 0.0 copy-done.4
  121.2 0.8 collective-permute-done.7
  122.0 0.2 pad_maximum_fusion.1.second
  122.3 0.2 collective-permute-done.2
  122.5 5.7 %collective-permute-done.3 = bf16[132,768]{1,0:T(8,128)(2,1)S(1)} collective-permute-done((bf16[132,768]{1,0:T(8,128)(2,1)S(1)}, bf16[132,768]{1,0:T(8,128)(2,1)S(1)}, u32[]{:S(2)}, u32[]{:S(2)}) %collective-permute-start.3) | collective-permute-done | bytes 202784 | tf_op jit(solution)/shard_map/ppermute | solution.py:23
  128.2 0.0 copy-done.3
  128.2 0.2 pad_maximum_fusion.first
  128.4 0.0 all-gather.5.cloned.1.call-done
  128.4 10.3 %shard_map.17 = f32[33,16,1056]{2,1,0:T(8,128)} custom-call(s32[1]{0:T(128)} %bitcast.place, bf16[528,1536]{1,0:T(8,128)(2,1)S(1)} %pad_maximum_fusion.first, bf16[528,1536]{1,0:T(8,128)(2,1)S(1)} %pad_maximum_fusion.1.second, bf16[16,2,80,1536]{3,2,1,0:T(8,128)(2,1)} %bitcast.60), custom_call_target="tpu_custom_call" | custom-call | flops 3425697792 | bytes 14000000 | tf_op jit(solution)/shard_map/pallas_call | solution.py:104
  (26 shorter events, 0.3 us)
Async XLA Ops:
  6.5 121.9 %all-gather.5.cloned.1.call-start = ((), (), s32[]{:S(2)}) async-start(), calls=%async_computation.1 | async-start | bytes 8355840 | tf_op jit(solution)/shard_map/all_gather | solution.py:136
  80.4 26.8 %collective-permute-start.5 = (bf16[132,1536]{1,0:T(8,128)(2,1)S(1)}, bf16[132,1536]{1,0:T(8,128)(2,1)S(1)}, u32[]{:S(2)}, u32[]{:S(2)}) collective-permute-start(bf16[132,1536]{1,0:T(8,128)(2,1)S(1)} %reshape.153), channel_id=1, source_target_pairs={{0,128},{128,256},{256,384},{384,0},{1,129},{129,257},{257,385},{3... | collective-permute-start | bytes 1216520 | tf_op jit(solution)/shard_map/ppermute | solution.py:23
  82.8 29.3 %collective-permute-start.4 = (bf16[132,1536]{1,0:T(8,128)(2,1)S(1)}, bf16[132,1536]{1,0:T(8,128)(2,1)S(1)}, u32[]{:S(2)}, u32[]{:S(2)}) collective-permute-start(bf16[132,1536]{1,0:T(8,128)(2,1)S(1)} %reshape.153), channel_id=1, source_target_pairs={{0,384},{128,0},{256,128},{384,256},{1,385},{129,1},{257,129},{385... | collective-permute-start | bytes 1216520 | tf_op jit(solution)/shard_map/ppermute | solution.py:23
  101.3 19.9 %copy-start = (bf16[132,1536]{1,0:T(8,128)(2,1)}, bf16[132,1536]{1,0:T(8,128)(2,1)S(1)}, u32[]{:S(2)}) copy-start(bf16[132,1536]{1,0:T(8,128)(2,1)S(1)} %reshape.152) | copy-start | bytes 1216516
  101.3 12.7 %collective-permute-start.1 = (bf16[132,1536]{1,0:T(8,128)(2,1)S(1)}, bf16[132,1536]{1,0:T(8,128)(2,1)S(1)}, u32[]{:S(2)}, u32[]{:S(2)}) collective-permute-start(bf16[132,1536]{1,0:T(8,128)(2,1)S(1)} %reshape.152), channel_id=1, source_target_pairs={{0,128},{128,256},{256,384},{384,0},{1,129},{129,257},{257,385},{3... | collective-permute-start | bytes 1216520 | tf_op jit(solution)/shard_map/ppermute | solution.py:23
  105.0 14.3 %collective-permute-start = (bf16[132,1536]{1,0:T(8,128)(2,1)S(1)}, bf16[132,1536]{1,0:T(8,128)(2,1)S(1)}, u32[]{:S(2)}, u32[]{:S(2)}) collective-permute-start(bf16[132,1536]{1,0:T(8,128)(2,1)S(1)} %reshape.152), channel_id=1, source_target_pairs={{0,384},{128,0},{256,128},{384,256},{1,385},{129,1},{257,129},{385... | collective-permute-start | bytes 1216520 | tf_op jit(solution)/shard_map/ppermute | solution.py:23
  107.2 13.9 %collective-permute-start.6 = (bf16[132,768]{1,0:T(8,128)(2,1)S(1)}, bf16[132,768]{1,0:T(8,128)(2,1)S(1)}, u32[]{:S(2)}, u32[]{:S(2)}) collective-permute-start(bf16[132,768]{1,0:T(8,128)(2,1)S(1)} %slice.108), channel_id=1, source_target_pairs={{0,128},{128,256},{256,384},{384,0},{1,129},{129,257},{257,385},{3... | collective-permute-start | bytes 608264 | tf_op jit(solution)/shard_map/ppermute | solution.py:23
  112.1 9.9 %collective-permute-start.7 = (bf16[132,768]{1,0:T(8,128)(2,1)S(1)}, bf16[132,768]{1,0:T(8,128)(2,1)S(1)}, u32[]{:S(2)}, u32[]{:S(2)}) collective-permute-start(bf16[132,768]{1,0:T(8,128)(2,1)S(1)} %slice.109), channel_id=1, source_target_pairs={{0,384},{128,0},{256,128},{384,256},{1,385},{129,1},{257,129},{385... | collective-permute-start | bytes 608264 | tf_op jit(solution)/shard_map/ppermute | solution.py:23
  114.0 7.2 %copy-start.2 = (bf16[132,1536]{1,0:T(8,128)(2,1)}, bf16[132,1536]{1,0:T(8,128)(2,1)S(1)}, u32[]{:S(2)}) copy-start(bf16[132,1536]{1,0:T(8,128)(2,1)S(1)} %collective-permute-done.1) | copy-start | bytes 1216516
  114.1 8.4 %collective-permute-start.2 = (bf16[132,768]{1,0:T(8,128)(2,1)S(1)}, bf16[132,768]{1,0:T(8,128)(2,1)S(1)}, u32[]{:S(2)}, u32[]{:S(2)}) collective-permute-start(bf16[132,768]{1,0:T(8,128)(2,1)S(1)} %slice.106), channel_id=1, source_target_pairs={{0,128},{128,256},{256,384},{384,0},{1,129},{129,257},{257,385},{3... | collective-permute-start | bytes 608264 | tf_op jit(solution)/shard_map/ppermute | solution.py:23
  119.2 2.0 %copy-start.4 = (bf16[132,1536]{1,0:T(8,128)(2,1)}, bf16[132,1536]{1,0:T(8,128)(2,1)S(1)}, u32[]{:S(2)}) copy-start(bf16[132,1536]{1,0:T(8,128)(2,1)S(1)} %collective-permute-done) | copy-start | bytes 1216516
  119.3 8.9 %collective-permute-start.3 = (bf16[132,768]{1,0:T(8,128)(2,1)S(1)}, bf16[132,768]{1,0:T(8,128)(2,1)S(1)}, u32[]{:S(2)}, u32[]{:S(2)}) collective-permute-start(bf16[132,768]{1,0:T(8,128)(2,1)S(1)} %slice.107), channel_id=1, source_target_pairs={{0,384},{128,0},{256,128},{384,256},{1,385},{129,1},{257,129},{385... | collective-permute-start | bytes 608264 | tf_op jit(solution)/shard_map/ppermute | solution.py:23
  122.0 6.1 %copy-start.1 = (bf16[132,1536]{1,0:T(8,128)(2,1)S(1)}, bf16[132,1536]{1,0:T(8,128)(2,1)}, u32[]{:S(2)}) copy-start(bf16[132,1536]{1,0:T(8,128)(2,1)} %copy-done) | copy-start | bytes 1216516
  122.0 6.1 %copy-start.3 = (bf16[132,1536]{1,0:T(8,128)(2,1)S(1)}, bf16[132,1536]{1,0:T(8,128)(2,1)}, u32[]{:S(2)}) copy-start(bf16[132,1536]{1,0:T(8,128)(2,1)} %copy-done.2) | copy-start | bytes 1216516
  122.0 6.1 %copy-start.5 = (bf16[132,1536]{1,0:T(8,128)(2,1)S(1)}, bf16[132,1536]{1,0:T(8,128)(2,1)}, u32[]{:S(2)}) copy-start(bf16[132,1536]{1,0:T(8,128)(2,1)} %copy-done.4) | copy-start | bytes 1216516
Sparse Core Ops, SparseCore 0:
  58.0 57.5 all-gather.4

commit v6 on v3

v6 whole, which is shorter than its diff:
```python
import jax
import jax.numpy as jnp
from jax import lax
from jax.experimental import pallas as pl
from jax.experimental.pallas import tpu as pltpu
from jax.sharding import Mesh, PartitionSpec as P

TIME = 3072
HALF = TIME // 2
AXES = ("x", "zl", "zh", "y", "core")
SIZES = (4, 4, 2, 8, 2)
BULK = ("zh", "y", "core")
SHARE = 33
FOUR = 4 * SHARE
WINDOW = 40
ROWS = 1056
GROUP = 8 * SHARE
EDGES = (0, 256, 512, 768, ROWS)

epsilon = 1e-06


def standardize(rows):
    average = jnp.sum(rows, axis=1, keepdims=True) / TIME
    centered = rows - average
    variance = jnp.sum(centered * centered, axis=1, keepdims=True) / TIME
    return (centered * lax.rsqrt(variance + epsilon)).astype(jnp.bfloat16)


def shift(array, axis, by):
    size = lax.axis_size(axis)
    return lax.ppermute(array, axis, [(i, (i + by) % size) for i in range(size)])


def contract(first, second, block, low, high):
    product = 0.0
    for t, part in enumerate((first, second)):
        product += lax.dot_general(
            part[...],
            block[low:high, HALF * t : HALF * t + HALF],
            (((1,), (1,)), ((), ())),
            preferred_element_type=jnp.float32,
        )
    return product * (1.0 / TIME)


def near_kernel(first, second, windows, block, near, held, arrived):
    copies = []
    for group in range(4):
        half, parity = divmod(group, 2)
        copy = pltpu.make_async_copy(
            windows.at[pl.ds(8 * parity, 8), half], held.at[group], arrived.at[group]
        )
        copy.start()
        copies.append(copy)
    for group in range(4):
        copies[group].wait()
        for i in range(8):
            start = GROUP * group + 32 * i
            size = 32 if i < 7 else 40
            block[start : start + size, :] = held[group, i, :size, :]
        low, high = EDGES[group], EDGES[group + 1]
        product = contract(first, second, block, low, high)
        for k in range(3):
            near[k, :, low:high] = product[FOUR * k : FOUR * k + FOUR, :]


def far_kernel(place, first, second, block, near, out, turned):
    for low, high in zip(EDGES[:-1], EDGES[1:]):
        width = high - low
        product = contract(first, second, block, low, high)
        turned[2, :, :width] = product
        for n, k in enumerate((0, 1, 3)):
            turned[k, :, :width] = near[n, :, low:high]
        for x in range(4):
            rows = turned[lax.rem(x - place[0] + 4, 4), :, :width]
            out[:, 4 * x : 4 * x + 4, low:high] = rows.reshape(SHARE, 4, width)


VMEM = pl.BlockSpec(memory_space=pltpu.VMEM)


def multiply_near(first, second, windows):
    rows = first.shape[0]
    return pl.pallas_call(
        near_kernel,
        out_shape=(
            jax.ShapeDtypeStruct((ROWS, TIME), jnp.bfloat16),
            jax.ShapeDtypeStruct((3, FOUR, ROWS), jnp.float32),
        ),
        in_specs=[VMEM, VMEM, pl.BlockSpec(memory_space=pl.ANY)],
        out_specs=(VMEM, VMEM),
        scratch_shapes=[
            pltpu.VMEM((4, 8, WINDOW, TIME), jnp.bfloat16),
            pltpu.SemaphoreType.DMA((4,)),
        ],
        compiler_params=pltpu.CompilerParams(vmem_limit_bytes=48 * 1024 * 1024),
        cost_estimate=pl.CostEstimate(
            flops=2 * rows * ROWS * TIME, bytes_accessed=14_000_000, transcendentals=0
        ),
    )(first, second, windows)


def multiply_far(first, second, block, near):
    place = lax.axis_index("x").astype(jnp.int32).reshape(1)
    return pl.pallas_call(
        far_kernel,
        out_shape=jax.ShapeDtypeStruct((SHARE, 16, ROWS), jnp.float32),
        in_specs=[pl.BlockSpec(memory_space=pltpu.SMEM), VMEM, VMEM, VMEM, VMEM],
        out_specs=VMEM,
        scratch_shapes=[pltpu.VMEM((4, FOUR, 384), jnp.float32)],
        compiler_params=pltpu.CompilerParams(vmem_limit_bytes=12 * 1024 * 1024),
        cost_estimate=pl.CostEstimate(
            flops=2 * FOUR * ROWS * TIME, bytes_accessed=8_000_000, transcendentals=0
        ),
    )(place, first, second, block, near)


def on_device(series):
    groups = series.reshape(4, GROUP, -1)
    windows = jnp.stack([groups[:, 32 * i : 32 * i + WINDOW] for i in range(8)], axis=1)
    windows = windows.reshape(32, WINDOW, -1)
    pieces = lax.all_to_all(windows, BULK, 0, 0, tiled=True)
    window = standardize(pieces.transpose(1, 0, 2).reshape(WINDOW, TIME))
    own = lax.dynamic_slice_in_dim(window, lax.rem(lax.axis_index(BULK), 8), SHARE, 0)
    pair = lax.all_gather(window, "zh")
    gathered = lax.all_gather(pair, ("y", "core"))

    part = lax.all_gather(own, "zl").transpose(1, 0, 2).reshape(FOUR, TIME)
    first, second = part[:, :HALF], part[:, HALF:]
    after_first, before_second = shift(first, "x", 1), shift(second, "x", -1)
    after_second, before_first = shift(second, "x", 1), shift(first, "x", -1)
    far_first, far_second = shift(after_first, "x", 1), shift(before_second, "x", -1)

    near_first = jnp.concatenate([first, before_first, after_first])
    near_second = jnp.concatenate([second, before_second, after_second])
    block, near = multiply_near(near_first, near_second, gathered)
    return multiply_far(far_first, far_second, block, near).transpose(1, 0, 2)


def solution(mesh):
    split = Mesh(mesh.devices.reshape(SIZES), AXES)
    return jax.shard_map(
        on_device,
        mesh=split,
        in_specs=(P(("x", "zl"), BULK),),
        out_specs=P(None, BULK, ("x", "zl")),
        check_vma=False,
    )
```

time: 146 us -> 145 us (level)
  the two profiles are of different devices: /device:TPU:6 before, /device:TPU:8 now
where the time goes in v6:
time: 145 us
  blocking collectives  77.8 us (54%)
  starting transfers between devices  20.6 us (14%)
  Pallas kernels  14.7 us (10%)
  between operations  13.7 us (9%)
  waiting for transfers between devices  8.74 us (6%)
  local copies, waits for them, and re-layouts  5.99 us (4%)
  other arithmetic  3.18 us (2%)
    all_to_all x1, blocking collectives, on_device(): pieces = lax.all_to_all(windows, BULK, 0, 0, tiled=True)  40.7 us
    all_gather x1, blocking collectives, on_device(): part = lax.all_gather(own, 'zl').transpose(1, 0, 2).reshape(FOUR, TIME)  25.7 us
    ppermute x6, starting transfers between devices, shift(): lax.ppermute(array, axis, [(i, (i + by) % size) for i in range(size)])  20.6 us
    all_gather x1, blocking collectives, on_device(): pair = lax.all_gather(window, 'zh')  11.4 us
    pallas_call x1, Pallas kernels, multiply_near(): pl.pallas_call(near_kernel, out_shape=(jax.ShapeDtypeStruct((ROWS, TIME),...  10.4 us
    ppermute x6, waiting for transfers between devices, shift(): lax.ppermute(array, axis, [(i, (i + by) % size) for i in range(size)])  8.7 us
    pallas_call x1, Pallas kernels, multiply_far(): pl.pallas_call(far_kernel, out_shape=jax.ShapeDtypeStruct((SHARE, 16, ROW...  4.3 us
    unnamed x12, local copies, waits for them, and re-layouts  4.11 us
  transfers between devices with their start and end apart: 7, of which 2 were waited for; matrix products, arithmetic and copies ran while one was open for 3% of the time, Pallas kernels for 7%

profile of v6, /device:TPU:8, one launch (start us, length us, event | category | flops | bytes accessed | tf_op | source)
XLA Modules:
  0.0 144.6 jit_solution(2602670306540113465)
XLA Ops:
  6.5 0.0 all-gather.5.cloned.1.call-start
  6.5 1.2 copy.10
  7.9 40.7 %all_to_all.5 = f32[32,40,96]{2,1,0:T(8,128)S(1)} all-to-all(f32[32,40,96]{2,1,0:T(8,128)S(1)} %bitcast.53), channel_id=1, replica_groups=mesh['x'=4,'zl'=4,'zh'=2,'y'=8,'core'=2] {'zh','y','core'}, dimensions={0} | all-to-all | bytes 983040 | tf_op jit(solution)/shard_map/all_to_all | solution.py:123
  48.6 0.2 reduce_sum.18
  48.8 0.3 multiply_reduce_fusion
  49.0 0.1 copy.12
  49.2 0.3 reshape.93
  49.5 0.1 multiply_convert_fusion
  49.6 11.4 %all_gather.18 = bf16[2,40,3072]{2,1,0:T(8,128)(2,1)} all-gather(bf16[1,40,3072]{2,1,0:T(8,128)(2,1)S(1)} %multiply_convert_fusion), channel_id=1, replica_groups=mesh['x'=4,'zl'=4,'zh'=2,'y'=8,'core'=2] {'zh'}, dimensions={0}, use_global_device_ids=true | all-gather | bytes 737280 | tf_op jit(solution)/shard_map/all_gather | solution.py:126
  61.1 0.0 all-gather.5.cloned.1.call-update
  61.1 0.1 dynamic-slice.1
  61.2 0.1 dynamic-slice
  61.3 0.3 reshape.91
  61.6 0.1 fusion.2
  61.7 25.7 %all-gather.2 = bf16[4,33,3072]{2,1,0:T(8,128)(2,1)S(1)} all-gather(bf16[1,33,3072]{2,1,0:T(8,128)(2,1)S(1)} %fusion.2), channel_id=2, replica_groups=mesh['x'=4,'zl'=4,'zh'=2,'y'=8,'core'=2] {'zl'}, dimensions={0}, use_global_device_ids=true | all-gather | bytes 1013760 | tf_op jit(solution)/shard_map/all_gather | solution.py:129
  87.4 0.6 copy.13
  88.0 0.2 reshape.92
  88.2 0.1 fusion.11
  88.3 0.0 copy-start.1
  88.3 4.7 %collective-permute-start.2 = (bf16[132,1536]{1,0:T(8,128)(2,1)S(1)}, bf16[132,1536]{1,0:T(8,128)(2,1)}, u32[]{:S(2)}, u32[]{:S(2)}) collective-permute-start(bf16[132,1536]{1,0:T(8,128)(2,1)S(1)} %get-tuple-element.9), channel_id=1, source_target_pairs={{0,384},{128,0},{256,128},{384,256},{1,385},{129,1},{257,129},{385... | collective-permute-start | bytes 1216520 | tf_op jit(solution)/shard_map/ppermute | solution.py:32
  93.0 1.9 %collective-permute-start = (bf16[132,1536]{1,0:T(8,128)(2,1)S(1)}, bf16[132,1536]{1,0:T(8,128)(2,1)}, u32[]{:S(2)}, u32[]{:S(2)}) collective-permute-start(bf16[132,1536]{1,0:T(8,128)(2,1)S(1)} %get-tuple-element.10), channel_id=1, source_target_pairs={{0,128},{128,256},{256,384},{384,0},{1,129},{129,257},{257,385},{3... | collective-permute-start | bytes 1216520 | tf_op jit(solution)/shard_map/ppermute | solution.py:32
  94.9 2.7 %collective-permute-start.5 = (bf16[132,1536]{1,0:T(8,128)(2,1)S(1)}, bf16[132,1536]{1,0:T(8,128)(2,1)S(1)}, u32[]{:S(2)}, u32[]{:S(2)}) collective-permute-start(bf16[132,1536]{1,0:T(8,128)(2,1)S(1)} %get-tuple-element.9), channel_id=1, source_target_pairs={{0,128},{128,256},{256,384},{384,0},{1,129},{129,257},{257,385},{3... | collective-permute-start | bytes 1216520 | tf_op jit(solution)/shard_map/ppermute | solution.py:32
  97.6 4.4 %collective-permute-start.4 = (bf16[132,1536]{1,0:T(8,128)(2,1)S(1)}, bf16[132,1536]{1,0:T(8,128)(2,1)}, u32[]{:S(2)}, u32[]{:S(2)}) collective-permute-start(bf16[132,1536]{1,0:T(8,128)(2,1)S(1)} %get-tuple-element.10), channel_id=1, source_target_pairs={{0,384},{128,0},{256,128},{384,256},{1,385},{129,1},{257,129},{385... | collective-permute-start | bytes 1216520 | tf_op jit(solution)/shard_map/ppermute | solution.py:32
  102.0 0.0 collective-permute-done.2
  102.0 5.0 %collective-permute-start.3 = (bf16[132,1536]{1,0:T(8,128)(2,1)}, bf16[132,1536]{1,0:T(8,128)(2,1)S(1)}, u32[]{:S(2)}, u32[]{:S(2)}) collective-permute-start(bf16[132,1536]{1,0:T(8,128)(2,1)} %collective-permute-done.2), channel_id=1, source_target_pairs={{0,384},{128,0},{256,128},{384,256},{1,385},{129,1},{257,129},{385... | collective-permute-start | bytes 1216520 | tf_op jit(solution)/shard_map/ppermute | solution.py:32
  107.0 1.8 %collective-permute-done = bf16[132,1536]{1,0:T(8,128)(2,1)} collective-permute-done((bf16[132,1536]{1,0:T(8,128)(2,1)S(1)}, bf16[132,1536]{1,0:T(8,128)(2,1)}, u32[]{:S(2)}, u32[]{:S(2)}) %collective-permute-start) | collective-permute-done | bytes 405536 | tf_op jit(solution)/shard_map/ppermute | solution.py:32
  108.8 1.9 %collective-permute-start.1 = (bf16[132,1536]{1,0:T(8,128)(2,1)}, bf16[132,1536]{1,0:T(8,128)(2,1)S(1)}, u32[]{:S(2)}, u32[]{:S(2)}) collective-permute-start(bf16[132,1536]{1,0:T(8,128)(2,1)} %collective-permute-done), channel_id=1, source_target_pairs={{0,128},{128,256},{256,384},{384,0},{1,129},{129,257},{257,385},{3... | collective-permute-start | bytes 1216520 | tf_op jit(solution)/shard_map/ppermute | solution.py:32
  110.7 6.9 %collective-permute-done.5 = bf16[132,1536]{1,0:T(8,128)(2,1)S(1)} collective-permute-done((bf16[132,1536]{1,0:T(8,128)(2,1)S(1)}, bf16[132,1536]{1,0:T(8,128)(2,1)S(1)}, u32[]{:S(2)}, u32[]{:S(2)}) %collective-permute-start.5) | collective-permute-done | bytes 405536 | tf_op jit(solution)/shard_map/ppermute | solution.py:32
  117.6 1.1 pad_maximum_fusion.1.second
  118.8 0.0 copy-done.1
  118.8 0.0 collective-permute-done.4
  118.8 1.4 pad_maximum_fusion.first
  120.2 0.0 all-gather.5.cloned.1.call-done
  120.2 10.4 %shard_map.17 = (bf16[1056,3072]{1,0:T(8,128)(2,1)}, f32[3,132,1056]{2,1,0:T(8,128)S(1)}) custom-call(bf16[396,1536]{1,0:T(8,128)(2,1)S(1)} %pad_maximum_fusion.first, bf16[396,1536]{1,0:T(8,128)(2,1)S(1)} %pad_maximum_fusion.1.second, bf16[16,2,40,3072]{3,2,1,0:T(8,128)(2,1)} %bitcast.43), custom_call_target="tpu_custom_call" | custom-call | flops 2569273344 | bytes 14000000 | tf_op jit(solution)/shard_map/pallas_call | solution.py:85
  130.6 0.0 collective-permute-done.3.second
  130.6 0.0 collective-permute-done.1.first
  130.6 0.0 copy-start
  130.6 2.8 %copy-done = bf16[1056,3072]{1,0:T(8,128)(2,1)S(1)} copy-done((bf16[1056,3072]{1,0:T(8,128)(2,1)S(1)}, bf16[1056,3072]{1,0:T(8,128)(2,1)}, u32[]{:S(2)}) %copy-start) | copy-done | bytes 6488088
  133.4 4.3 %shard_map.18 = f32[33,16,1056]{2,1,0:T(8,128)} custom-call(s32[1]{0:T(128)} %bitcast.place, bf16[132,1536]{1,0:T(8,128)(2,1)S(1)} %collective-permute-done.1.first, bf16[132,1536]{1,0:T(8,128)(2,1)S(1)} %collective-permute-done.3.second, bf16[1056,3072]{1,0:T(8,128)(2,1)S(1)} %copy-done, f32[3,132,1056]{2,1,0:T(8,128)S(1)} %get-tuple-element.8.near), custom_call_target="tpu_custom_call" | custom-call | flops 856424448 | bytes 8000000 | tf_op jit(solution)/shard_map/pallas_call | solution.py:106
  (11 shorter events, 0.1 us)
Async XLA Ops:
  6.5 113.7 %all-gather.5.cloned.1.call-start = ((), (), s32[]{:S(2)}) async-start(), calls=%async_computation.1 | async-start | bytes 8355840 | tf_op jit(solution)/shard_map/all_gather | solution.py:127
  88.3 30.5 %copy-start.1 = (bf16[132,1536]{1,0:T(8,128)(2,1)}, bf16[132,1536]{1,0:T(8,128)(2,1)S(1)}, u32[]{:S(2)}) copy-start(bf16[132,1536]{1,0:T(8,128)(2,1)S(1)} %get-tuple-element.10) | copy-start | bytes 1216516
  88.3 13.7 %collective-permute-start.2 = (bf16[132,1536]{1,0:T(8,128)(2,1)S(1)}, bf16[132,1536]{1,0:T(8,128)(2,1)}, u32[]{:S(2)}, u32[]{:S(2)}) collective-permute-start(bf16[132,1536]{1,0:T(8,128)(2,1)S(1)} %get-tuple-element.9), channel_id=1, source_target_pairs={{0,384},{128,0},{256,128},{384,256},{1,385},{129,1},{257,129},{385... | collective-permute-start | bytes 1216520 | tf_op jit(solution)/shard_map/ppermute | solution.py:32
  93.0 15.8 %collective-permute-start = (bf16[132,1536]{1,0:T(8,128)(2,1)S(1)}, bf16[132,1536]{1,0:T(8,128)(2,1)}, u32[]{:S(2)}, u32[]{:S(2)}) collective-permute-start(bf16[132,1536]{1,0:T(8,128)(2,1)S(1)} %get-tuple-element.10), channel_id=1, source_target_pairs={{0,128},{128,256},{256,384},{384,0},{1,129},{129,257},{257,385},{3... | collective-permute-start | bytes 1216520 | tf_op jit(solution)/shard_map/ppermute | solution.py:32
  94.9 22.7 %collective-permute-start.5 = (bf16[132,1536]{1,0:T(8,128)(2,1)S(1)}, bf16[132,1536]{1,0:T(8,128)(2,1)S(1)}, u32[]{:S(2)}, u32[]{:S(2)}) collective-permute-start(bf16[132,1536]{1,0:T(8,128)(2,1)S(1)} %get-tuple-element.9), channel_id=1, source_target_pairs={{0,128},{128,256},{256,384},{384,0},{1,129},{129,257},{257,385},{3... | collective-permute-start | bytes 1216520 | tf_op jit(solution)/shard_map/ppermute | solution.py:32
  97.6 21.2 %collective-permute-start.4 = (bf16[132,1536]{1,0:T(8,128)(2,1)S(1)}, bf16[132,1536]{1,0:T(8,128)(2,1)}, u32[]{:S(2)}, u32[]{:S(2)}) collective-permute-start(bf16[132,1536]{1,0:T(8,128)(2,1)S(1)} %get-tuple-element.10), channel_id=1, source_target_pairs={{0,384},{128,0},{256,128},{384,256},{1,385},{129,1},{257,129},{385... | collective-permute-start | bytes 1216520 | tf_op jit(solution)/shard_map/ppermute | solution.py:32
  102.0 28.6 %collective-permute-start.3 = (bf16[132,1536]{1,0:T(8,128)(2,1)}, bf16[132,1536]{1,0:T(8,128)(2,1)S(1)}, u32[]{:S(2)}, u32[]{:S(2)}) collective-permute-start(bf16[132,1536]{1,0:T(8,128)(2,1)} %collective-permute-done.2), channel_id=1, source_target_pairs={{0,384},{128,0},{256,128},{384,256},{1,385},{129,1},{257,129},{385... | collective-permute-start | bytes 1216520 | tf_op jit(solution)/shard_map/ppermute | solution.py:32
  108.8 21.8 %collective-permute-start.1 = (bf16[132,1536]{1,0:T(8,128)(2,1)}, bf16[132,1536]{1,0:T(8,128)(2,1)S(1)}, u32[]{:S(2)}, u32[]{:S(2)}) collective-permute-start(bf16[132,1536]{1,0:T(8,128)(2,1)} %collective-permute-done), channel_id=1, source_target_pairs={{0,128},{128,256},{256,384},{384,0},{1,129},{129,257},{257,385},{3... | collective-permute-start | bytes 1216520 | tf_op jit(solution)/shard_map/ppermute | solution.py:32
  130.6 2.8 %copy-start = (bf16[1056,3072]{1,0:T(8,128)(2,1)S(1)}, bf16[1056,3072]{1,0:T(8,128)(2,1)}, u32[]{:S(2)}) copy-start(bf16[1056,3072]{1,0:T(8,128)(2,1)} %get-tuple-element.7.block) | copy-start | bytes 19464196
Sparse Core Ops, SparseCore 0:
  61.2 53.7 all-gather.4

commit v7 on v6

--- a/solution.py
+++ b/solution.py
@@ -12,6 +12,7 @@
 BULK = ("zh", "y", "core")
 SHARE = 33
 FOUR = 4 * SHARE
+SLOT = 144
 WINDOW = 40
 ROWS = 1056
 GROUP = 8 * SHARE
@@ -44,7 +45,8 @@
     return product * (1.0 / TIME)
 
 
-def near_kernel(first, second, windows, block, near, held, arrived):
+def near_kernel(*refs):
+    pieces, (windows, block, near, held, parts, arrived) = refs[:6], refs[6:]
     copies = []
     for group in range(4):
         half, parity = divmod(group, 2)
@@ -53,6 +55,9 @@
         )
         copy.start()
         copies.append(copy)
+    for t in range(2):
+        for k in range(3):
+            parts[t, SLOT * k : SLOT * k + FOUR, :] = pieces[3 * t + k][...]
     for group in range(4):
         copies[group].wait()
         for i in range(8):
@@ -60,9 +65,9 @@
             size = 32 if i < 7 else 40
             block[start : start + size, :] = held[group, i, :size, :]
         low, high = EDGES[group], EDGES[group + 1]
-        product = contract(first, second, block, low, high)
+        product = contract(parts.at[0], parts.at[1], block, low, high)
         for k in range(3):
-            near[k, :, low:high] = product[FOUR * k : FOUR * k + FOUR, :]
+            near[k, :, low:high] = product[SLOT * k : SLOT * k + FOUR, :]
 
 
 def far_kernel(place, first, second, block, near, out, turned):
@@ -80,25 +85,25 @@
 VMEM = pl.BlockSpec(memory_space=pltpu.VMEM)
 
 
-def multiply_near(first, second, windows):
-    rows = first.shape[0]
+def multiply_near(pieces, windows):
     return pl.pallas_call(
         near_kernel,
         out_shape=(
             jax.ShapeDtypeStruct((ROWS, TIME), jnp.bfloat16),
             jax.ShapeDtypeStruct((3, FOUR, ROWS), jnp.float32),
         ),
-        in_specs=[VMEM, VMEM, pl.BlockSpec(memory_space=pl.ANY)],
+        in_specs=[VMEM] * 6 + [pl.BlockSpec(memory_space=pl.ANY)],
         out_specs=(VMEM, VMEM),
         scratch_shapes=[
             pltpu.VMEM((4, 8, WINDOW, TIME), jnp.bfloat16),
+            pltpu.VMEM((2, 3 * SLOT, HALF), jnp.bfloat16),
             pltpu.SemaphoreType.DMA((4,)),
         ],
-        compiler_params=pltpu.CompilerParams(vmem_limit_bytes=48 * 1024 * 1024),
+        compiler_params=pltpu.CompilerParams(vmem_limit_bytes=40 * 1024 * 1024),
         cost_estimate=pl.CostEstimate(
-            flops=2 * rows * ROWS * TIME, bytes_accessed=14_000_000, transcendentals=0
+            flops=6 * FOUR * ROWS * TIME, bytes_accessed=14_000_000, transcendentals=0
         ),
-    )(first, second, windows)
+    )(*pieces, windows)
 
 
 def multiply_far(first, second, block, near):
@@ -109,7 +114,7 @@
         in_specs=[pl.BlockSpec(memory_space=pltpu.SMEM), VMEM, VMEM, VMEM, VMEM],
         out_specs=VMEM,
         scratch_shapes=[pltpu.VMEM((4, FOUR, 384), jnp.float32)],
-        compiler_params=pltpu.CompilerParams(vmem_limit_bytes=12 * 1024 * 1024),
+        compiler_params=pltpu.CompilerParams(vmem_limit_bytes=24 * 1024 * 1024),
         cost_estimate=pl.CostEstimate(
             flops=2 * FOUR * ROWS * TIME, bytes_accessed=8_000_000, transcendentals=0
         ),
@@ -132,9 +137,8 @@
     after_second, before_first = shift(second, "x", 1), shift(first, "x", -1)
     far_first, far_second = shift(after_first, "x", 1), shift(before_second, "x", -1)
 
-    near_first = jnp.concatenate([first, before_first, after_first])
-    near_second = jnp.concatenate([second, before_second, after_second])
-    block, near = multiply_near(near_first, near_second, gathered)
+    pieces = (first, before_first, after_first, second, before_second, after_second)
+    block, near = multiply_near(pieces, gathered)
     return multiply_far(far_first, far_second, block, near).transpose(1, 0, 2)
 
 

time: 145 us -> 138 us (0.952)
  the two profiles are of different devices: /device:TPU:8 before, /device:TPU:6 now
where the time goes in v7:
time: 138 us; the launch traced here: 136 us
  blocking collectives  77.2 us (56%)
  starting transfers between devices  17.6 us (13%)
  between operations  13.6 us (10%)
  Pallas kernels  12.8 us (9%)
  waiting for transfers between devices  11 us (8%)
  local copies, waits for them, and re-layouts  3.15 us (2%)
    all_to_all x1, blocking collectives, on_device(): pieces = lax.all_to_all(windows, BULK, 0, 0, tiled=True)  40.4 us
    all_gather x1, blocking collectives, on_device(): part = lax.all_gather(own, 'zl').transpose(1, 0, 2).reshape(FOUR, TIME)  25.7 us
    ppermute x6, starting transfers between devices, shift(): lax.ppermute(array, axis, [(i, (i + by) % size) for i in range(size)])  17.6 us
    all_gather x1, blocking collectives, on_device(): pair = lax.all_gather(window, 'zh')  11.1 us
    ppermute x6, waiting for transfers between devices, shift(): lax.ppermute(array, axis, [(i, (i + by) % size) for i in range(size)])  9.39 us
    pallas_call x1, Pallas kernels, multiply_near(): pl.pallas_call(near_kernel, out_shape=(jax.ShapeDtypeStruct((ROWS, TIME),...  8.51 us
    pallas_call x1, Pallas kernels, multiply_far(): pl.pallas_call(far_kernel, out_shape=jax.ShapeDtypeStruct((SHARE, 16, ROW...  4.26 us
  transfers between devices with their start and end apart: 7, of which 4 were waited for; matrix products, arithmetic and copies ran while one was open for 1% of the time, Pallas kernels for 6%

profile of v7, /device:TPU:6, one launch (start us, length us, event | category | flops | bytes accessed | tf_op | source)
XLA Modules:
  0.0 136.1 jit_solution(10291462284676214860)
XLA Ops:
  6.5 0.0 all-gather.5.cloned.1.call-start
  6.5 1.2 copy.10
  7.9 40.4 %all_to_all.5 = f32[32,40,96]{2,1,0:T(8,128)S(1)} all-to-all(f32[32,40,96]{2,1,0:T(8,128)S(1)} %bitcast.53), channel_id=1, replica_groups=mesh['x'=4,'zl'=4,'zh'=2,'y'=8,'core'=2] {'zh','y','core'}, dimensions={0} | all-to-all | bytes 983040 | tf_op jit(solution)/shard_map/all_to_all | solution.py:128
  48.4 0.2 reduce_sum.18
  48.5 0.3 multiply_reduce_fusion
  48.8 0.1 copy.12
  48.9 0.3 reshape.93
  49.3 0.1 multiply_convert_fusion
  49.4 11.1 %all_gather.18 = bf16[2,40,3072]{2,1,0:T(8,128)(2,1)} all-gather(bf16[1,40,3072]{2,1,0:T(8,128)(2,1)S(1)} %multiply_convert_fusion), channel_id=1, replica_groups=mesh['x'=4,'zl'=4,'zh'=2,'y'=8,'core'=2] {'zh'}, dimensions={0}, use_global_device_ids=true | all-gather | bytes 737280 | tf_op jit(solution)/shard_map/all_gather | solution.py:131
  60.5 0.0 all-gather.5.cloned.1.call-update
  60.6 0.1 dynamic-slice.1
  60.7 0.1 dynamic-slice
  60.7 0.3 reshape.91
  61.1 0.1 fusion.2
  61.2 25.7 %all-gather.2 = bf16[4,33,3072]{2,1,0:T(8,128)(2,1)S(1)} all-gather(bf16[1,33,3072]{2,1,0:T(8,128)(2,1)S(1)} %fusion.2), channel_id=2, replica_groups=mesh['x'=4,'zl'=4,'zh'=2,'y'=8,'core'=2] {'zl'}, dimensions={0}, use_global_device_ids=true | all-gather | bytes 1013760 | tf_op jit(solution)/shard_map/all_gather | solution.py:134
  86.9 0.6 copy.13
  87.5 0.2 reshape.92
  87.7 0.1 fusion.11
  87.8 2.4 %collective-permute-start = (bf16[132,1536]{1,0:T(8,128)(2,1)S(1)}, bf16[132,1536]{1,0:T(8,128)(2,1)S(1)}, u32[]{:S(2)}, u32[]{:S(2)}) collective-permute-start(bf16[132,1536]{1,0:T(8,128)(2,1)S(1)} %get-tuple-element.10.refs_0_), channel_id=1, source_target_pairs={{0,128},{128,256},{256,384},{384,0},{1,129},{129,257},{257,385},{3... | collective-permute-start | bytes 1216520 | tf_op jit(solution)/shard_map/ppermute | solution.py:33
  90.2 3.5 %collective-permute-start.2 = (bf16[132,1536]{1,0:T(8,128)(2,1)S(1)}, bf16[132,1536]{1,0:T(8,128)(2,1)S(1)}, u32[]{:S(2)}, u32[]{:S(2)}) collective-permute-start(bf16[132,1536]{1,0:T(8,128)(2,1)S(1)} %get-tuple-element.9.refs_3_), channel_id=1, source_target_pairs={{0,384},{128,0},{256,128},{384,256},{1,385},{129,1},{257,129},{385... | collective-permute-start | bytes 1216520 | tf_op jit(solution)/shard_map/ppermute | solution.py:33
  93.6 2.7 %collective-permute-start.4 = (bf16[132,1536]{1,0:T(8,128)(2,1)S(1)}, bf16[132,1536]{1,0:T(8,128)(2,1)S(1)}, u32[]{:S(2)}, u32[]{:S(2)}) collective-permute-start(bf16[132,1536]{1,0:T(8,128)(2,1)S(1)} %get-tuple-element.10.refs_0_), channel_id=1, source_target_pairs={{0,384},{128,0},{256,128},{384,256},{1,385},{129,1},{257,129},{385... | collective-permute-start | bytes 1216520 | tf_op jit(solution)/shard_map/ppermute | solution.py:33
  96.4 4.3 %collective-permute-start.5 = (bf16[132,1536]{1,0:T(8,128)(2,1)S(1)}, bf16[132,1536]{1,0:T(8,128)(2,1)S(1)}, u32[]{:S(2)}, u32[]{:S(2)}) collective-permute-start(bf16[132,1536]{1,0:T(8,128)(2,1)S(1)} %get-tuple-element.9.refs_3_), channel_id=1, source_target_pairs={{0,128},{128,256},{256,384},{384,0},{1,129},{129,257},{257,385},{3... | collective-permute-start | bytes 1216520 | tf_op jit(solution)/shard_map/ppermute | solution.py:33
  100.7 0.3 collective-permute-done.refs_2_
  101.0 2.5 %collective-permute-start.1 = (bf16[132,1536]{1,0:T(8,128)(2,1)S(1)}, bf16[132,1536]{1,0:T(8,128)(2,1)S(1)}, u32[]{:S(2)}, u32[]{:S(2)}) collective-permute-start(bf16[132,1536]{1,0:T(8,128)(2,1)S(1)} %collective-permute-done.refs_2_), channel_id=1, source_target_pairs={{0,128},{128,256},{256,384},{384,0},{1,129},{129,257},{257,385},{3... | collective-permute-start | bytes 1216520 | tf_op jit(solution)/shard_map/ppermute | solution.py:33
  103.5 2.3 %collective-permute-done.2.refs_4_ = bf16[132,1536]{1,0:T(8,128)(2,1)S(1)} collective-permute-done((bf16[132,1536]{1,0:T(8,128)(2,1)S(1)}, bf16[132,1536]{1,0:T(8,128)(2,1)S(1)}, u32[]{:S(2)}, u32[]{:S(2)}) %collective-permute-start.2) | collective-permute-done | bytes 405536 | tf_op jit(solution)/shard_map/ppermute | solution.py:33
  105.8 2.2 %collective-permute-start.3 = (bf16[132,1536]{1,0:T(8,128)(2,1)S(1)}, bf16[132,1536]{1,0:T(8,128)(2,1)S(1)}, u32[]{:S(2)}, u32[]{:S(2)}) collective-permute-start(bf16[132,1536]{1,0:T(8,128)(2,1)S(1)} %collective-permute-done.2.refs_4_), channel_id=1, source_target_pairs={{0,384},{128,0},{256,128},{384,256},{1,385},{129,1},{257,129},{385... | collective-permute-start | bytes 1216520 | tf_op jit(solution)/shard_map/ppermute | solution.py:33
  108.1 6.7 %collective-permute-done.4.refs_1_ = bf16[132,1536]{1,0:T(8,128)(2,1)S(1)} collective-permute-done((bf16[132,1536]{1,0:T(8,128)(2,1)S(1)}, bf16[132,1536]{1,0:T(8,128)(2,1)S(1)}, u32[]{:S(2)}, u32[]{:S(2)}) %collective-permute-start.4) | collective-permute-done | bytes 405536 | tf_op jit(solution)/shard_map/ppermute | solution.py:33
  114.8 0.0 collective-permute-done.5.refs_5_
  114.8 1.6 %all-gather.5.cloned.1.call-done = bf16[32,40,3072]{2,1,0:T(8,128)(2,1)} async-done(((bf16[2,40,3072]{2,1,0:T(8,128)(2,1)}), bf16[32,40,3072]{2,1,0:T(8,128)(2,1)}) %all-gather.5.cloned.1.call-update) | async-done | bytes 7864336 | tf_op jit(solution)/shard_map/all_gather | solution.py:132
  116.4 8.5 %shard_map.17 = (bf16[1056,3072]{1,0:T(8,128)(2,1)S(1)}, f32[3,132,1056]{2,1,0:T(8,128)S(1)}) custom-call(bf16[132,1536]{1,0:T(8,128)(2,1)S(1)} %get-tuple-element.10.refs_0_, bf16[132,1536]{1,0:T(8,128)(2,1)S(1)} %collective-permute-done.4.refs_1_, bf16[132,1536]{1,0:T(8,128)(2,1)S(1)} %collective-permute-done.refs_2_, ...), custom_call_target="tpu_custom_call" | custom-call | flops 2569273344 | bytes 14000000 | tf_op jit(solution)/shard_map/pallas_call | solution.py:89
  125.0 0.0 collective-permute-done.1.first
  125.0 0.0 collective-permute-done.3.second
  125.0 4.3 %shard_map.18 = f32[33,16,1056]{2,1,0:T(8,128)} custom-call(s32[1]{0:T(128)} %bitcast.place, bf16[132,1536]{1,0:T(8,128)(2,1)S(1)} %collective-permute-done.1.first, bf16[132,1536]{1,0:T(8,128)(2,1)S(1)} %collective-permute-done.3.second, bf16[1056,3072]{1,0:T(8,128)(2,1)S(1)} %get-tuple-element.7.block, f32[3,132,1056]{2,1,0:T(8,128)S(1)} %get-tuple-element.8.near), custom_call_target="tpu_custom_call" | custom-call | flops 856424448 | bytes 8000000 | tf_op jit(solution)/shard_map/pallas_call | solution.py:111
  (11 shorter events, 0.1 us)
Async XLA Ops:
  6.5 109.9 %all-gather.5.cloned.1.call-start = ((), (), s32[]{:S(2)}) async-start(), calls=%async_computation.1 | async-start | bytes 8355840 | tf_op jit(solution)/shard_map/all_gather | solution.py:132
  87.8 13.3 %collective-permute-start = (bf16[132,1536]{1,0:T(8,128)(2,1)S(1)}, bf16[132,1536]{1,0:T(8,128)(2,1)S(1)}, u32[]{:S(2)}, u32[]{:S(2)}) collective-permute-start(bf16[132,1536]{1,0:T(8,128)(2,1)S(1)} %get-tuple-element.10.refs_0_), channel_id=1, source_target_pairs={{0,128},{128,256},{256,384},{384,0},{1,129},{129,257},{257,385},{3... | collective-permute-start | bytes 1216520 | tf_op jit(solution)/shard_map/ppermute | solution.py:33
  90.2 15.7 %collective-permute-start.2 = (bf16[132,1536]{1,0:T(8,128)(2,1)S(1)}, bf16[132,1536]{1,0:T(8,128)(2,1)S(1)}, u32[]{:S(2)}, u32[]{:S(2)}) collective-permute-start(bf16[132,1536]{1,0:T(8,128)(2,1)S(1)} %get-tuple-element.9.refs_3_), channel_id=1, source_target_pairs={{0,384},{128,0},{256,128},{384,256},{1,385},{129,1},{257,129},{385... | collective-permute-start | bytes 1216520 | tf_op jit(solution)/shard_map/ppermute | solution.py:33
  93.6 21.2 %collective-permute-start.4 = (bf16[132,1536]{1,0:T(8,128)(2,1)S(1)}, bf16[132,1536]{1,0:T(8,128)(2,1)S(1)}, u32[]{:S(2)}, u32[]{:S(2)}) collective-permute-start(bf16[132,1536]{1,0:T(8,128)(2,1)S(1)} %get-tuple-element.10.refs_0_), channel_id=1, source_target_pairs={{0,384},{128,0},{256,128},{384,256},{1,385},{129,1},{257,129},{385... | collective-permute-start | bytes 1216520 | tf_op jit(solution)/shard_map/ppermute | solution.py:33
  96.4 18.4 %collective-permute-start.5 = (bf16[132,1536]{1,0:T(8,128)(2,1)S(1)}, bf16[132,1536]{1,0:T(8,128)(2,1)S(1)}, u32[]{:S(2)}, u32[]{:S(2)}) collective-permute-start(bf16[132,1536]{1,0:T(8,128)(2,1)S(1)} %get-tuple-element.9.refs_3_), channel_id=1, source_target_pairs={{0,128},{128,256},{256,384},{384,0},{1,129},{129,257},{257,385},{3... | collective-permute-start | bytes 1216520 | tf_op jit(solution)/shard_map/ppermute | solution.py:33
  101.0 23.9 %collective-permute-start.1 = (bf16[132,1536]{1,0:T(8,128)(2,1)S(1)}, bf16[132,1536]{1,0:T(8,128)(2,1)S(1)}, u32[]{:S(2)}, u32[]{:S(2)}) collective-permute-start(bf16[132,1536]{1,0:T(8,128)(2,1)S(1)} %collective-permute-done.refs_2_), channel_id=1, source_target_pairs={{0,128},{128,256},{256,384},{384,0},{1,129},{129,257},{257,385},{3... | collective-permute-start | bytes 1216520 | tf_op jit(solution)/shard_map/ppermute | solution.py:33
  105.8 19.1 %collective-permute-start.3 = (bf16[132,1536]{1,0:T(8,128)(2,1)S(1)}, bf16[132,1536]{1,0:T(8,128)(2,1)S(1)}, u32[]{:S(2)}, u32[]{:S(2)}) collective-permute-start(bf16[132,1536]{1,0:T(8,128)(2,1)S(1)} %collective-permute-done.2.refs_4_), channel_id=1, source_target_pairs={{0,384},{128,0},{256,128},{384,256},{1,385},{129,1},{257,129},{385... | collective-permute-start | bytes 1216520 | tf_op jit(solution)/shard_map/ppermute | solution.py:33
Sparse Core Ops, SparseCore 0:
  60.7 55.7 all-gather.4

commit v8 on v7

--- a/solution.py
+++ b/solution.py
@@ -14,6 +14,7 @@
 FOUR = 4 * SHARE
 SLOT = 144
 WINDOW = 40
+WIDE = TIME + 128
 ROWS = 1056
 GROUP = 8 * SHARE
 EDGES = (0, 256, 512, 768, ROWS)
@@ -22,10 +23,30 @@
 
 
 def standardize(rows):
-    average = jnp.sum(rows, axis=1, keepdims=True) / TIME
+    axes = tuple(range(1, rows.ndim))
+    average = jnp.sum(rows, axis=axes, keepdims=True) / TIME
     centered = rows - average
-    variance = jnp.sum(centered * centered, axis=1, keepdims=True) / TIME
+    variance = jnp.sum(centered * centered, axis=axes, keepdims=True) / TIME
     return (centered * lax.rsqrt(variance + epsilon)).astype(jnp.bfloat16)
+
+
+def pack(series):
+    groups = series.reshape(4, GROUP, 96)
+    windows = jnp.stack([groups[:, 32 * i : 32 * i + WINDOW] for i in range(8)], axis=1)
+    windows = windows.reshape(32, WINDOW, 96)
+    single = groups[:, 256:].reshape(32, 1, 96)
+    cuts = [slice(32 * p, 32 * p + 32) for p in range(3)]
+    side = [windows[:, 32:, cut] for cut in cuts] + [single[:, :, cut] for cut in cuts]
+    side = jnp.concatenate(side + [jnp.zeros((32, 5, 32), series.dtype)], axis=1)
+    return jnp.concatenate([windows[:, :32], side], axis=2)
+
+
+def unpack(pieces):
+    side = pieces[:, :, 96:]
+    last = jnp.concatenate([side[:, 8 * p : 8 * p + 8] for p in range(3)], axis=2)
+    window = jnp.concatenate([pieces[:, :, :96], last], axis=1)
+    single = jnp.concatenate([side[:, 24 + p] for p in range(3)], axis=1)
+    return window.transpose(1, 0, 2).reshape(WINDOW, TIME), single[None]
 
 
 def shift(array, axis, by):
@@ -46,7 +67,7 @@
 
 
 def near_kernel(*refs):
-    pieces, (windows, block, near, held, parts, arrived) = refs[:6], refs[6:]
+    pieces, (windows, block, near, held, parts, singles, tail, arrived) = refs[:6], refs[6:]
     copies = []
     for group in range(4):
         half, parity = divmod(group, 2)
@@ -62,8 +83,13 @@
         copies[group].wait()
         for i in range(8):
             start = GROUP * group + 32 * i
-            size = 32 if i < 7 else 40
-            block[start : start + size, :] = held[group, i, :size, :]
+            block[start : start + 32, :] = held[group, i, :, :TIME]
+            singles[32 * i : 32 * i + 32, :] = held[group, i, :, TIME:].astype(jnp.float32)
+        for source in range(32):
+            steps = singles[pl.ds(source, 8, stride=32), :]
+            tail[:, 96 * source : 96 * source + 96] = steps[:, :96]
+        start = GROUP * group + 256
+        block[start : start + 8, :] = tail[...].astype(jnp.bfloat16)
         low, high = EDGES[group], EDGES[group + 1]
         product = contract(parts.at[0], parts.at[1], block, low, high)
         for k in range(3):
@@ -95,8 +121,10 @@
         in_specs=[VMEM] * 6 + [pl.BlockSpec(memory_space=pl.ANY)],
         out_specs=(VMEM, VMEM),
         scratch_shapes=[
-            pltpu.VMEM((4, 8, WINDOW, TIME), jnp.bfloat16),
+            pltpu.VMEM((4, 8, 32, WIDE), jnp.bfloat16),
             pltpu.VMEM((2, 3 * SLOT, HALF), jnp.bfloat16),
+            pltpu.VMEM((256, 128), jnp.float32),
+            pltpu.VMEM((8, TIME), jnp.float32),
             pltpu.SemaphoreType.DMA((4,)),
         ],
         compiler_params=pltpu.CompilerParams(vmem_limit_bytes=40 * 1024 * 1024),
@@ -122,14 +150,11 @@
 
 
 def on_device(series):
-    groups = series.reshape(4, GROUP, -1)
-    windows = jnp.stack([groups[:, 32 * i : 32 * i + WINDOW] for i in range(8)], axis=1)
-    windows = windows.reshape(32, WINDOW, -1)
-    pieces = lax.all_to_all(windows, BULK, 0, 0, tiled=True)
-    window = standardize(pieces.transpose(1, 0, 2).reshape(WINDOW, TIME))
+    window, single = unpack(lax.all_to_all(pack(series), BULK, 0, 0, tiled=True))
+    window, single = standardize(window), standardize(single)
     own = lax.dynamic_slice_in_dim(window, lax.rem(lax.axis_index(BULK), 8), SHARE, 0)
-    pair = lax.all_gather(window, "zh")
-    gathered = lax.all_gather(pair, ("y", "core"))
+    wide = jnp.concatenate([window[:32], jnp.pad(single[0], ((0, 0), (0, 32)))], axis=1)
+    gathered = lax.all_gather(lax.all_gather(wide, "zh"), ("y", "core"))
 
     part = lax.all_gather(own, "zl").transpose(1, 0, 2).reshape(FOUR, TIME)
     first, second = part[:, :HALF], part[:, HALF:]

time: 138 us -> 137 us (level)
  blocking collectives: 77.2 us -> 72.7 us
  other arithmetic: 0.68 us -> 3.62 us
  between operations: 13.6 us -> 16.3 us
  waiting for transfers between devices: 11 us -> 9.45 us
    reduce_sum x2 -> x6, other arithmetic: 0.43 us -> 3.19 us  [the longest x4 2.23 us: standardize(): average = jnp.sum(rows, axis=axes, keepdims=True) / TIME]
    all_to_all x1, blocking collectives: 40.4 us -> 38.1 us  [on_device(): lax.all_to_all(pack(series), BULK, 0, 0, tiled=True)]
    all_gather x1, waiting for transfers between devices: 1.63 us -> 0.01 us  [on_device(): gathered = lax.all_gather(lax.all_gather(wide, 'zh'), ('y', 'core'))]
    all_gather x1, blocking collectives: 25.7 us -> 24.2 us  [on_device(): part = lax.all_gather(own, 'zl').transpose(1, 0, 2).reshape(FOUR, TIME)]
  transfers between devices with their start and end apart: 7 -> 7, of which waited for: 4 -> 2; matrix products, arithmetic and copies ran while one was open for 1% -> 1% of each run, Pallas kernels for 6% -> 6%
where the time goes in v8:
time: 137 us; the launch traced here: 136 us
  blocking collectives  72.7 us (53%)
  starting transfers between devices  17.5 us (13%)
  between operations  16.3 us (12%)
  Pallas kernels  12.7 us (9%)
  waiting for transfers between devices  9.45 us (7%)
  other arithmetic  3.62 us (3%)
  local copies, waits for them, and re-layouts  3.38 us (2%)
    all_to_all x1, blocking collectives, on_device(): lax.all_to_all(pack(series), BULK, 0, 0, tiled=True)  38.1 us
    all_gather x1, blocking collectives, on_device(): part = lax.all_gather(own, 'zl').transpose(1, 0, 2).reshape(FOUR, TIME)  24.2 us
    ppermute x6, starting transfers between devices, shift(): lax.ppermute(array, axis, [(i, (i + by) % size) for i in range(size)])  17.5 us
    all_gather x1, blocking collectives, on_device(): gathered = lax.all_gather(lax.all_gather(wide, 'zh'), ('y', 'core'))  10.5 us
    ppermute x6, waiting for transfers between devices, shift(): lax.ppermute(array, axis, [(i, (i + by) % size) for i in range(size)])  9.43 us
    pallas_call x1, Pallas kernels, multiply_near(): pl.pallas_call(near_kernel, out_shape=(jax.ShapeDtypeStruct((ROWS, TIME),...  8.47 us
    pallas_call x1, Pallas kernels, multiply_far(): pl.pallas_call(far_kernel, out_shape=jax.ShapeDtypeStruct((SHARE, 16, ROW...  4.26 us
  transfers between devices with their start and end apart: 7, of which 2 were waited for; matrix products, arithmetic and copies ran while one was open for 1% of the time, Pallas kernels for 6%

profile of v8, /device:TPU:6, one launch (start us, length us, event | category | flops | bytes accessed | tf_op | source)
XLA Modules:
  0.0 135.8 jit_solution(3211390322071784554)
XLA Ops:
  6.5 0.0 all-gather.6.cloned.1.call-start
  6.5 1.2 copy.22
  8.0 0.1 fusion.18
  8.1 0.1 slice.119
  8.2 0.1 fusion.20
  8.3 0.1 concatenate.41
  8.5 0.2 pad_maximum_fusion
  8.7 38.1 %all_to_all.5 = f32[32,32,128]{2,1,0:T(8,128)S(1)} all-to-all(f32[32,32,128]{2,1,0:T(8,128)S(1)} %pad_maximum_fusion), channel_id=1, replica_groups=mesh['x'=4,'zl'=4,'zh'=2,'y'=8,'core'=2] {'zh','y','core'}, dimensions={0} | all-to-all | bytes 1048576 | tf_op jit(solution)/shard_map/all_to_all | solution.py:153
  46.8 0.7 slice_reduce_fusion
  47.5 0.7 reduce_sum.54
  48.1 0.6 reduce_sum.55
  50.6 0.7 fusion.15
  52.0 0.2 fusion.19
  52.2 0.2 fusion.1
  52.4 0.3 multiply_reduce_fusion
  52.7 0.1 copy.27
  52.9 0.3 reshape.120
  53.2 0.1 multiply_convert_fusion
  53.3 0.1 fusion.13
  53.5 10.5 %all-gather.1 = bf16[64,3200]{1,0:T(8,128)(2,1)} all-gather(bf16[32,3200]{1,0:T(8,128)(2,1)S(1)} %fusion.3), channel_id=3, replica_groups=mesh['x'=4,'zl'=4,'zh'=2,'y'=8,'core'=2] {'zh'}, dimensions={0}, use_global_device_ids=true | all-gather | bytes 614400 | tf_op jit(solution)/shard_map/all_gather | solution.py:157
  63.9 0.0 all-gather.6.cloned.1.call-update
  64.0 0.1 dynamic-slice_bitcast_fusion
  64.0 24.2 %all-gather.3 = bf16[4,33,3072]{2,1,0:T(8,128)(2,1)S(1)} all-gather(bf16[1,33,3072]{2,1,0:T(8,128)(2,1)S(1)} %dynamic-slice_bitcast_fusion), channel_id=2, replica_groups=mesh['x'=4,'zl'=4,'zh'=2,'y'=8,'core'=2] {'zl'}, dimensions={0}, use_global_device_ids=true | all-gather | bytes 1013760 | tf_op jit(solution)/shard_map/all_gather | solution.py:159
  88.2 0.6 copy.28
  88.8 0.2 reshape.121
  89.0 0.1 fusion.17
  89.1 2.4 %collective-permute-start = (bf16[132,1536]{1,0:T(8,128)(2,1)S(1)}, bf16[132,1536]{1,0:T(8,128)(2,1)S(1)}, u32[]{:S(2)}, u32[]{:S(2)}) collective-permute-start(bf16[132,1536]{1,0:T(8,128)(2,1)S(1)} %get-tuple-element.12.refs_0_), channel_id=1, source_target_pairs={{0,128},{128,256},{256,384},{384,0},{1,129},{129,257},{257,385},{3... | collective-permute-start | bytes 1216520 | tf_op jit(solution)/shard_map/ppermute | solution.py:54
  91.5 3.5 %collective-permute-start.2 = (bf16[132,1536]{1,0:T(8,128)(2,1)S(1)}, bf16[132,1536]{1,0:T(8,128)(2,1)S(1)}, u32[]{:S(2)}, u32[]{:S(2)}) collective-permute-start(bf16[132,1536]{1,0:T(8,128)(2,1)S(1)} %get-tuple-element.11.refs_3_), channel_id=1, source_target_pairs={{0,384},{128,0},{256,128},{384,256},{1,385},{129,1},{257,129},{385... | collective-permute-start | bytes 1216520 | tf_op jit(solution)/shard_map/ppermute | solution.py:54
  95.0 2.7 %collective-permute-start.4 = (bf16[132,1536]{1,0:T(8,128)(2,1)S(1)}, bf16[132,1536]{1,0:T(8,128)(2,1)S(1)}, u32[]{:S(2)}, u32[]{:S(2)}) collective-permute-start(bf16[132,1536]{1,0:T(8,128)(2,1)S(1)} %get-tuple-element.12.refs_0_), channel_id=1, source_target_pairs={{0,384},{128,0},{256,128},{384,256},{1,385},{129,1},{257,129},{385... | collective-permute-start | bytes 1216520 | tf_op jit(solution)/shard_map/ppermute | solution.py:54
  97.7 4.3 %collective-permute-start.5 = (bf16[132,1536]{1,0:T(8,128)(2,1)S(1)}, bf16[132,1536]{1,0:T(8,128)(2,1)S(1)}, u32[]{:S(2)}, u32[]{:S(2)}) collective-permute-start(bf16[132,1536]{1,0:T(8,128)(2,1)S(1)} %get-tuple-element.11.refs_3_), channel_id=1, source_target_pairs={{0,128},{128,256},{256,384},{384,0},{1,129},{129,257},{257,385},{3... | collective-permute-start | bytes 1216520 | tf_op jit(solution)/shard_map/ppermute | solution.py:54
  102.0 0.0 collective-permute-done.refs_2_
  102.0 2.4 %collective-permute-start.1 = (bf16[132,1536]{1,0:T(8,128)(2,1)S(1)}, bf16[132,1536]{1,0:T(8,128)(2,1)S(1)}, u32[]{:S(2)}, u32[]{:S(2)}) collective-permute-start(bf16[132,1536]{1,0:T(8,128)(2,1)S(1)} %collective-permute-done.refs_2_), channel_id=1, source_target_pairs={{0,128},{128,256},{256,384},{384,0},{1,129},{129,257},{257,385},{3... | collective-permute-start | bytes 1216520 | tf_op jit(solution)/shard_map/ppermute | solution.py:54
  104.5 2.7 %collective-permute-done.2.refs_4_ = bf16[132,1536]{1,0:T(8,128)(2,1)S(1)} collective-permute-done((bf16[132,1536]{1,0:T(8,128)(2,1)S(1)}, bf16[132,1536]{1,0:T(8,128)(2,1)S(1)}, u32[]{:S(2)}, u32[]{:S(2)}) %collective-permute-start.2) | collective-permute-done | bytes 405536 | tf_op jit(solution)/shard_map/ppermute | solution.py:54
  107.2 2.2 %collective-permute-start.3 = (bf16[132,1536]{1,0:T(8,128)(2,1)S(1)}, bf16[132,1536]{1,0:T(8,128)(2,1)S(1)}, u32[]{:S(2)}, u32[]{:S(2)}) collective-permute-start(bf16[132,1536]{1,0:T(8,128)(2,1)S(1)} %collective-permute-done.2.refs_4_), channel_id=1, source_target_pairs={{0,384},{128,0},{256,128},{384,256},{1,385},{129,1},{257,129},{385... | collective-permute-start | bytes 1216520 | tf_op jit(solution)/shard_map/ppermute | solution.py:54
  109.4 6.7 %collective-permute-done.4.refs_1_ = bf16[132,1536]{1,0:T(8,128)(2,1)S(1)} collective-permute-done((bf16[132,1536]{1,0:T(8,128)(2,1)S(1)}, bf16[132,1536]{1,0:T(8,128)(2,1)S(1)}, u32[]{:S(2)}, u32[]{:S(2)}) %collective-permute-start.4) | collective-permute-done | bytes 405536 | tf_op jit(solution)/shard_map/ppermute | solution.py:54
  116.1 0.0 collective-permute-done.5.refs_5_
  116.1 0.0 all-gather.6.cloned.1.call-done
  116.1 8.5 %shard_map.17 = (bf16[1056,3072]{1,0:T(8,128)(2,1)S(1)}, f32[3,132,1056]{2,1,0:T(8,128)S(1)}) custom-call(bf16[132,1536]{1,0:T(8,128)(2,1)S(1)} %get-tuple-element.12.refs_0_, bf16[132,1536]{1,0:T(8,128)(2,1)S(1)} %collective-permute-done.4.refs_1_, bf16[132,1536]{1,0:T(8,128)(2,1)S(1)} %collective-permute-done.refs_2_, ...), custom_call_target="tpu_custom_call" | custom-call | flops 2569273344 | bytes 14000000 | tf_op jit(solution)/shard_map/pallas_call | solution.py:115
  124.6 0.0 collective-permute-done.1.first
  124.6 0.0 collective-permute-done.3.second
  124.6 4.3 %shard_map.18 = f32[33,16,1056]{2,1,0:T(8,128)} custom-call(s32[1]{0:T(128)} %bitcast.place, bf16[132,1536]{1,0:T(8,128)(2,1)S(1)} %collective-permute-done.1.first, bf16[132,1536]{1,0:T(8,128)(2,1)S(1)} %collective-permute-done.3.second, bf16[1056,3072]{1,0:T(8,128)(2,1)S(1)} %get-tuple-element.7.block, f32[3,132,1056]{2,1,0:T(8,128)S(1)} %get-tuple-element.8.near), custom_call_target="tpu_custom_call" | custom-call | flops 856424448 | bytes 8000000 | tf_op jit(solution)/shard_map/pallas_call | solution.py:139
  (15 shorter events, 0.2 us)
Async XLA Ops:
  6.5 109.6 %all-gather.6.cloned.1.call-start = ((), (), s32[]{:S(2)}) async-start(), calls=%async_computation.1 | async-start | bytes 6963200 | tf_op jit(solution)/shard_map/all_gather | solution.py:157
  89.1 12.9 %collective-permute-start = (bf16[132,1536]{1,0:T(8,128)(2,1)S(1)}, bf16[132,1536]{1,0:T(8,128)(2,1)S(1)}, u32[]{:S(2)}, u32[]{:S(2)}) collective-permute-start(bf16[132,1536]{1,0:T(8,128)(2,1)S(1)} %get-tuple-element.12.refs_0_), channel_id=1, source_target_pairs={{0,128},{128,256},{256,384},{384,0},{1,129},{129,257},{257,385},{3... | collective-permute-start | bytes 1216520 | tf_op jit(solution)/shard_map/ppermute | solution.py:54
  91.5 15.7 %collective-permute-start.2 = (bf16[132,1536]{1,0:T(8,128)(2,1)S(1)}, bf16[132,1536]{1,0:T(8,128)(2,1)S(1)}, u32[]{:S(2)}, u32[]{:S(2)}) collective-permute-start(bf16[132,1536]{1,0:T(8,128)(2,1)S(1)} %get-tuple-element.11.refs_3_), channel_id=1, source_target_pairs={{0,384},{128,0},{256,128},{384,256},{1,385},{129,1},{257,129},{385... | collective-permute-start | bytes 1216520 | tf_op jit(solution)/shard_map/ppermute | solution.py:54
  95.0 21.2 %collective-permute-start.4 = (bf16[132,1536]{1,0:T(8,128)(2,1)S(1)}, bf16[132,1536]{1,0:T(8,128)(2,1)S(1)}, u32[]{:S(2)}, u32[]{:S(2)}) collective-permute-start(bf16[132,1536]{1,0:T(8,128)(2,1)S(1)} %get-tuple-element.12.refs_0_), channel_id=1, source_target_pairs={{0,384},{128,0},{256,128},{384,256},{1,385},{129,1},{257,129},{385... | collective-permute-start | bytes 1216520 | tf_op jit(solution)/shard_map/ppermute | solution.py:54
  97.7 18.4 %collective-permute-start.5 = (bf16[132,1536]{1,0:T(8,128)(2,1)S(1)}, bf16[132,1536]{1,0:T(8,128)(2,1)S(1)}, u32[]{:S(2)}, u32[]{:S(2)}) collective-permute-start(bf16[132,1536]{1,0:T(8,128)(2,1)S(1)} %get-tuple-element.11.refs_3_), channel_id=1, source_target_pairs={{0,128},{128,256},{256,384},{384,0},{1,129},{129,257},{257,385},{3... | collective-permute-start | bytes 1216520 | tf_op jit(solution)/shard_map/ppermute | solution.py:54
  102.0 22.6 %collective-permute-start.1 = (bf16[132,1536]{1,0:T(8,128)(2,1)S(1)}, bf16[132,1536]{1,0:T(8,128)(2,1)S(1)}, u32[]{:S(2)}, u32[]{:S(2)}) collective-permute-start(bf16[132,1536]{1,0:T(8,128)(2,1)S(1)} %collective-permute-done.refs_2_), channel_id=1, source_target_pairs={{0,128},{128,256},{256,384},{384,0},{1,129},{129,257},{257,385},{3... | collective-permute-start | bytes 1216520 | tf_op jit(solution)/shard_map/ppermute | solution.py:54
  107.2 17.5 %collective-permute-start.3 = (bf16[132,1536]{1,0:T(8,128)(2,1)S(1)}, bf16[132,1536]{1,0:T(8,128)(2,1)S(1)}, u32[]{:S(2)}, u32[]{:S(2)}) collective-permute-start(bf16[132,1536]{1,0:T(8,128)(2,1)S(1)} %collective-permute-done.2.refs_4_), channel_id=1, source_target_pairs={{0,384},{128,0},{256,128},{384,256},{1,385},{129,1},{257,129},{385... | collective-permute-start | bytes 1216520 | tf_op jit(solution)/shard_map/ppermute | solution.py:54
Sparse Core Ops, SparseCore 0:
  64.1 48.0 all-gather.5

commit v9 on v8

--- a/solution.py
+++ b/solution.py
@@ -19,15 +19,50 @@
 GROUP = 8 * SHARE
 EDGES = (0, 256, 512, 768, ROWS)
 
+VMEM = pl.BlockSpec(memory_space=pltpu.VMEM)
+
 epsilon = 1e-06
 
 
-def standardize(rows):
-    axes = tuple(range(1, rows.ndim))
+def standardize(rows, axes):
     average = jnp.sum(rows, axis=axes, keepdims=True) / TIME
     centered = rows - average
     variance = jnp.sum(centered * centered, axis=axes, keepdims=True) / TIME
     return (centered * lax.rsqrt(variance + epsilon)).astype(jnp.bfloat16)
+
+
+def standardize_kernel(pieces, window, wide, rows, single):
+    for source in range(32):
+        start = 96 * source
+        rows[:32, start : start + 96] = pieces[source, :, :96]
+        for p in range(3):
+            cut = slice(start + 32 * p, start + 32 * p + 32)
+            rows[32:, cut] = pieces[source, 8 * p : 8 * p + 8, 96:]
+            single[source : source + 1, 32 * p : 32 * p + 32] = pieces[
+                source, 24 + p : 25 + p, 96:
+            ]
+    scores = standardize(rows[...], (1,))
+    window[...] = scores
+    wide[:, :TIME] = scores[:32]
+    wide[:, TIME:] = jnp.zeros((32, 128), jnp.bfloat16)
+    wide[:, TIME : TIME + 96] = standardize(single[:, :96], (0, 1))
+
+
+def standardize_pieces(pieces):
+    return pl.pallas_call(
+        standardize_kernel,
+        out_shape=(
+            jax.ShapeDtypeStruct((WINDOW, TIME), jnp.bfloat16),
+            jax.ShapeDtypeStruct((32, WIDE), jnp.bfloat16),
+        ),
+        in_specs=[VMEM],
+        out_specs=(VMEM, VMEM),
+        scratch_shapes=[
+            pltpu.VMEM((WINDOW, TIME), jnp.float32),
+            pltpu.VMEM((32, 128), jnp.float32),
+        ],
+        compiler_params=pltpu.CompilerParams(vmem_limit_bytes=8 * 1024 * 1024),
+    )(pieces)
 
 
 def pack(series):
@@ -39,14 +74,6 @@
     side = [windows[:, 32:, cut] for cut in cuts] + [single[:, :, cut] for cut in cuts]
     side = jnp.concatenate(side + [jnp.zeros((32, 5, 32), series.dtype)], axis=1)
     return jnp.concatenate([windows[:, :32], side], axis=2)
-
-
-def unpack(pieces):
-    side = pieces[:, :, 96:]
-    last = jnp.concatenate([side[:, 8 * p : 8 * p + 8] for p in range(3)], axis=2)
-    window = jnp.concatenate([pieces[:, :, :96], last], axis=1)
-    single = jnp.concatenate([side[:, 24 + p] for p in range(3)], axis=1)
-    return window.transpose(1, 0, 2).reshape(WINDOW, TIME), single[None]
 
 
 def shift(array, axis, by):
@@ -108,9 +135,6 @@
             out[:, 4 * x : 4 * x + 4, low:high] = rows.reshape(SHARE, 4, width)
 
 
-VMEM = pl.BlockSpec(memory_space=pltpu.VMEM)
-
-
 def multiply_near(pieces, windows):
     return pl.pallas_call(
         near_kernel,
@@ -150,10 +174,8 @@
 
 
 def on_device(series):
-    window, single = unpack(lax.all_to_all(pack(series), BULK, 0, 0, tiled=True))
-    window, single = standardize(window), standardize(single)
+    window, wide = standardize_pieces(lax.all_to_all(pack(series), BULK, 0, 0, tiled=True))
     own = lax.dynamic_slice_in_dim(window, lax.rem(lax.axis_index(BULK), 8), SHARE, 0)
-    wide = jnp.concatenate([window[:32], jnp.pad(single[0], ((0, 0), (0, 32)))], axis=1)
     gathered = lax.all_gather(lax.all_gather(wide, "zh"), ("y", "core"))
 
     part = lax.all_gather(own, "zl").transpose(1, 0, 2).reshape(FOUR, TIME)

time: 137 us -> 131 us (0.956)
  other arithmetic: 3.62 us -> 0.21 us
  between operations: 16.3 us -> 13.7 us
    reduce_sum x6 -> x0, other arithmetic: 3.19 us -> none  [the longest x4 2.23 us: standardize(): average = jnp.sum(rows, axis=axes, keepdims=True) / TIME]
  transfers between devices with their start and end apart: 7 -> 7, of which waited for: 2 -> 2; matrix products, arithmetic and copies ran while one was open for 1% -> 1% of each run, Pallas kernels for 6% -> 7%
where the time goes in v9:
time: 131 us; the launch traced here: 130 us
  blocking collectives  72.7 us (55%)
  starting transfers between devices  17.5 us (13%)
  between operations  13.7 us (10%)
  Pallas kernels  13.3 us (10%)
  waiting for transfers between devices  9.45 us (7%)
  local copies, waits for them, and re-layouts  2.74 us (2%)
    all_to_all x1, blocking collectives, on_device(): lax.all_to_all(pack(series), BULK, 0, 0, tiled=True)  38.1 us
    all_gather x1, blocking collectives, on_device(): part = lax.all_gather(own, 'zl').transpose(1, 0, 2).reshape(FOUR, TIME)  24.2 us
    ppermute x6, starting transfers between devices, shift(): lax.ppermute(array, axis, [(i, (i + by) % size) for i in range(size)])  17.5 us
    all_gather x1, blocking collectives, on_device(): gathered = lax.all_gather(lax.all_gather(wide, 'zh'), ('y', 'core'))  10.5 us
    ppermute x6, waiting for transfers between devices, shift(): lax.ppermute(array, axis, [(i, (i + by) % size) for i in range(size)])  9.43 us
    pallas_call x1, Pallas kernels, multiply_near(): pl.pallas_call(near_kernel, out_shape=(jax.ShapeDtypeStruct((ROWS, TIME),...  8.48 us
    pallas_call x1, Pallas kernels, multiply_far(): pl.pallas_call(far_kernel, out_shape=jax.ShapeDtypeStruct((SHARE, 16, ROW...  4.26 us
  transfers between devices with their start and end apart: 7, of which 2 were waited for; matrix products, arithmetic and copies ran while one was open for 1% of the time, Pallas kernels for 7%

profile of v9, /device:TPU:6, one launch (start us, length us, event | category | flops | bytes accessed | tf_op | source)
XLA Modules:
  0.0 129.7 jit_solution(2095919738843700605)
XLA Ops:
  6.5 0.0 all-gather.6.cloned.1.call-start
  6.5 1.2 copy.14
  8.0 0.1 fusion.9
  8.1 0.1 slice.80
  8.2 0.1 fusion.10
  8.3 0.1 concatenate.6
  8.5 0.2 pad_maximum_fusion
  8.7 38.1 %all_to_all.5.pieces = f32[32,32,128]{2,1,0:T(8,128)S(1)} all-to-all(f32[32,32,128]{2,1,0:T(8,128)S(1)} %pad_maximum_fusion), channel_id=1, replica_groups=mesh['x'=4,'zl'=4,'zh'=2,'y'=8,'core'=2] {'zh','y','core'}, dimensions={0} | all-to-all | bytes 1048576 | tf_op jit(solution)/shard_map/all_to_all | solution.py:177
  46.8 0.6 shard_map.17
  47.4 10.5 %all-gather.1 = bf16[64,3200]{1,0:T(8,128)(2,1)} all-gather(bf16[32,3200]{1,0:T(8,128)(2,1)S(1)} %get-tuple-element.10), channel_id=3, replica_groups=mesh['x'=4,'zl'=4,'zh'=2,'y'=8,'core'=2] {'zh'}, dimensions={0}, use_global_device_ids=true | all-gather | bytes 614400 | tf_op jit(solution)/shard_map/all_gather | solution.py:179
  57.8 0.0 all-gather.6.cloned.1.call-update
  57.9 0.1 dynamic-slice_bitcast_fusion
  58.0 24.2 %all-gather.3 = bf16[4,33,3072]{2,1,0:T(8,128)(2,1)S(1)} all-gather(bf16[1,33,3072]{2,1,0:T(8,128)(2,1)S(1)} %dynamic-slice_bitcast_fusion), channel_id=2, replica_groups=mesh['x'=4,'zl'=4,'zh'=2,'y'=8,'core'=2] {'zl'}, dimensions={0}, use_global_device_ids=true | all-gather | bytes 1013760 | tf_op jit(solution)/shard_map/all_gather | solution.py:181
  82.1 0.6 copy.16
  82.8 0.2 reshape.19
  83.0 0.1 fusion.8
  83.0 2.4 %collective-permute-start = (bf16[132,1536]{1,0:T(8,128)(2,1)S(1)}, bf16[132,1536]{1,0:T(8,128)(2,1)S(1)}, u32[]{:S(2)}, u32[]{:S(2)}) collective-permute-start(bf16[132,1536]{1,0:T(8,128)(2,1)S(1)} %get-tuple-element.14.refs_0_), channel_id=1, source_target_pairs={{0,128},{128,256},{256,384},{384,0},{1,129},{129,257},{257,385},{3... | collective-permute-start | bytes 1216520 | tf_op jit(solution)/shard_map/ppermute | solution.py:81
  85.4 3.5 %collective-permute-start.2 = (bf16[132,1536]{1,0:T(8,128)(2,1)S(1)}, bf16[132,1536]{1,0:T(8,128)(2,1)S(1)}, u32[]{:S(2)}, u32[]{:S(2)}) collective-permute-start(bf16[132,1536]{1,0:T(8,128)(2,1)S(1)} %get-tuple-element.13.refs_3_), channel_id=1, source_target_pairs={{0,384},{128,0},{256,128},{384,256},{1,385},{129,1},{257,129},{385... | collective-permute-start | bytes 1216520 | tf_op jit(solution)/shard_map/ppermute | solution.py:81
  88.9 2.7 %collective-permute-start.4 = (bf16[132,1536]{1,0:T(8,128)(2,1)S(1)}, bf16[132,1536]{1,0:T(8,128)(2,1)S(1)}, u32[]{:S(2)}, u32[]{:S(2)}) collective-permute-start(bf16[132,1536]{1,0:T(8,128)(2,1)S(1)} %get-tuple-element.14.refs_0_), channel_id=1, source_target_pairs={{0,384},{128,0},{256,128},{384,256},{1,385},{129,1},{257,129},{385... | collective-permute-start | bytes 1216520 | tf_op jit(solution)/shard_map/ppermute | solution.py:81
  91.6 4.3 %collective-permute-start.5 = (bf16[132,1536]{1,0:T(8,128)(2,1)S(1)}, bf16[132,1536]{1,0:T(8,128)(2,1)S(1)}, u32[]{:S(2)}, u32[]{:S(2)}) collective-permute-start(bf16[132,1536]{1,0:T(8,128)(2,1)S(1)} %get-tuple-element.13.refs_3_), channel_id=1, source_target_pairs={{0,128},{128,256},{256,384},{384,0},{1,129},{129,257},{257,385},{3... | collective-permute-start | bytes 1216520 | tf_op jit(solution)/shard_map/ppermute | solution.py:81
  96.0 0.0 collective-permute-done.refs_2_
  96.0 2.4 %collective-permute-start.1 = (bf16[132,1536]{1,0:T(8,128)(2,1)S(1)}, bf16[132,1536]{1,0:T(8,128)(2,1)S(1)}, u32[]{:S(2)}, u32[]{:S(2)}) collective-permute-start(bf16[132,1536]{1,0:T(8,128)(2,1)S(1)} %collective-permute-done.refs_2_), channel_id=1, source_target_pairs={{0,128},{128,256},{256,384},{384,0},{1,129},{129,257},{257,385},{3... | collective-permute-start | bytes 1216520 | tf_op jit(solution)/shard_map/ppermute | solution.py:81
  98.4 2.7 %collective-permute-done.2.refs_4_ = bf16[132,1536]{1,0:T(8,128)(2,1)S(1)} collective-permute-done((bf16[132,1536]{1,0:T(8,128)(2,1)S(1)}, bf16[132,1536]{1,0:T(8,128)(2,1)S(1)}, u32[]{:S(2)}, u32[]{:S(2)}) %collective-permute-start.2) | collective-permute-done | bytes 405536 | tf_op jit(solution)/shard_map/ppermute | solution.py:81
  101.1 2.2 %collective-permute-start.3 = (bf16[132,1536]{1,0:T(8,128)(2,1)S(1)}, bf16[132,1536]{1,0:T(8,128)(2,1)S(1)}, u32[]{:S(2)}, u32[]{:S(2)}) collective-permute-start(bf16[132,1536]{1,0:T(8,128)(2,1)S(1)} %collective-permute-done.2.refs_4_), channel_id=1, source_target_pairs={{0,384},{128,0},{256,128},{384,256},{1,385},{129,1},{257,129},{385... | collective-permute-start | bytes 1216520 | tf_op jit(solution)/shard_map/ppermute | solution.py:81
  103.4 6.7 %collective-permute-done.4.refs_1_ = bf16[132,1536]{1,0:T(8,128)(2,1)S(1)} collective-permute-done((bf16[132,1536]{1,0:T(8,128)(2,1)S(1)}, bf16[132,1536]{1,0:T(8,128)(2,1)S(1)}, u32[]{:S(2)}, u32[]{:S(2)}) %collective-permute-start.4) | collective-permute-done | bytes 405536 | tf_op jit(solution)/shard_map/ppermute | solution.py:81
  110.1 0.0 collective-permute-done.5.refs_5_
  110.1 0.0 all-gather.6.cloned.1.call-done
  110.1 8.5 %shard_map.18 = (bf16[1056,3072]{1,0:T(8,128)(2,1)S(1)}, f32[3,132,1056]{2,1,0:T(8,128)S(1)}) custom-call(bf16[132,1536]{1,0:T(8,128)(2,1)S(1)} %get-tuple-element.14.refs_0_, bf16[132,1536]{1,0:T(8,128)(2,1)S(1)} %collective-permute-done.4.refs_1_, bf16[132,1536]{1,0:T(8,128)(2,1)S(1)} %collective-permute-done.refs_2_, ...), custom_call_target="tpu_custom_call" | custom-call | flops 2569273344 | bytes 14000000 | tf_op jit(solution)/shard_map/pallas_call | solution.py:139
  118.5 0.0 collective-permute-done.1.first
  118.6 0.0 collective-permute-done.3.second
  118.6 4.3 %shard_map.19 = f32[33,16,1056]{2,1,0:T(8,128)} custom-call(s32[1]{0:T(128)} %bitcast.place, bf16[132,1536]{1,0:T(8,128)(2,1)S(1)} %collective-permute-done.1.first, bf16[132,1536]{1,0:T(8,128)(2,1)S(1)} %collective-permute-done.3.second, bf16[1056,3072]{1,0:T(8,128)(2,1)S(1)} %get-tuple-element.11.block, f32[3,132,1056]{2,1,0:T(8,128)S(1)} %get-tuple-element.12.near), custom_call_target="tpu_custom_call" | custom-call | flops 856424448 | bytes 8000000 | tf_op jit(solution)/shard_map/pallas_call | solution.py:163
  (11 shorter events, 0.1 us)
Async XLA Ops:
  6.5 103.5 %all-gather.6.cloned.1.call-start = ((), (), s32[]{:S(2)}) async-start(), calls=%async_computation.1 | async-start | bytes 6963200 | tf_op jit(solution)/shard_map/all_gather | solution.py:179
  83.0 12.9 %collective-permute-start = (bf16[132,1536]{1,0:T(8,128)(2,1)S(1)}, bf16[132,1536]{1,0:T(8,128)(2,1)S(1)}, u32[]{:S(2)}, u32[]{:S(2)}) collective-permute-start(bf16[132,1536]{1,0:T(8,128)(2,1)S(1)} %get-tuple-element.14.refs_0_), channel_id=1, source_target_pairs={{0,128},{128,256},{256,384},{384,0},{1,129},{129,257},{257,385},{3... | collective-permute-start | bytes 1216520 | tf_op jit(solution)/shard_map/ppermute | solution.py:81
  85.4 15.7 %collective-permute-start.2 = (bf16[132,1536]{1,0:T(8,128)(2,1)S(1)}, bf16[132,1536]{1,0:T(8,128)(2,1)S(1)}, u32[]{:S(2)}, u32[]{:S(2)}) collective-permute-start(bf16[132,1536]{1,0:T(8,128)(2,1)S(1)} %get-tuple-element.13.refs_3_), channel_id=1, source_target_pairs={{0,384},{128,0},{256,128},{384,256},{1,385},{129,1},{257,129},{385... | collective-permute-start | bytes 1216520 | tf_op jit(solution)/shard_map/ppermute | solution.py:81
  88.9 21.2 %collective-permute-start.4 = (bf16[132,1536]{1,0:T(8,128)(2,1)S(1)}, bf16[132,1536]{1,0:T(8,128)(2,1)S(1)}, u32[]{:S(2)}, u32[]{:S(2)}) collective-permute-start(bf16[132,1536]{1,0:T(8,128)(2,1)S(1)} %get-tuple-element.14.refs_0_), channel_id=1, source_target_pairs={{0,384},{128,0},{256,128},{384,256},{1,385},{129,1},{257,129},{385... | collective-permute-start | bytes 1216520 | tf_op jit(solution)/shard_map/ppermute | solution.py:81
  91.6 18.4 %collective-permute-start.5 = (bf16[132,1536]{1,0:T(8,128)(2,1)S(1)}, bf16[132,1536]{1,0:T(8,128)(2,1)S(1)}, u32[]{:S(2)}, u32[]{:S(2)}) collective-permute-start(bf16[132,1536]{1,0:T(8,128)(2,1)S(1)} %get-tuple-element.13.refs_3_), channel_id=1, source_target_pairs={{0,128},{128,256},{256,384},{384,0},{1,129},{129,257},{257,385},{3... | collective-permute-start | bytes 1216520 | tf_op jit(solution)/shard_map/ppermute | solution.py:81
  96.0 22.6 %collective-permute-start.1 = (bf16[132,1536]{1,0:T(8,128)(2,1)S(1)}, bf16[132,1536]{1,0:T(8,128)(2,1)S(1)}, u32[]{:S(2)}, u32[]{:S(2)}) collective-permute-start(bf16[132,1536]{1,0:T(8,128)(2,1)S(1)} %collective-permute-done.refs_2_), channel_id=1, source_target_pairs={{0,128},{128,256},{256,384},{384,0},{1,129},{129,257},{257,385},{3... | collective-permute-start | bytes 1216520 | tf_op jit(solution)/shard_map/ppermute | solution.py:81
  101.1 17.5 %collective-permute-start.3 = (bf16[132,1536]{1,0:T(8,128)(2,1)S(1)}, bf16[132,1536]{1,0:T(8,128)(2,1)S(1)}, u32[]{:S(2)}, u32[]{:S(2)}) collective-permute-start(bf16[132,1536]{1,0:T(8,128)(2,1)S(1)} %collective-permute-done.2.refs_4_), channel_id=1, source_target_pairs={{0,384},{128,0},{256,128},{384,256},{1,385},{129,1},{257,129},{385... | collective-permute-start | bytes 1216520 | tf_op jit(solution)/shard_map/ppermute | solution.py:81
Sparse Core Ops, SparseCore 0:
  58.0 48.0 all-gather.5

commit v10 on v9

--- a/solution.py
+++ b/solution.py
@@ -65,15 +65,28 @@
     )(pieces)
 
 
+def pack_kernel(steps, packed, rows):
+    rows[...] = steps[...].T
+    for device in range(32):
+        group, i = divmod(device, 8)
+        start, single = GROUP * group + 32 * i, GROUP * group + 256 + i
+        packed[device, :, :96] = rows[start : start + 32, :]
+        for p in range(3):
+            cut = slice(32 * p, 32 * p + 32)
+            packed[device, 8 * p : 8 * p + 8, 96:] = rows[start + 32 : start + 40, cut]
+            packed[device, 24 + p : 25 + p, 96:] = rows[single : single + 1, cut]
+        packed[device, 27:, 96:] = jnp.zeros((5, 32), jnp.float32)
+
+
 def pack(series):
-    groups = series.reshape(4, GROUP, 96)
-    windows = jnp.stack([groups[:, 32 * i : 32 * i + WINDOW] for i in range(8)], axis=1)
-    windows = windows.reshape(32, WINDOW, 96)
-    single = groups[:, 256:].reshape(32, 1, 96)
-    cuts = [slice(32 * p, 32 * p + 32) for p in range(3)]
-    side = [windows[:, 32:, cut] for cut in cuts] + [single[:, :, cut] for cut in cuts]
-    side = jnp.concatenate(side + [jnp.zeros((32, 5, 32), series.dtype)], axis=1)
-    return jnp.concatenate([windows[:, :32], side], axis=2)
+    return pl.pallas_call(
+        pack_kernel,
+        out_shape=jax.ShapeDtypeStruct((32, 32, 128), jnp.float32),
+        in_specs=[VMEM],
+        out_specs=VMEM,
+        scratch_shapes=[pltpu.VMEM((ROWS, 96), jnp.float32)],
+        compiler_params=pltpu.CompilerParams(vmem_limit_bytes=8 * 1024 * 1024),
+    )(series.T)
 
 
 def shift(array, axis, by):
@@ -106,8 +119,9 @@
     for t in range(2):
         for k in range(3):
             parts[t, SLOT * k : SLOT * k + FOUR, :] = pieces[3 * t + k][...]
+    for copy in copies:
+        copy.wait()
     for group in range(4):
-        copies[group].wait()
         for i in range(8):
             start = GROUP * group + 32 * i
             block[start : start + 32, :] = held[group, i, :, :TIME]
@@ -117,14 +131,15 @@
             tail[:, 96 * source : 96 * source + 96] = steps[:, :96]
         start = GROUP * group + 256
         block[start : start + 8, :] = tail[...].astype(jnp.bfloat16)
-        low, high = EDGES[group], EDGES[group + 1]
+    for low, high in zip(EDGES[:-1], EDGES[1:]):
         product = contract(parts.at[0], parts.at[1], block, low, high)
         for k in range(3):
             near[k, :, low:high] = product[SLOT * k : SLOT * k + FOUR, :]
 
 
-def far_kernel(place, first, second, block, near, out, turned):
-    for low, high in zip(EDGES[:-1], EDGES[1:]):
+def far_kernel(place, first, second, block, near, out, turned, ready, sent):
+    copies = []
+    for tile, (low, high) in enumerate(zip(EDGES[:-1], EDGES[1:])):
         width = high - low
         product = contract(first, second, block, low, high)
         turned[2, :, :width] = product
@@ -132,7 +147,13 @@
             turned[k, :, :width] = near[n, :, low:high]
         for x in range(4):
             rows = turned[lax.rem(x - place[0] + 4, 4), :, :width]
-            out[:, 4 * x : 4 * x + 4, low:high] = rows.reshape(SHARE, 4, width)
+            ready[:, 4 * x : 4 * x + 4, low:high] = rows.reshape(SHARE, 4, width)
+        done = slice(low, high)
+        copy = pltpu.make_async_copy(ready.at[:, :, done], out.at[:, :, done], sent.at[tile])
+        copy.start()
+        copies.append(copy)
+    for copy in copies:
+        copy.wait()
 
 
 def multiply_near(pieces, windows):
@@ -164,8 +185,12 @@
         far_kernel,
         out_shape=jax.ShapeDtypeStruct((SHARE, 16, ROWS), jnp.float32),
         in_specs=[pl.BlockSpec(memory_space=pltpu.SMEM), VMEM, VMEM, VMEM, VMEM],
-        out_specs=VMEM,
-        scratch_shapes=[pltpu.VMEM((4, FOUR, 384), jnp.float32)],
+        out_specs=pl.BlockSpec(memory_space=pl.ANY),
+        scratch_shapes=[
+            pltpu.VMEM((4, FOUR, 384), jnp.float32),
+            pltpu.VMEM((SHARE, 16, ROWS), jnp.float32),
+            pltpu.SemaphoreType.DMA((4,)),
+        ],
         compiler_params=pltpu.CompilerParams(vmem_limit_bytes=24 * 1024 * 1024),
         cost_estimate=pl.CostEstimate(
             flops=2 * FOUR * ROWS * TIME, bytes_accessed=8_000_000, transcendentals=0
@@ -178,7 +203,8 @@
     own = lax.dynamic_slice_in_dim(window, lax.rem(lax.axis_index(BULK), 8), SHARE, 0)
     gathered = lax.all_gather(lax.all_gather(wide, "zh"), ("y", "core"))
 
-    part = lax.all_gather(own, "zl").transpose(1, 0, 2).reshape(FOUR, TIME)
+    part = lax.all_gather(own.reshape(SHARE, TIME // 128, 128), "zl")
+    part = part.transpose(1, 0, 2, 3).reshape(FOUR, TIME)
     first, second = part[:, :HALF], part[:, HALF:]
     after_first, before_second = shift(first, "x", 1), shift(second, "x", -1)
     after_second, before_first = shift(second, "x", 1), shift(first, "x", -1)

time: 131 us -> 125 us (0.954)
  blocking collectives: 72.7 us -> 70.6 us
  Pallas kernels: 13.3 us -> 11.8 us
    all_gather x1, blocking collectives: 24.2 us -> 22.1 us  [on_device(): part = lax.all_gather(own.reshape(SHARE, TIME // 128, 128), 'zl')]
    pallas_call x1, Pallas kernels: 8.48 us -> 6.81 us  [multiply_near(): pl.pallas_call(near_kernel, out_shape=(jax.ShapeDtypeStruct((ROWS, TIME),...]
  transfers between devices with their start and end apart: 7 -> 7, of which waited for: 2 -> 2; matrix products, arithmetic and copies ran while one was open for 1% -> 0% of each run, Pallas kernels for 7% -> 5%
where the time goes in v10:
time: 125 us; the launch traced here: 124 us
  blocking collectives  70.6 us (56%)
  starting transfers between devices  17.5 us (14%)
  between operations  13.6 us (11%)
  Pallas kernels  11.8 us (9%)
  waiting for transfers between devices  9.48 us (8%)
  local copies, waits for them, and re-layouts  1.49 us (1%)
    all_to_all x1, blocking collectives, on_device(): lax.all_to_all(pack(series), BULK, 0, 0, tiled=True)  38.1 us
    all_gather x1, blocking collectives, on_device(): part = lax.all_gather(own.reshape(SHARE, TIME // 128, 128), 'zl')  22.1 us
    ppermute x6, starting transfers between devices, shift(): lax.ppermute(array, axis, [(i, (i + by) % size) for i in range(size)])  17.5 us
    all_gather x1, blocking collectives, on_device(): gathered = lax.all_gather(lax.all_gather(wide, 'zh'), ('y', 'core'))  10.5 us
    ppermute x6, waiting for transfers between devices, shift(): lax.ppermute(array, axis, [(i, (i + by) % size) for i in range(size)])  9.46 us
    pallas_call x1, Pallas kernels, multiply_near(): pl.pallas_call(near_kernel, out_shape=(jax.ShapeDtypeStruct((ROWS, TIME),...  6.81 us
    pallas_call x1, Pallas kernels, multiply_far(): pl.pallas_call(far_kernel, out_shape=jax.ShapeDtypeStruct((SHARE, 16, ROW...  3.89 us
  transfers between devices with their start and end apart: 7, of which 2 were waited for; matrix products, arithmetic and copies ran while one was open for 0% of the time, Pallas kernels for 5%

profile of v10, /device:TPU:6, one launch (start us, length us, event | category | flops | bytes accessed | tf_op | source)
XLA Modules:
  0.0 124.5 jit_solution(14088733370246529179)
XLA Ops:
  6.5 0.0 all-gather.4.cloned.1.call-start
  6.5 0.0 copy-start
  6.5 1.0 copy-done
  7.6 0.5 shard_map.17
  8.1 38.1 %all_to_all.5.pieces = f32[32,32,128]{2,1,0:T(8,128)S(1)} all-to-all(f32[32,32,128]{2,1,0:T(8,128)S(1)} %shard_map.17), channel_id=1, replica_groups=mesh['x'=4,'zl'=4,'zh'=2,'y'=8,'core'=2] {'zh','y','core'}, dimensions={0} | all-to-all | bytes 1048576 | tf_op jit(solution)/shard_map/all_to_all | solution.py:202
  46.1 0.6 shard_map.18
  46.8 10.5 %all-gather = bf16[64,3200]{1,0:T(8,128)(2,1)} all-gather(bf16[32,3200]{1,0:T(8,128)(2,1)S(1)} %get-tuple-element.10), channel_id=2, replica_groups=mesh['x'=4,'zl'=4,'zh'=2,'y'=8,'core'=2] {'zh'}, dimensions={0}, use_global_device_ids=true | all-gather | bytes 614400 | tf_op jit(solution)/shard_map/all_gather | solution.py:204
  57.2 0.0 all-gather.4.cloned.1.call-update
  57.3 0.1 constant_dynamic-slice_fusion
  57.4 22.1 %all_gather.15 = bf16[4,33,24,128]{3,2,0,1:T(8,128)(2,1)S(1)} all-gather(bf16[1,33,24,128]{3,2,0,1:T(8,128)(2,1)S(1)} %slice_bitcast_fusion), channel_id=1, replica_groups=mesh['x'=4,'zl'=4,'zh'=2,'y'=8,'core'=2] {'zl'}, dimensions={0}, use_global_device_ids=true | all-gather | bytes 1013760 | tf_op jit(solution)/shard_map/all_gather | solution.py:206
  79.5 0.1 pad
  79.6 0.2 copy.3
  79.8 0.1 fusion
  79.9 2.4 %collective-permute-start = (bf16[132,1536]{1,0:T(8,128)(2,1)S(1)}, bf16[132,1536]{1,0:T(8,128)(2,1)S(1)}, u32[]{:S(2)}, u32[]{:S(2)}) collective-permute-start(bf16[132,1536]{1,0:T(8,128)(2,1)S(1)} %get-tuple-element.14.refs_0_), channel_id=1, source_target_pairs={{0,128},{128,256},{256,384},{384,0},{1,129},{129,257},{257,385},{3... | collective-permute-start | bytes 1216520 | tf_op jit(solution)/shard_map/ppermute | solution.py:94
  82.3 3.5 %collective-permute-start.2 = (bf16[132,1536]{1,0:T(8,128)(2,1)S(1)}, bf16[132,1536]{1,0:T(8,128)(2,1)S(1)}, u32[]{:S(2)}, u32[]{:S(2)}) collective-permute-start(bf16[132,1536]{1,0:T(8,128)(2,1)S(1)} %get-tuple-element.13.refs_3_), channel_id=1, source_target_pairs={{0,384},{128,0},{256,128},{384,256},{1,385},{129,1},{257,129},{385... | collective-permute-start | bytes 1216520 | tf_op jit(solution)/shard_map/ppermute | solution.py:94
  85.7 2.7 %collective-permute-start.4 = (bf16[132,1536]{1,0:T(8,128)(2,1)S(1)}, bf16[132,1536]{1,0:T(8,128)(2,1)S(1)}, u32[]{:S(2)}, u32[]{:S(2)}) collective-permute-start(bf16[132,1536]{1,0:T(8,128)(2,1)S(1)} %get-tuple-element.14.refs_0_), channel_id=1, source_target_pairs={{0,384},{128,0},{256,128},{384,256},{1,385},{129,1},{257,129},{385... | collective-permute-start | bytes 1216520 | tf_op jit(solution)/shard_map/ppermute | solution.py:94
  88.5 4.3 %collective-permute-start.5 = (bf16[132,1536]{1,0:T(8,128)(2,1)S(1)}, bf16[132,1536]{1,0:T(8,128)(2,1)S(1)}, u32[]{:S(2)}, u32[]{:S(2)}) collective-permute-start(bf16[132,1536]{1,0:T(8,128)(2,1)S(1)} %get-tuple-element.13.refs_3_), channel_id=1, source_target_pairs={{0,128},{128,256},{256,384},{384,0},{1,129},{129,257},{257,385},{3... | collective-permute-start | bytes 1216520 | tf_op jit(solution)/shard_map/ppermute | solution.py:94
  92.8 0.0 collective-permute-done.refs_2_
  92.8 2.4 %collective-permute-start.1 = (bf16[132,1536]{1,0:T(8,128)(2,1)S(1)}, bf16[132,1536]{1,0:T(8,128)(2,1)S(1)}, u32[]{:S(2)}, u32[]{:S(2)}) collective-permute-start(bf16[132,1536]{1,0:T(8,128)(2,1)S(1)} %collective-permute-done.refs_2_), channel_id=1, source_target_pairs={{0,128},{128,256},{256,384},{384,0},{1,129},{129,257},{257,385},{3... | collective-permute-start | bytes 1216520 | tf_op jit(solution)/shard_map/ppermute | solution.py:94
  95.2 2.7 %collective-permute-done.2.refs_4_ = bf16[132,1536]{1,0:T(8,128)(2,1)S(1)} collective-permute-done((bf16[132,1536]{1,0:T(8,128)(2,1)S(1)}, bf16[132,1536]{1,0:T(8,128)(2,1)S(1)}, u32[]{:S(2)}, u32[]{:S(2)}) %collective-permute-start.2) | collective-permute-done | bytes 405536 | tf_op jit(solution)/shard_map/ppermute | solution.py:94
  97.9 2.2 %collective-permute-start.3 = (bf16[132,1536]{1,0:T(8,128)(2,1)S(1)}, bf16[132,1536]{1,0:T(8,128)(2,1)S(1)}, u32[]{:S(2)}, u32[]{:S(2)}) collective-permute-start(bf16[132,1536]{1,0:T(8,128)(2,1)S(1)} %collective-permute-done.2.refs_4_), channel_id=1, source_target_pairs={{0,384},{128,0},{256,128},{384,256},{1,385},{129,1},{257,129},{385... | collective-permute-start | bytes 1216520 | tf_op jit(solution)/shard_map/ppermute | solution.py:94
  100.2 6.7 %collective-permute-done.4.refs_1_ = bf16[132,1536]{1,0:T(8,128)(2,1)S(1)} collective-permute-done((bf16[132,1536]{1,0:T(8,128)(2,1)S(1)}, bf16[132,1536]{1,0:T(8,128)(2,1)S(1)}, u32[]{:S(2)}, u32[]{:S(2)}) %collective-permute-start.4) | collective-permute-done | bytes 405536 | tf_op jit(solution)/shard_map/ppermute | solution.py:94
  106.9 0.0 collective-permute-done.5.refs_5_
  106.9 0.0 all-gather.4.cloned.1.call-done
  106.9 6.8 %shard_map.19 = (bf16[1056,3072]{1,0:T(8,128)(2,1)S(1)}, f32[3,132,1056]{2,1,0:T(8,128)S(1)}) custom-call(bf16[132,1536]{1,0:T(8,128)(2,1)S(1)} %get-tuple-element.14.refs_0_, bf16[132,1536]{1,0:T(8,128)(2,1)S(1)} %collective-permute-done.4.refs_1_, bf16[132,1536]{1,0:T(8,128)(2,1)S(1)} %collective-permute-done.refs_2_, ...), custom_call_target="tpu_custom_call" | custom-call | flops 2569273344 | bytes 14000000 | tf_op jit(solution)/shard_map/pallas_call | solution.py:160
  113.7 0.0 collective-permute-done.1.first
  113.7 0.0 collective-permute-done.3.second
  113.7 3.9 %shard_map.20 = f32[33,16,1056]{2,1,0:T(8,128)} custom-call(s32[1]{0:T(128)} %bitcast.place, bf16[132,1536]{1,0:T(8,128)(2,1)S(1)} %collective-permute-done.1.first, bf16[132,1536]{1,0:T(8,128)(2,1)S(1)} %collective-permute-done.3.second, bf16[1056,3072]{1,0:T(8,128)(2,1)S(1)} %get-tuple-element.11.block, f32[3,132,1056]{2,1,0:T(8,128)S(1)} %get-tuple-element.12.near), custom_call_target="tpu_custom_call" | custom-call | flops 856424448 | bytes 8000000 | tf_op jit(solution)/shard_map/pallas_call | solution.py:184
  (2 shorter events, 0.1 us)
Async XLA Ops:
  6.5 100.4 %all-gather.4.cloned.1.call-start = ((), (), s32[]{:S(2)}) async-start(), calls=%async_computation.1 | async-start | bytes 6963200 | tf_op jit(solution)/shard_map/all_gather | solution.py:204
  6.5 1.0 copy-start
  79.9 12.9 %collective-permute-start = (bf16[132,1536]{1,0:T(8,128)(2,1)S(1)}, bf16[132,1536]{1,0:T(8,128)(2,1)S(1)}, u32[]{:S(2)}, u32[]{:S(2)}) collective-permute-start(bf16[132,1536]{1,0:T(8,128)(2,1)S(1)} %get-tuple-element.14.refs_0_), channel_id=1, source_target_pairs={{0,128},{128,256},{256,384},{384,0},{1,129},{129,257},{257,385},{3... | collective-permute-start | bytes 1216520 | tf_op jit(solution)/shard_map/ppermute | solution.py:94
  82.3 15.7 %collective-permute-start.2 = (bf16[132,1536]{1,0:T(8,128)(2,1)S(1)}, bf16[132,1536]{1,0:T(8,128)(2,1)S(1)}, u32[]{:S(2)}, u32[]{:S(2)}) collective-permute-start(bf16[132,1536]{1,0:T(8,128)(2,1)S(1)} %get-tuple-element.13.refs_3_), channel_id=1, source_target_pairs={{0,384},{128,0},{256,128},{384,256},{1,385},{129,1},{257,129},{385... | collective-permute-start | bytes 1216520 | tf_op jit(solution)/shard_map/ppermute | solution.py:94
  85.7 21.2 %collective-permute-start.4 = (bf16[132,1536]{1,0:T(8,128)(2,1)S(1)}, bf16[132,1536]{1,0:T(8,128)(2,1)S(1)}, u32[]{:S(2)}, u32[]{:S(2)}) collective-permute-start(bf16[132,1536]{1,0:T(8,128)(2,1)S(1)} %get-tuple-element.14.refs_0_), channel_id=1, source_target_pairs={{0,384},{128,0},{256,128},{384,256},{1,385},{129,1},{257,129},{385... | collective-permute-start | bytes 1216520 | tf_op jit(solution)/shard_map/ppermute | solution.py:94
  88.5 18.4 %collective-permute-start.5 = (bf16[132,1536]{1,0:T(8,128)(2,1)S(1)}, bf16[132,1536]{1,0:T(8,128)(2,1)S(1)}, u32[]{:S(2)}, u32[]{:S(2)}) collective-permute-start(bf16[132,1536]{1,0:T(8,128)(2,1)S(1)} %get-tuple-element.13.refs_3_), channel_id=1, source_target_pairs={{0,128},{128,256},{256,384},{384,0},{1,129},{129,257},{257,385},{3... | collective-permute-start | bytes 1216520 | tf_op jit(solution)/shard_map/ppermute | solution.py:94
  92.8 20.9 %collective-permute-start.1 = (bf16[132,1536]{1,0:T(8,128)(2,1)S(1)}, bf16[132,1536]{1,0:T(8,128)(2,1)S(1)}, u32[]{:S(2)}, u32[]{:S(2)}) collective-permute-start(bf16[132,1536]{1,0:T(8,128)(2,1)S(1)} %collective-permute-done.refs_2_), channel_id=1, source_target_pairs={{0,128},{128,256},{256,384},{384,0},{1,129},{129,257},{257,385},{3... | collective-permute-start | bytes 1216520 | tf_op jit(solution)/shard_map/ppermute | solution.py:94
  97.9 15.8 %collective-permute-start.3 = (bf16[132,1536]{1,0:T(8,128)(2,1)S(1)}, bf16[132,1536]{1,0:T(8,128)(2,1)S(1)}, u32[]{:S(2)}, u32[]{:S(2)}) collective-permute-start(bf16[132,1536]{1,0:T(8,128)(2,1)S(1)} %collective-permute-done.2.refs_4_), channel_id=1, source_target_pairs={{0,384},{128,0},{256,128},{384,256},{1,385},{129,1},{257,129},{385... | collective-permute-start | bytes 1216520 | tf_op jit(solution)/shard_map/ppermute | solution.py:94
Sparse Core Ops, SparseCore 0:
  57.4 48.0 all-gather.3

commit v11 on v10

--- a/solution.py
+++ b/solution.py
@@ -106,8 +106,7 @@
     return product * (1.0 / TIME)
 
 
-def near_kernel(*refs):
-    pieces, (windows, block, near, held, parts, singles, tail, arrived) = refs[:6], refs[6:]
+def order_kernel(windows, block, held, singles, tail, arrived):
     copies = []
     for group in range(4):
         half, parity = divmod(group, 2)
@@ -116,12 +115,8 @@
         )
         copy.start()
         copies.append(copy)
-    for t in range(2):
-        for k in range(3):
-            parts[t, SLOT * k : SLOT * k + FOUR, :] = pieces[3 * t + k][...]
-    for copy in copies:
-        copy.wait()
     for group in range(4):
+        copies[group].wait()
         for i in range(8):
             start = GROUP * group + 32 * i
             block[start : start + 32, :] = held[group, i, :, :TIME]
@@ -131,20 +126,36 @@
             tail[:, 96 * source : 96 * source + 96] = steps[:, :96]
         start = GROUP * group + 256
         block[start : start + 8, :] = tail[...].astype(jnp.bfloat16)
-    for low, high in zip(EDGES[:-1], EDGES[1:]):
-        product = contract(parts.at[0], parts.at[1], block, low, high)
-        for k in range(3):
-            near[k, :, low:high] = product[SLOT * k : SLOT * k + FOUR, :]
-
-
-def far_kernel(place, first, second, block, near, out, turned, ready, sent):
+
+
+def order(windows):
+    return pl.pallas_call(
+        order_kernel,
+        out_shape=jax.ShapeDtypeStruct((ROWS, TIME), jnp.bfloat16),
+        in_specs=[pl.BlockSpec(memory_space=pl.ANY)],
+        out_specs=VMEM,
+        scratch_shapes=[
+            pltpu.VMEM((4, 8, 32, WIDE), jnp.bfloat16),
+            pltpu.VMEM((256, 128), jnp.float32),
+            pltpu.VMEM((8, TIME), jnp.float32),
+            pltpu.SemaphoreType.DMA((4,)),
+        ],
+        compiler_params=pltpu.CompilerParams(vmem_limit_bytes=44 * 1024 * 1024),
+        cost_estimate=pl.CostEstimate(flops=0, bytes_accessed=7_000_000, transcendentals=0),
+    )(windows)
+
+
+def product_kernel(place, *refs):
+    pieces, (block, out, parts, turned, ready, sent) = refs[:8], refs[8:]
+    for t in range(2):
+        for k in range(4):
+            parts[t, SLOT * k : SLOT * k + FOUR, :] = pieces[4 * t + k][...]
     copies = []
     for tile, (low, high) in enumerate(zip(EDGES[:-1], EDGES[1:])):
         width = high - low
-        product = contract(first, second, block, low, high)
-        turned[2, :, :width] = product
-        for n, k in enumerate((0, 1, 3)):
-            turned[k, :, :width] = near[n, :, low:high]
+        product = contract(parts.at[0], parts.at[1], block, low, high)
+        for k in range(4):
+            turned[k, :, :width] = product[SLOT * k : SLOT * k + FOUR, :]
         for x in range(4):
             rows = turned[lax.rem(x - place[0] + 4, 4), :, :width]
             ready[:, 4 * x : 4 * x + 4, low:high] = rows.reshape(SHARE, 4, width)
@@ -156,46 +167,24 @@
         copy.wait()
 
 
-def multiply_near(pieces, windows):
-    return pl.pallas_call(
-        near_kernel,
-        out_shape=(
-            jax.ShapeDtypeStruct((ROWS, TIME), jnp.bfloat16),
-            jax.ShapeDtypeStruct((3, FOUR, ROWS), jnp.float32),
-        ),
-        in_specs=[VMEM] * 6 + [pl.BlockSpec(memory_space=pl.ANY)],
-        out_specs=(VMEM, VMEM),
-        scratch_shapes=[
-            pltpu.VMEM((4, 8, 32, WIDE), jnp.bfloat16),
-            pltpu.VMEM((2, 3 * SLOT, HALF), jnp.bfloat16),
-            pltpu.VMEM((256, 128), jnp.float32),
-            pltpu.VMEM((8, TIME), jnp.float32),
-            pltpu.SemaphoreType.DMA((4,)),
-        ],
-        compiler_params=pltpu.CompilerParams(vmem_limit_bytes=40 * 1024 * 1024),
-        cost_estimate=pl.CostEstimate(
-            flops=6 * FOUR * ROWS * TIME, bytes_accessed=14_000_000, transcendentals=0
-        ),
-    )(*pieces, windows)
-
-
-def multiply_far(first, second, block, near):
+def multiply(pieces, block):
     place = lax.axis_index("x").astype(jnp.int32).reshape(1)
     return pl.pallas_call(
-        far_kernel,
+        product_kernel,
         out_shape=jax.ShapeDtypeStruct((SHARE, 16, ROWS), jnp.float32),
-        in_specs=[pl.BlockSpec(memory_space=pltpu.SMEM), VMEM, VMEM, VMEM, VMEM],
+        in_specs=[pl.BlockSpec(memory_space=pltpu.SMEM)] + [VMEM] * 9,
         out_specs=pl.BlockSpec(memory_space=pl.ANY),
         scratch_shapes=[
+            pltpu.VMEM((2, 4 * SLOT, HALF), jnp.bfloat16),
             pltpu.VMEM((4, FOUR, 384), jnp.float32),
             pltpu.VMEM((SHARE, 16, ROWS), jnp.float32),
             pltpu.SemaphoreType.DMA((4,)),
         ],
-        compiler_params=pltpu.CompilerParams(vmem_limit_bytes=24 * 1024 * 1024),
+        compiler_params=pltpu.CompilerParams(vmem_limit_bytes=28 * 1024 * 1024),
         cost_estimate=pl.CostEstimate(
-            flops=2 * FOUR * ROWS * TIME, bytes_accessed=8_000_000, transcendentals=0
+            flops=8 * FOUR * ROWS * TIME, bytes_accessed=2_400_000, transcendentals=0
         ),
-    )(place, first, second, block, near)
+    )(place, *pieces, block)
 
 
 def on_device(series):
@@ -210,9 +199,9 @@
     after_second, before_first = shift(second, "x", 1), shift(first, "x", -1)
     far_first, far_second = shift(after_first, "x", 1), shift(before_second, "x", -1)
 
-    pieces = (first, before_first, after_first, second, before_second, after_second)
-    block, near = multiply_near(pieces, gathered)
-    return multiply_far(far_first, far_second, block, near).transpose(1, 0, 2)
+    pieces = (first, before_first, far_first, after_first)
+    pieces += (second, before_second, far_second, after_second)
+    return multiply(pieces, order(gathered)).transpose(1, 0, 2)
 
 
 def solution(mesh):

time: 125 us -> 129 us (1.032)
  the two profiles are of different devices: /device:TPU:6 before, /device:TPU:8 now
where the time goes in v11:
time: 129 us
  blocking collectives  70.9 us (55%)
  starting transfers between devices  20.2 us (16%)
  between operations  13.6 us (11%)
  waiting for transfers between devices  12.1 us (9%)
  Pallas kernels  10.6 us (8%)
  local copies, waits for them, and re-layouts  1.49 us (1%)
    all_to_all x1, blocking collectives, on_device(): lax.all_to_all(pack(series), BULK, 0, 0, tiled=True)  37.8 us
    all_gather x1, blocking collectives, on_device(): part = lax.all_gather(own.reshape(SHARE, TIME // 128, 128), 'zl')  22.3 us
    ppermute x6, starting transfers between devices, shift(): lax.ppermute(array, axis, [(i, (i + by) % size) for i in range(size)])  20.2 us
    all_gather x1, blocking collectives, on_device(): gathered = lax.all_gather(lax.all_gather(wide, 'zh'), ('y', 'core'))  10.8 us
    ppermute x6, waiting for transfers between devices, shift(): lax.ppermute(array, axis, [(i, (i + by) % size) for i in range(size)])  9.39 us
    pallas_call x1, Pallas kernels, multiply(): pl.pallas_call(product_kernel, out_shape=jax.ShapeDtypeStruct((SHARE, 16,...  6.34 us
    pallas_call x1, Pallas kernels, order(): pl.pallas_call(order_kernel, out_shape=jax.ShapeDtypeStruct((ROWS, TIME),...  3.2 us
    all_gather x1, waiting for transfers between devices, on_device(): gathered = lax.all_gather(lax.all_gather(wide, 'zh'), ('y', 'core'))  2.67 us
  transfers between devices with their start and end apart: 7, of which 5 were waited for; matrix products, arithmetic and copies ran while one was open for 0% of the time, Pallas kernels for 2%

profile of v11, /device:TPU:8, one launch (start us, length us, event | category | flops | bytes accessed | tf_op | source)
XLA Modules:
  0.0 128.9 jit_solution(2664450684220339817)
XLA Ops:
  6.5 0.0 all-gather.4.cloned.1.call-start
  6.5 0.0 copy-start
  6.5 1.0 copy-done
  7.6 0.5 shard_map.17
  8.1 37.8 %all_to_all.5.pieces = f32[32,32,128]{2,1,0:T(8,128)S(1)} all-to-all(f32[32,32,128]{2,1,0:T(8,128)S(1)} %shard_map.17), channel_id=1, replica_groups=mesh['x'=4,'zl'=4,'zh'=2,'y'=8,'core'=2] {'zh','y','core'}, dimensions={0} | all-to-all | bytes 1048576 | tf_op jit(solution)/shard_map/all_to_all | solution.py:191
  45.8 0.6 shard_map.18
  46.5 10.8 %all-gather = bf16[64,3200]{1,0:T(8,128)(2,1)} all-gather(bf16[32,3200]{1,0:T(8,128)(2,1)S(1)} %get-tuple-element.8), channel_id=2, replica_groups=mesh['x'=4,'zl'=4,'zh'=2,'y'=8,'core'=2] {'zh'}, dimensions={0}, use_global_device_ids=true | all-gather | bytes 614400 | tf_op jit(solution)/shard_map/all_gather | solution.py:193
  57.3 0.0 all-gather.4.cloned.1.call-update
  57.3 0.1 constant_dynamic-slice_fusion
  57.5 22.3 %all_gather.15 = bf16[4,33,24,128]{3,2,0,1:T(8,128)(2,1)S(1)} all-gather(bf16[1,33,24,128]{3,2,0,1:T(8,128)(2,1)S(1)} %slice_bitcast_fusion), channel_id=1, replica_groups=mesh['x'=4,'zl'=4,'zh'=2,'y'=8,'core'=2] {'zl'}, dimensions={0}, use_global_device_ids=true | all-gather | bytes 1013760 | tf_op jit(solution)/shard_map/all_gather | solution.py:195
  79.7 0.1 pad
  79.9 0.2 copy.3
  80.1 0.1 fusion
  80.1 4.7 %collective-permute-start.3 = (bf16[132,1536]{1,0:T(8,128)(2,1)S(1)}, bf16[132,1536]{1,0:T(8,128)(2,1)S(1)}, u32[]{:S(2)}, u32[]{:S(2)}) collective-permute-start(bf16[132,1536]{1,0:T(8,128)(2,1)S(1)} %get-tuple-element.9.refs_4_), channel_id=1, source_target_pairs={{0,384},{128,0},{256,128},{384,256},{1,385},{129,1},{257,129},{385... | collective-permute-start | bytes 1216520 | tf_op jit(solution)/shard_map/ppermute | solution.py:94
  84.8 1.9 %collective-permute-start.1 = (bf16[132,1536]{1,0:T(8,128)(2,1)S(1)}, bf16[132,1536]{1,0:T(8,128)(2,1)S(1)}, u32[]{:S(2)}, u32[]{:S(2)}) collective-permute-start(bf16[132,1536]{1,0:T(8,128)(2,1)S(1)} %get-tuple-element.10.refs_0_), channel_id=1, source_target_pairs={{0,128},{128,256},{256,384},{384,0},{1,129},{129,257},{257,385},{3... | collective-permute-start | bytes 1216520 | tf_op jit(solution)/shard_map/ppermute | solution.py:94
  86.7 2.7 %collective-permute-start.5 = (bf16[132,1536]{1,0:T(8,128)(2,1)S(1)}, bf16[132,1536]{1,0:T(8,128)(2,1)S(1)}, u32[]{:S(2)}, u32[]{:S(2)}) collective-permute-start(bf16[132,1536]{1,0:T(8,128)(2,1)S(1)} %get-tuple-element.9.refs_4_), channel_id=1, source_target_pairs={{0,128},{128,256},{256,384},{384,0},{1,129},{129,257},{257,385},{3... | collective-permute-start | bytes 1216520 | tf_op jit(solution)/shard_map/ppermute | solution.py:94
  89.4 4.4 %collective-permute-start = (bf16[132,1536]{1,0:T(8,128)(2,1)S(1)}, bf16[132,1536]{1,0:T(8,128)(2,1)S(1)}, u32[]{:S(2)}, u32[]{:S(2)}) collective-permute-start(bf16[132,1536]{1,0:T(8,128)(2,1)S(1)} %get-tuple-element.10.refs_0_), channel_id=1, source_target_pairs={{0,384},{128,0},{256,128},{384,256},{1,385},{129,1},{257,129},{385... | collective-permute-start | bytes 1216520 | tf_op jit(solution)/shard_map/ppermute | solution.py:94
  93.8 0.0 collective-permute-done.3.refs_5_
  93.8 4.7 %collective-permute-start.4 = (bf16[132,1536]{1,0:T(8,128)(2,1)S(1)}, bf16[132,1536]{1,0:T(8,128)(2,1)S(1)}, u32[]{:S(2)}, u32[]{:S(2)}) collective-permute-start(bf16[132,1536]{1,0:T(8,128)(2,1)S(1)} %collective-permute-done.3.refs_5_), channel_id=1, source_target_pairs={{0,384},{128,0},{256,128},{384,256},{1,385},{129,1},{257,129},{385... | collective-permute-start | bytes 1216520 | tf_op jit(solution)/shard_map/ppermute | solution.py:94
  98.5 2.0 %collective-permute-done.1.refs_3_ = bf16[132,1536]{1,0:T(8,128)(2,1)S(1)} collective-permute-done((bf16[132,1536]{1,0:T(8,128)(2,1)S(1)}, bf16[132,1536]{1,0:T(8,128)(2,1)S(1)}, u32[]{:S(2)}, u32[]{:S(2)}) %collective-permute-start.1) | collective-permute-done | bytes 405536 | tf_op jit(solution)/shard_map/ppermute | solution.py:94
  100.5 1.9 %collective-permute-start.2 = (bf16[132,1536]{1,0:T(8,128)(2,1)S(1)}, bf16[132,1536]{1,0:T(8,128)(2,1)S(1)}, u32[]{:S(2)}, u32[]{:S(2)}) collective-permute-start(bf16[132,1536]{1,0:T(8,128)(2,1)S(1)} %collective-permute-done.1.refs_3_), channel_id=1, source_target_pairs={{0,128},{128,256},{256,384},{384,0},{1,129},{129,257},{257,385},{3... | collective-permute-start | bytes 1216520 | tf_op jit(solution)/shard_map/ppermute | solution.py:94
  102.4 2.7 %all-gather.4.cloned.1.call-done = bf16[32,32,3200]{2,1,0:T(8,128)(2,1)} async-done(((bf16[2,32,3200]{2,1,0:T(8,128)(2,1)}), bf16[32,32,3200]{2,1,0:T(8,128)(2,1)}) %all-gather.4.cloned.1.call-update) | async-done | bytes 6553616 | tf_op jit(solution)/shard_map/all_gather | solution.py:193
  105.1 3.2 %shard_map.19.refs_8_ = bf16[1056,3072]{1,0:T(8,128)(2,1)S(1)} custom-call(bf16[16,2,32,3200]{3,2,1,0:T(8,128)(2,1)} %bitcast.17), custom_call_target="tpu_custom_call" | custom-call | bytes 7000000 | tf_op jit(solution)/shard_map/pallas_call | solution.py:132
  108.3 1.2 collective-permute-done.5.refs_7_
  109.4 0.0 collective-permute-done.refs_1_
  109.4 0.9 collective-permute-done.4.refs_6_
  110.4 5.3 %collective-permute-done.2.refs_2_ = bf16[132,1536]{1,0:T(8,128)(2,1)S(1)} collective-permute-done((bf16[132,1536]{1,0:T(8,128)(2,1)S(1)}, bf16[132,1536]{1,0:T(8,128)(2,1)S(1)}, u32[]{:S(2)}, u32[]{:S(2)}) %collective-permute-start.2) | collective-permute-done | bytes 405536 | tf_op jit(solution)/shard_map/ppermute | solution.py:94
  115.7 6.3 %shard_map.20 = f32[33,16,1056]{2,1,0:T(8,128)} custom-call(s32[1]{0:T(128)} %bitcast.place, bf16[132,1536]{1,0:T(8,128)(2,1)S(1)} %get-tuple-element.10.refs_0_, bf16[132,1536]{1,0:T(8,128)(2,1)S(1)} %collective-permute-done.refs_1_, bf16[132,1536]{1,0:T(8,128)(2,1)S(1)} %collective-permute-done.2.refs_2_, ...), custom_call_target="tpu_custom_call" | custom-call | flops 3425697792 | bytes 2400000 | tf_op jit(solution)/shard_map/pallas_call | solution.py:172
  (2 shorter events, 0.1 us)
Async XLA Ops:
  6.5 98.5 %all-gather.4.cloned.1.call-start = ((), (), s32[]{:S(2)}) async-start(), calls=%async_computation.1 | async-start | bytes 6963200 | tf_op jit(solution)/shard_map/all_gather | solution.py:193
  6.5 1.0 copy-start
  80.1 13.7 %collective-permute-start.3 = (bf16[132,1536]{1,0:T(8,128)(2,1)S(1)}, bf16[132,1536]{1,0:T(8,128)(2,1)S(1)}, u32[]{:S(2)}, u32[]{:S(2)}) collective-permute-start(bf16[132,1536]{1,0:T(8,128)(2,1)S(1)} %get-tuple-element.9.refs_4_), channel_id=1, source_target_pairs={{0,384},{128,0},{256,128},{384,256},{1,385},{129,1},{257,129},{385... | collective-permute-start | bytes 1216520 | tf_op jit(solution)/shard_map/ppermute | solution.py:94
  84.8 15.7 %collective-permute-start.1 = (bf16[132,1536]{1,0:T(8,128)(2,1)S(1)}, bf16[132,1536]{1,0:T(8,128)(2,1)S(1)}, u32[]{:S(2)}, u32[]{:S(2)}) collective-permute-start(bf16[132,1536]{1,0:T(8,128)(2,1)S(1)} %get-tuple-element.10.refs_0_), channel_id=1, source_target_pairs={{0,128},{128,256},{256,384},{384,0},{1,129},{129,257},{257,385},{3... | collective-permute-start | bytes 1216520 | tf_op jit(solution)/shard_map/ppermute | solution.py:94
  86.7 22.7 %collective-permute-start.5 = (bf16[132,1536]{1,0:T(8,128)(2,1)S(1)}, bf16[132,1536]{1,0:T(8,128)(2,1)S(1)}, u32[]{:S(2)}, u32[]{:S(2)}) collective-permute-start(bf16[132,1536]{1,0:T(8,128)(2,1)S(1)} %get-tuple-element.9.refs_4_), channel_id=1, source_target_pairs={{0,128},{128,256},{256,384},{384,0},{1,129},{129,257},{257,385},{3... | collective-permute-start | bytes 1216520 | tf_op jit(solution)/shard_map/ppermute | solution.py:94
  89.4 20.0 %collective-permute-start = (bf16[132,1536]{1,0:T(8,128)(2,1)S(1)}, bf16[132,1536]{1,0:T(8,128)(2,1)S(1)}, u32[]{:S(2)}, u32[]{:S(2)}) collective-permute-start(bf16[132,1536]{1,0:T(8,128)(2,1)S(1)} %get-tuple-element.10.refs_0_), channel_id=1, source_target_pairs={{0,384},{128,0},{256,128},{384,256},{1,385},{129,1},{257,129},{385... | collective-permute-start | bytes 1216520 | tf_op jit(solution)/shard_map/ppermute | solution.py:94
  93.8 16.6 %collective-permute-start.4 = (bf16[132,1536]{1,0:T(8,128)(2,1)S(1)}, bf16[132,1536]{1,0:T(8,128)(2,1)S(1)}, u32[]{:S(2)}, u32[]{:S(2)}) collective-permute-start(bf16[132,1536]{1,0:T(8,128)(2,1)S(1)} %collective-permute-done.3.refs_5_), channel_id=1, source_target_pairs={{0,384},{128,0},{256,128},{384,256},{1,385},{129,1},{257,129},{385... | collective-permute-start | bytes 1216520 | tf_op jit(solution)/shard_map/ppermute | solution.py:94
  100.5 15.2 %collective-permute-start.2 = (bf16[132,1536]{1,0:T(8,128)(2,1)S(1)}, bf16[132,1536]{1,0:T(8,128)(2,1)S(1)}, u32[]{:S(2)}, u32[]{:S(2)}) collective-permute-start(bf16[132,1536]{1,0:T(8,128)(2,1)S(1)} %collective-permute-done.1.refs_3_), channel_id=1, source_target_pairs={{0,128},{128,256},{256,384},{384,0},{1,129},{129,257},{257,385},{3... | collective-permute-start | bytes 1216520 | tf_op jit(solution)/shard_map/ppermute | solution.py:94
Sparse Core Ops, SparseCore 0:
  57.4 47.5 all-gather.3

commit v12 on v10

--- a/solution.py
+++ b/solution.py
@@ -107,34 +107,65 @@
 
 
 def near_kernel(*refs):
-    pieces, (windows, block, near, held, parts, singles, tail, arrived) = refs[:6], refs[6:]
-    copies = []
+    pieces, refs = refs[:6], refs[6:]
+    windows, block, near, held, raw, parts, singles, tail, direct, arrived = refs
+    copies = {}
     for group in range(4):
         half, parity = divmod(group, 2)
-        copy = pltpu.make_async_copy(
-            windows.at[pl.ds(8 * parity, 8), half], held.at[group], arrived.at[group]
+        devices, steps = pl.ds(8 * parity, 8), pl.ds(0, TIME)
+        if parity:
+            copies[group] = [
+                pltpu.make_async_copy(
+                    windows.at[devices, half, :, steps], held.at[half], arrived.at[group]
+                )
+            ]
+        else:
+            copies[group] = [
+                pltpu.make_async_copy(
+                    windows.at[i, half, :, steps],
+                    block.at[pl.ds(GROUP * group + 32 * i, 32), :],
+                    direct.at[half, i],
+                )
+                for i in range(8)
+            ]
+        copies[group].append(
+            pltpu.make_async_copy(
+                windows.at[devices, half, :, pl.ds(TIME, 128)],
+                raw.at[group],
+                arrived.at[4 + group],
+            )
         )
-        copy.start()
-        copies.append(copy)
+        for copy in copies[group]:
+            copy.start()
     for t in range(2):
         for k in range(3):
             parts[t, SLOT * k : SLOT * k + FOUR, :] = pieces[3 * t + k][...]
-    for copy in copies:
+
+    def multiply_rows(low, high):
+        product = contract(parts.at[0], parts.at[1], block, low, high)
+        for k in range(3):
+            near[k, :, low:high] = product[SLOT * k : SLOT * k + FOUR, :]
+
+    for copy in copies[0]:
         copy.wait()
+    multiply_rows(EDGES[0], EDGES[1])
+    for group in range(1, 4):
+        for copy in copies[group]:
+            copy.wait()
     for group in range(4):
+        half, parity = divmod(group, 2)
         for i in range(8):
             start = GROUP * group + 32 * i
-            block[start : start + 32, :] = held[group, i, :, :TIME]
-            singles[32 * i : 32 * i + 32, :] = held[group, i, :, TIME:].astype(jnp.float32)
+            if parity:
+                block[start : start + 32, :] = held[half, i]
+            singles[32 * i : 32 * i + 32, :] = raw[group, i].astype(jnp.float32)
         for source in range(32):
             steps = singles[pl.ds(source, 8, stride=32), :]
             tail[:, 96 * source : 96 * source + 96] = steps[:, :96]
         start = GROUP * group + 256
         block[start : start + 8, :] = tail[...].astype(jnp.bfloat16)
-    for low, high in zip(EDGES[:-1], EDGES[1:]):
-        product = contract(parts.at[0], parts.at[1], block, low, high)
-        for k in range(3):
-            near[k, :, low:high] = product[SLOT * k : SLOT * k + FOUR, :]
+    for low, high in zip(EDGES[1:-1], EDGES[2:]):
+        multiply_rows(low, high)
 
 
 def far_kernel(place, first, second, block, near, out, turned, ready, sent):
@@ -166,11 +197,13 @@
         in_specs=[VMEM] * 6 + [pl.BlockSpec(memory_space=pl.ANY)],
         out_specs=(VMEM, VMEM),
         scratch_shapes=[
-            pltpu.VMEM((4, 8, 32, WIDE), jnp.bfloat16),
+            pltpu.VMEM((2, 8, 32, TIME), jnp.bfloat16),
+            pltpu.VMEM((4, 8, 32, 128), jnp.bfloat16),
             pltpu.VMEM((2, 3 * SLOT, HALF), jnp.bfloat16),
             pltpu.VMEM((256, 128), jnp.float32),
             pltpu.VMEM((8, TIME), jnp.float32),
-            pltpu.SemaphoreType.DMA((4,)),
+            pltpu.SemaphoreType.DMA((2, 8)),
+            pltpu.SemaphoreType.DMA((8,)),
         ],
         compiler_params=pltpu.CompilerParams(vmem_limit_bytes=40 * 1024 * 1024),
         cost_estimate=pl.CostEstimate(

time: 125 us -> 125 us (level)
  transfers between devices with their start and end apart: 7 -> 7, of which waited for: 2 -> 2; matrix products, arithmetic and copies ran while one was open for 0% -> 0% of each run, Pallas kernels for 5% -> 6%
where the time goes in v12:
time: 125 us
  blocking collectives  70.6 us (56%)
  starting transfers between devices  17.5 us (14%)
  between operations  13.6 us (11%)
  Pallas kernels  12.1 us (10%)
  waiting for transfers between devices  9.48 us (8%)
  local copies, waits for them, and re-layouts  1.49 us (1%)
    all_to_all x1, blocking collectives, on_device(): lax.all_to_all(pack(series), BULK, 0, 0, tiled=True)  38.1 us
    all_gather x1, blocking collectives, on_device(): part = lax.all_gather(own.reshape(SHARE, TIME // 128, 128), 'zl')  22.1 us
    ppermute x6, starting transfers between devices, shift(): lax.ppermute(array, axis, [(i, (i + by) % size) for i in range(size)])  17.5 us
    all_gather x1, blocking collectives, on_device(): gathered = lax.all_gather(lax.all_gather(wide, 'zh'), ('y', 'core'))  10.5 us
    ppermute x6, waiting for transfers between devices, shift(): lax.ppermute(array, axis, [(i, (i + by) % size) for i in range(size)])  9.46 us
    pallas_call x1, Pallas kernels, multiply_near(): pl.pallas_call(near_kernel, out_shape=(jax.ShapeDtypeStruct((ROWS, TIME),...  7.09 us
    pallas_call x1, Pallas kernels, multiply_far(): pl.pallas_call(far_kernel, out_shape=jax.ShapeDtypeStruct((SHARE, 16, ROW...  3.89 us
  transfers between devices with their start and end apart: 7, of which 2 were waited for; matrix products, arithmetic and copies ran while one was open for 0% of the time, Pallas kernels for 6%

profile of v12, /device:TPU:6, one launch (start us, length us, event | category | flops | bytes accessed | tf_op | source)
XLA Modules:
  0.0 124.8 jit_solution(14192671453074761913)
XLA Ops:
  6.5 0.0 all-gather.4.cloned.1.call-start
  6.5 0.0 copy-start
  6.5 1.0 copy-done
  7.6 0.5 shard_map.17
  8.1 38.1 %all_to_all.5.pieces = f32[32,32,128]{2,1,0:T(8,128)S(1)} all-to-all(f32[32,32,128]{2,1,0:T(8,128)S(1)} %shard_map.17), channel_id=1, replica_groups=mesh['x'=4,'zl'=4,'zh'=2,'y'=8,'core'=2] {'zh','y','core'}, dimensions={0} | all-to-all | bytes 1048576 | tf_op jit(solution)/shard_map/all_to_all | solution.py:235
  46.1 0.6 shard_map.18
  46.8 10.5 %all-gather = bf16[64,3200]{1,0:T(8,128)(2,1)} all-gather(bf16[32,3200]{1,0:T(8,128)(2,1)S(1)} %get-tuple-element.10), channel_id=2, replica_groups=mesh['x'=4,'zl'=4,'zh'=2,'y'=8,'core'=2] {'zh'}, dimensions={0}, use_global_device_ids=true | all-gather | bytes 614400 | tf_op jit(solution)/shard_map/all_gather | solution.py:237
  57.2 0.0 all-gather.4.cloned.1.call-update
  57.3 0.1 constant_dynamic-slice_fusion
  57.4 22.1 %all_gather.15 = bf16[4,33,24,128]{3,2,0,1:T(8,128)(2,1)S(1)} all-gather(bf16[1,33,24,128]{3,2,0,1:T(8,128)(2,1)S(1)} %slice_bitcast_fusion), channel_id=1, replica_groups=mesh['x'=4,'zl'=4,'zh'=2,'y'=8,'core'=2] {'zl'}, dimensions={0}, use_global_device_ids=true | all-gather | bytes 1013760 | tf_op jit(solution)/shard_map/all_gather | solution.py:239
  79.5 0.1 pad
  79.6 0.2 copy.3
  79.8 0.1 fusion
  79.9 2.4 %collective-permute-start = (bf16[132,1536]{1,0:T(8,128)(2,1)S(1)}, bf16[132,1536]{1,0:T(8,128)(2,1)S(1)}, u32[]{:S(2)}, u32[]{:S(2)}) collective-permute-start(bf16[132,1536]{1,0:T(8,128)(2,1)S(1)} %get-tuple-element.14.refs_0_), channel_id=1, source_target_pairs={{0,128},{128,256},{256,384},{384,0},{1,129},{129,257},{257,385},{3... | collective-permute-start | bytes 1216520 | tf_op jit(solution)/shard_map/ppermute | solution.py:94
  82.3 3.5 %collective-permute-start.2 = (bf16[132,1536]{1,0:T(8,128)(2,1)S(1)}, bf16[132,1536]{1,0:T(8,128)(2,1)S(1)}, u32[]{:S(2)}, u32[]{:S(2)}) collective-permute-start(bf16[132,1536]{1,0:T(8,128)(2,1)S(1)} %get-tuple-element.13.refs_3_), channel_id=1, source_target_pairs={{0,384},{128,0},{256,128},{384,256},{1,385},{129,1},{257,129},{385... | collective-permute-start | bytes 1216520 | tf_op jit(solution)/shard_map/ppermute | solution.py:94
  85.7 2.7 %collective-permute-start.4 = (bf16[132,1536]{1,0:T(8,128)(2,1)S(1)}, bf16[132,1536]{1,0:T(8,128)(2,1)S(1)}, u32[]{:S(2)}, u32[]{:S(2)}) collective-permute-start(bf16[132,1536]{1,0:T(8,128)(2,1)S(1)} %get-tuple-element.14.refs_0_), channel_id=1, source_target_pairs={{0,384},{128,0},{256,128},{384,256},{1,385},{129,1},{257,129},{385... | collective-permute-start | bytes 1216520 | tf_op jit(solution)/shard_map/ppermute | solution.py:94
  88.5 4.3 %collective-permute-start.5 = (bf16[132,1536]{1,0:T(8,128)(2,1)S(1)}, bf16[132,1536]{1,0:T(8,128)(2,1)S(1)}, u32[]{:S(2)}, u32[]{:S(2)}) collective-permute-start(bf16[132,1536]{1,0:T(8,128)(2,1)S(1)} %get-tuple-element.13.refs_3_), channel_id=1, source_target_pairs={{0,128},{128,256},{256,384},{384,0},{1,129},{129,257},{257,385},{3... | collective-permute-start | bytes 1216520 | tf_op jit(solution)/shard_map/ppermute | solution.py:94
  92.8 0.0 collective-permute-done.refs_2_
  92.8 2.4 %collective-permute-start.1 = (bf16[132,1536]{1,0:T(8,128)(2,1)S(1)}, bf16[132,1536]{1,0:T(8,128)(2,1)S(1)}, u32[]{:S(2)}, u32[]{:S(2)}) collective-permute-start(bf16[132,1536]{1,0:T(8,128)(2,1)S(1)} %collective-permute-done.refs_2_), channel_id=1, source_target_pairs={{0,128},{128,256},{256,384},{384,0},{1,129},{129,257},{257,385},{3... | collective-permute-start | bytes 1216520 | tf_op jit(solution)/shard_map/ppermute | solution.py:94
  95.2 2.7 %collective-permute-done.2.refs_4_ = bf16[132,1536]{1,0:T(8,128)(2,1)S(1)} collective-permute-done((bf16[132,1536]{1,0:T(8,128)(2,1)S(1)}, bf16[132,1536]{1,0:T(8,128)(2,1)S(1)}, u32[]{:S(2)}, u32[]{:S(2)}) %collective-permute-start.2) | collective-permute-done | bytes 405536 | tf_op jit(solution)/shard_map/ppermute | solution.py:94
  97.9 2.2 %collective-permute-start.3 = (bf16[132,1536]{1,0:T(8,128)(2,1)S(1)}, bf16[132,1536]{1,0:T(8,128)(2,1)S(1)}, u32[]{:S(2)}, u32[]{:S(2)}) collective-permute-start(bf16[132,1536]{1,0:T(8,128)(2,1)S(1)} %collective-permute-done.2.refs_4_), channel_id=1, source_target_pairs={{0,384},{128,0},{256,128},{384,256},{1,385},{129,1},{257,129},{385... | collective-permute-start | bytes 1216520 | tf_op jit(solution)/shard_map/ppermute | solution.py:94
  100.2 6.7 %collective-permute-done.4.refs_1_ = bf16[132,1536]{1,0:T(8,128)(2,1)S(1)} collective-permute-done((bf16[132,1536]{1,0:T(8,128)(2,1)S(1)}, bf16[132,1536]{1,0:T(8,128)(2,1)S(1)}, u32[]{:S(2)}, u32[]{:S(2)}) %collective-permute-start.4) | collective-permute-done | bytes 405536 | tf_op jit(solution)/shard_map/ppermute | solution.py:94
  106.9 0.0 collective-permute-done.5.refs_5_
  106.9 0.0 all-gather.4.cloned.1.call-done
  106.9 7.1 %shard_map.19 = (bf16[1056,3072]{1,0:T(8,128)(2,1)S(1)}, f32[3,132,1056]{2,1,0:T(8,128)S(1)}) custom-call(bf16[132,1536]{1,0:T(8,128)(2,1)S(1)} %get-tuple-element.14.refs_0_, bf16[132,1536]{1,0:T(8,128)(2,1)S(1)} %collective-permute-done.4.refs_1_, bf16[132,1536]{1,0:T(8,128)(2,1)S(1)} %collective-permute-done.refs_2_, ...), custom_call_target="tpu_custom_call" | custom-call | flops 2569273344 | bytes 14000000 | tf_op jit(solution)/shard_map/pallas_call | solution.py:191
  114.0 0.0 collective-permute-done.1.first
  114.0 0.0 collective-permute-done.3.second
  114.0 3.9 %shard_map.20 = f32[33,16,1056]{2,1,0:T(8,128)} custom-call(s32[1]{0:T(128)} %bitcast.place, bf16[132,1536]{1,0:T(8,128)(2,1)S(1)} %collective-permute-done.1.first, bf16[132,1536]{1,0:T(8,128)(2,1)S(1)} %collective-permute-done.3.second, bf16[1056,3072]{1,0:T(8,128)(2,1)S(1)} %get-tuple-element.11.block, f32[3,132,1056]{2,1,0:T(8,128)S(1)} %get-tuple-element.12.near), custom_call_target="tpu_custom_call" | custom-call | flops 856424448 | bytes 8000000 | tf_op jit(solution)/shard_map/pallas_call | solution.py:217
  (2 shorter events, 0.1 us)
Async XLA Ops:
  6.5 100.4 %all-gather.4.cloned.1.call-start = ((), (), s32[]{:S(2)}) async-start(), calls=%async_computation.1 | async-start | bytes 6963200 | tf_op jit(solution)/shard_map/all_gather | solution.py:237
  6.5 1.0 copy-start
  79.9 12.9 %collective-permute-start = (bf16[132,1536]{1,0:T(8,128)(2,1)S(1)}, bf16[132,1536]{1,0:T(8,128)(2,1)S(1)}, u32[]{:S(2)}, u32[]{:S(2)}) collective-permute-start(bf16[132,1536]{1,0:T(8,128)(2,1)S(1)} %get-tuple-element.14.refs_0_), channel_id=1, source_target_pairs={{0,128},{128,256},{256,384},{384,0},{1,129},{129,257},{257,385},{3... | collective-permute-start | bytes 1216520 | tf_op jit(solution)/shard_map/ppermute | solution.py:94
  82.3 15.7 %collective-permute-start.2 = (bf16[132,1536]{1,0:T(8,128)(2,1)S(1)}, bf16[132,1536]{1,0:T(8,128)(2,1)S(1)}, u32[]{:S(2)}, u32[]{:S(2)}) collective-permute-start(bf16[132,1536]{1,0:T(8,128)(2,1)S(1)} %get-tuple-element.13.refs_3_), channel_id=1, source_target_pairs={{0,384},{128,0},{256,128},{384,256},{1,385},{129,1},{257,129},{385... | collective-permute-start | bytes 1216520 | tf_op jit(solution)/shard_map/ppermute | solution.py:94
  85.7 21.2 %collective-permute-start.4 = (bf16[132,1536]{1,0:T(8,128)(2,1)S(1)}, bf16[132,1536]{1,0:T(8,128)(2,1)S(1)}, u32[]{:S(2)}, u32[]{:S(2)}) collective-permute-start(bf16[132,1536]{1,0:T(8,128)(2,1)S(1)} %get-tuple-element.14.refs_0_), channel_id=1, source_target_pairs={{0,384},{128,0},{256,128},{384,256},{1,385},{129,1},{257,129},{385... | collective-permute-start | bytes 1216520 | tf_op jit(solution)/shard_map/ppermute | solution.py:94
  88.5 18.4 %collective-permute-start.5 = (bf16[132,1536]{1,0:T(8,128)(2,1)S(1)}, bf16[132,1536]{1,0:T(8,128)(2,1)S(1)}, u32[]{:S(2)}, u32[]{:S(2)}) collective-permute-start(bf16[132,1536]{1,0:T(8,128)(2,1)S(1)} %get-tuple-element.13.refs_3_), channel_id=1, source_target_pairs={{0,128},{128,256},{256,384},{384,0},{1,129},{129,257},{257,385},{3... | collective-permute-start | bytes 1216520 | tf_op jit(solution)/shard_map/ppermute | solution.py:94
  92.8 21.2 %collective-permute-start.1 = (bf16[132,1536]{1,0:T(8,128)(2,1)S(1)}, bf16[132,1536]{1,0:T(8,128)(2,1)S(1)}, u32[]{:S(2)}, u32[]{:S(2)}) collective-permute-start(bf16[132,1536]{1,0:T(8,128)(2,1)S(1)} %collective-permute-done.refs_2_), channel_id=1, source_target_pairs={{0,128},{128,256},{256,384},{384,0},{1,129},{129,257},{257,385},{3... | collective-permute-start | bytes 1216520 | tf_op jit(solution)/shard_map/ppermute | solution.py:94
  97.9 16.1 %collective-permute-start.3 = (bf16[132,1536]{1,0:T(8,128)(2,1)S(1)}, bf16[132,1536]{1,0:T(8,128)(2,1)S(1)}, u32[]{:S(2)}, u32[]{:S(2)}) collective-permute-start(bf16[132,1536]{1,0:T(8,128)(2,1)S(1)} %collective-permute-done.2.refs_4_), channel_id=1, source_target_pairs={{0,384},{128,0},{256,128},{384,256},{1,385},{129,1},{257,129},{385... | collective-permute-start | bytes 1216520 | tf_op jit(solution)/shard_map/ppermute | solution.py:94
Sparse Core Ops, SparseCore 0:
  57.4 48.0 all-gather.3

commit v13 on v11

--- a/solution.py
+++ b/solution.py
@@ -145,34 +145,85 @@
     )(windows)
 
 
-def product_kernel(place, *refs):
-    pieces, (block, out, parts, turned, ready, sent) = refs[:8], refs[8:]
-    for t in range(2):
-        for k in range(4):
-            parts[t, SLOT * k : SLOT * k + FOUR, :] = pieces[4 * t + k][...]
-    copies = []
-    for tile, (low, high) in enumerate(zip(EDGES[:-1], EDGES[1:])):
-        width = high - low
+def near_kernel(place, *refs):
+    pieces, (block, near, parts) = refs[:6], refs[6:]
+
+    @pl.when(place[1] == 0)
+    def _():
+        for t in range(2):
+            for k in range(3):
+                parts[t, SLOT * k : SLOT * k + FOUR, :] = pieces[3 * t + k][...]
+        for low, high in zip(EDGES[:-1], EDGES[1:]):
+            product = contract(parts.at[0], parts.at[1], block, low, high)
+            for k in range(3):
+                near[k, :, low:high] = product[SLOT * k : SLOT * k + FOUR, :]
+
+
+def final_kernel(place, *refs):
+    pieces, refs = refs[:8], refs[8:]
+    block, near, out, parts, turned, ready, sent = refs
+
+    def write(multiply_tile):
+        copies = []
+        for tile, (low, high) in enumerate(zip(EDGES[:-1], EDGES[1:])):
+            width = high - low
+            multiply_tile(low, high)
+            for x in range(4):
+                rows = turned[lax.rem(x - place[0] + 4, 4), :, :width]
+                ready[:, 4 * x : 4 * x + 4, low:high] = rows.reshape(SHARE, 4, width)
+            done = slice(low, high)
+            copy = pltpu.make_async_copy(
+                ready.at[:, :, done], out.at[:, :, done], sent.at[tile]
+            )
+            copy.start()
+            copies.append(copy)
+        for copy in copies:
+            copy.wait()
+
+    def far_tile(low, high):
+        turned[2, :, : high - low] = contract(pieces[2], pieces[6], block, low, high)
+        for n, k in enumerate((0, 1, 3)):
+            turned[k, :, : high - low] = near[n, :, low:high]
+
+    def whole_tile(low, high):
         product = contract(parts.at[0], parts.at[1], block, low, high)
         for k in range(4):
-            turned[k, :, :width] = product[SLOT * k : SLOT * k + FOUR, :]
-        for x in range(4):
-            rows = turned[lax.rem(x - place[0] + 4, 4), :, :width]
-            ready[:, 4 * x : 4 * x + 4, low:high] = rows.reshape(SHARE, 4, width)
-        done = slice(low, high)
-        copy = pltpu.make_async_copy(ready.at[:, :, done], out.at[:, :, done], sent.at[tile])
-        copy.start()
-        copies.append(copy)
-    for copy in copies:
-        copy.wait()
-
-
-def multiply(pieces, block):
-    place = lax.axis_index("x").astype(jnp.int32).reshape(1)
-    return pl.pallas_call(
-        product_kernel,
+            turned[k, :, : high - low] = product[SLOT * k : SLOT * k + FOUR, :]
+
+    @pl.when(place[1] == 0)
+    def _():
+        write(far_tile)
+
+    @pl.when(place[1] != 0)
+    def _():
+        for t in range(2):
+            for k in range(4):
+                parts[t, SLOT * k : SLOT * k + FOUR, :] = pieces[4 * t + k][...]
+        write(whole_tile)
+
+
+SMEM = pl.BlockSpec(memory_space=pltpu.SMEM)
+
+
+def multiply_near(place, pieces, block):
+    return pl.pallas_call(
+        near_kernel,
+        out_shape=jax.ShapeDtypeStruct((3, FOUR, ROWS), jnp.float32),
+        in_specs=[SMEM] + [VMEM] * 7,
+        out_specs=VMEM,
+        scratch_shapes=[pltpu.VMEM((2, 3 * SLOT, HALF), jnp.bfloat16)],
+        compiler_params=pltpu.CompilerParams(vmem_limit_bytes=24 * 1024 * 1024),
+        cost_estimate=pl.CostEstimate(
+            flops=6 * FOUR * ROWS * TIME, bytes_accessed=2_000_000, transcendentals=0
+        ),
+    )(place, *pieces, block)
+
+
+def multiply(place, pieces, block, near):
+    return pl.pallas_call(
+        final_kernel,
         out_shape=jax.ShapeDtypeStruct((SHARE, 16, ROWS), jnp.float32),
-        in_specs=[pl.BlockSpec(memory_space=pltpu.SMEM)] + [VMEM] * 9,
+        in_specs=[SMEM] + [VMEM] * 10,
         out_specs=pl.BlockSpec(memory_space=pl.ANY),
         scratch_shapes=[
             pltpu.VMEM((2, 4 * SLOT, HALF), jnp.bfloat16),
@@ -182,9 +233,9 @@
         ],
         compiler_params=pltpu.CompilerParams(vmem_limit_bytes=28 * 1024 * 1024),
         cost_estimate=pl.CostEstimate(
-            flops=8 * FOUR * ROWS * TIME, bytes_accessed=2_400_000, transcendentals=0
+            flops=2 * FOUR * ROWS * TIME, bytes_accessed=2_400_000, transcendentals=0
         ),
-    )(place, *pieces, block)
+    )(place, *pieces, block, near)
 
 
 def on_device(series):
@@ -199,9 +250,13 @@
     after_second, before_first = shift(second, "x", 1), shift(first, "x", -1)
     far_first, far_second = shift(after_first, "x", 1), shift(before_second, "x", -1)
 
+    place = jnp.stack([lax.axis_index("x"), lax.axis_index("core")]).astype(jnp.int32)
+    block = order(gathered)
+    pieces = (first, before_first, after_first, second, before_second, after_second)
+    near = multiply_near(place, pieces, block)
     pieces = (first, before_first, far_first, after_first)
     pieces += (second, before_second, far_second, after_second)
-    return multiply(pieces, order(gathered)).transpose(1, 0, 2)
+    return multiply(place, pieces, block, near).transpose(1, 0, 2)
 
 
 def solution(mesh):

time: 129 us -> 127 us (0.984)
  the two profiles are of different devices: /device:TPU:8 before, /device:TPU:9 now
where the time goes in v13:
time: 127 us
  blocking collectives  69.7 us (55%)
  starting transfers between devices  18.6 us (15%)
  between operations  13.6 us (11%)
  waiting for transfers between devices  11.8 us (9%)
  Pallas kernels  11.7 us (9%)
  local copies, waits for them, and re-layouts  1.49 us (1%)
    all_to_all x1, blocking collectives, on_device(): lax.all_to_all(pack(series), BULK, 0, 0, tiled=True)  37 us
    all_gather x1, blocking collectives, on_device(): part = lax.all_gather(own.reshape(SHARE, TIME // 128, 128), 'zl')  22.7 us
    ppermute x6, starting transfers between devices, shift(): lax.ppermute(array, axis, [(i, (i + by) % size) for i in range(size)])  18.6 us
    all_gather x1, blocking collectives, on_device(): gathered = lax.all_gather(lax.all_gather(wide, 'zh'), ('y', 'core'))  10 us
    all_gather x1, waiting for transfers between devices, on_device(): gathered = lax.all_gather(lax.all_gather(wide, 'zh'), ('y', 'core'))  7.81 us
    pallas_call x1, Pallas kernels, multiply(): pl.pallas_call(final_kernel, out_shape=jax.ShapeDtypeStruct((SHARE, 16, R...  6.89 us
    ppermute x6, waiting for transfers between devices, shift(): lax.ppermute(array, axis, [(i, (i + by) % size) for i in range(size)])  4.01 us
    pallas_call x1, Pallas kernels, order(): pl.pallas_call(order_kernel, out_shape=jax.ShapeDtypeStruct((ROWS, TIME),...  3.2 us
  transfers between devices with their start and end apart: 7, of which 2 were waited for; matrix products, arithmetic and copies ran while one was open for 0% of the time, Pallas kernels for 3%

profile of v13, /device:TPU:9, one launch (start us, length us, event | category | flops | bytes accessed | tf_op | source)
XLA Modules:
  0.0 127.0 jit_solution(5098238502225517815)
XLA Ops:
  6.5 0.0 all-gather.4.cloned.1.call-start
  6.5 0.0 copy-start
  6.5 1.0 copy-done
  7.6 0.5 shard_map.17
  8.1 37.0 %all_to_all.5.pieces = f32[32,32,128]{2,1,0:T(8,128)S(1)} all-to-all(f32[32,32,128]{2,1,0:T(8,128)S(1)} %shard_map.17), channel_id=1, replica_groups=mesh['x'=4,'zl'=4,'zh'=2,'y'=8,'core'=2] {'zh','y','core'}, dimensions={0} | all-to-all | bytes 1048576 | tf_op jit(solution)/shard_map/all_to_all | solution.py:242
  45.1 0.6 shard_map.18
  45.7 10.0 %all-gather = bf16[64,3200]{1,0:T(8,128)(2,1)} all-gather(bf16[32,3200]{1,0:T(8,128)(2,1)S(1)} %get-tuple-element.8), channel_id=2, replica_groups=mesh['x'=4,'zl'=4,'zh'=2,'y'=8,'core'=2] {'zh'}, dimensions={0}, use_global_device_ids=true | all-gather | bytes 614400 | tf_op jit(solution)/shard_map/all_gather | solution.py:244
  55.7 0.0 all-gather.4.cloned.1.call-update
  55.7 0.1 constant_dynamic-slice_fusion
  55.9 22.7 %all_gather.15 = bf16[4,33,24,128]{3,2,0,1:T(8,128)(2,1)S(1)} all-gather(bf16[1,33,24,128]{3,2,0,1:T(8,128)(2,1)S(1)} %slice_bitcast_fusion), channel_id=1, replica_groups=mesh['x'=4,'zl'=4,'zh'=2,'y'=8,'core'=2] {'zl'}, dimensions={0}, use_global_device_ids=true | all-gather | bytes 1013760 | tf_op jit(solution)/shard_map/all_gather | solution.py:246
  78.5 0.1 pad.2
  78.7 0.2 copy.3
  78.8 0.1 fusion
  78.9 4.4 %collective-permute-start.3 = (bf16[132,1536]{1,0:T(8,128)(2,1)S(1)}, bf16[132,1536]{1,0:T(8,128)(2,1)S(1)}, u32[]{:S(2)}, u32[]{:S(2)}) collective-permute-start(bf16[132,1536]{1,0:T(8,128)(2,1)S(1)} %get-tuple-element.9.refs_3_.refs_4_), channel_id=1, source_target_pairs={{0,384},{128,0},{256,128},{384,256},{1,385},{129,1},{257,129},{385... | collective-permute-start | bytes 1216520 | tf_op jit(solution)/shard_map/ppermute | solution.py:94
  83.3 1.9 %collective-permute-start.1 = (bf16[132,1536]{1,0:T(8,128)(2,1)S(1)}, bf16[132,1536]{1,0:T(8,128)(2,1)S(1)}, u32[]{:S(2)}, u32[]{:S(2)}) collective-permute-start(bf16[132,1536]{1,0:T(8,128)(2,1)S(1)} %get-tuple-element.10.refs_0_), channel_id=1, source_target_pairs={{0,128},{128,256},{256,384},{384,0},{1,129},{129,257},{257,385},{3... | collective-permute-start | bytes 1216520 | tf_op jit(solution)/shard_map/ppermute | solution.py:94
  85.2 2.1 %collective-permute-start.5 = (bf16[132,1536]{1,0:T(8,128)(2,1)S(1)}, bf16[132,1536]{1,0:T(8,128)(2,1)S(1)}, u32[]{:S(2)}, u32[]{:S(2)}) collective-permute-start(bf16[132,1536]{1,0:T(8,128)(2,1)S(1)} %get-tuple-element.9.refs_3_.refs_4_), channel_id=1, source_target_pairs={{0,128},{128,256},{256,384},{384,0},{1,129},{129,257},{257,385},{3... | collective-permute-start | bytes 1216520 | tf_op jit(solution)/shard_map/ppermute | solution.py:94
  87.3 4.4 %collective-permute-start = (bf16[132,1536]{1,0:T(8,128)(2,1)S(1)}, bf16[132,1536]{1,0:T(8,128)(2,1)S(1)}, u32[]{:S(2)}, u32[]{:S(2)}) collective-permute-start(bf16[132,1536]{1,0:T(8,128)(2,1)S(1)} %get-tuple-element.10.refs_0_), channel_id=1, source_target_pairs={{0,384},{128,0},{256,128},{384,256},{1,385},{129,1},{257,129},{385... | collective-permute-start | bytes 1216520 | tf_op jit(solution)/shard_map/ppermute | solution.py:94
  91.7 0.0 collective-permute-done.3.refs_4_.refs_5_
  91.7 3.9 %collective-permute-start.4 = (bf16[132,1536]{1,0:T(8,128)(2,1)S(1)}, bf16[132,1536]{1,0:T(8,128)(2,1)S(1)}, u32[]{:S(2)}, u32[]{:S(2)}) collective-permute-start(bf16[132,1536]{1,0:T(8,128)(2,1)S(1)} %collective-permute-done.3.refs_4_.refs_5_), channel_id=1, source_target_pairs={{0,384},{128,0},{256,128},{384,256},{1,385},{129,1},{257,129},{385... | collective-permute-start | bytes 1216520 | tf_op jit(solution)/shard_map/ppermute | solution.py:94
  95.6 0.0 collective-permute-done.1.refs_2_.refs_3_
  95.6 1.9 %collective-permute-start.2 = (bf16[132,1536]{1,0:T(8,128)(2,1)S(1)}, bf16[132,1536]{1,0:T(8,128)(2,1)S(1)}, u32[]{:S(2)}, u32[]{:S(2)}) collective-permute-start(bf16[132,1536]{1,0:T(8,128)(2,1)S(1)} %collective-permute-done.1.refs_2_.refs_3_), channel_id=1, source_target_pairs={{0,128},{128,256},{256,384},{384,0},{1,129},{129,257},{257,385},{3... | collective-permute-start | bytes 1216520 | tf_op jit(solution)/shard_map/ppermute | solution.py:94
  97.6 0.1 pad_add_fusion.place
  97.7 7.8 %all-gather.4.cloned.1.call-done = bf16[32,32,3200]{2,1,0:T(8,128)(2,1)} async-done(((bf16[2,32,3200]{2,1,0:T(8,128)(2,1)}), bf16[32,32,3200]{2,1,0:T(8,128)(2,1)}) %all-gather.4.cloned.1.call-update) | async-done | bytes 6553616 | tf_op jit(solution)/shard_map/all_gather | solution.py:244
  105.5 3.2 %shard_map.19.refs_6_.refs_8_ = bf16[1056,3072]{1,0:T(8,128)(2,1)S(1)} custom-call(bf16[16,2,32,3200]{3,2,1,0:T(8,128)(2,1)} %bitcast.18), custom_call_target="tpu_custom_call" | custom-call | bytes 7000000 | tf_op jit(solution)/shard_map/pallas_call | solution.py:132
  108.7 0.0 collective-permute-done.5.refs_5_.refs_7_
  108.7 0.0 collective-permute-done.refs_1_
  108.7 0.6 shard_map.20.refs_9_
  109.3 0.0 collective-permute-done.4.refs_6_
  109.3 4.0 %collective-permute-done.2.refs_2_ = bf16[132,1536]{1,0:T(8,128)(2,1)S(1)} collective-permute-done((bf16[132,1536]{1,0:T(8,128)(2,1)S(1)}, bf16[132,1536]{1,0:T(8,128)(2,1)S(1)}, u32[]{:S(2)}, u32[]{:S(2)}) %collective-permute-start.2) | collective-permute-done | bytes 405536 | tf_op jit(solution)/shard_map/ppermute | solution.py:94
  113.3 6.9 %shard_map.21 = f32[33,16,1056]{2,1,0:T(8,128)} custom-call(s32[2]{0:T(128)S(1)} %pad_add_fusion.place, bf16[132,1536]{1,0:T(8,128)(2,1)S(1)} %get-tuple-element.10.refs_0_, bf16[132,1536]{1,0:T(8,128)(2,1)S(1)} %collective-permute-done.refs_1_, bf16[132,1536]{1,0:T(8,128)(2,1)S(1)} %collective-permute-done.2.refs_2_, ...), custom_call_target="tpu_custom_call" | custom-call | flops 856424448 | bytes 2400000 | tf_op jit(solution)/shard_map/pallas_call | solution.py:223
  (2 shorter events, 0.1 us)
Async XLA Ops:
  6.5 98.9 %all-gather.4.cloned.1.call-start = ((), (), s32[]{:S(2)}) async-start(), calls=%async_computation.1 | async-start | bytes 6963200 | tf_op jit(solution)/shard_map/all_gather | solution.py:244
  6.5 1.0 copy-start
  78.9 12.8 %collective-permute-start.3 = (bf16[132,1536]{1,0:T(8,128)(2,1)S(1)}, bf16[132,1536]{1,0:T(8,128)(2,1)S(1)}, u32[]{:S(2)}, u32[]{:S(2)}) collective-permute-start(bf16[132,1536]{1,0:T(8,128)(2,1)S(1)} %get-tuple-element.9.refs_3_.refs_4_), channel_id=1, source_target_pairs={{0,384},{128,0},{256,128},{384,256},{1,385},{129,1},{257,129},{385... | collective-permute-start | bytes 1216520 | tf_op jit(solution)/shard_map/ppermute | solution.py:94
  83.3 12.3 %collective-permute-start.1 = (bf16[132,1536]{1,0:T(8,128)(2,1)S(1)}, bf16[132,1536]{1,0:T(8,128)(2,1)S(1)}, u32[]{:S(2)}, u32[]{:S(2)}) collective-permute-start(bf16[132,1536]{1,0:T(8,128)(2,1)S(1)} %get-tuple-element.10.refs_0_), channel_id=1, source_target_pairs={{0,128},{128,256},{256,384},{384,0},{1,129},{129,257},{257,385},{3... | collective-permute-start | bytes 1216520 | tf_op jit(solution)/shard_map/ppermute | solution.py:94
  85.2 23.5 %collective-permute-start.5 = (bf16[132,1536]{1,0:T(8,128)(2,1)S(1)}, bf16[132,1536]{1,0:T(8,128)(2,1)S(1)}, u32[]{:S(2)}, u32[]{:S(2)}) collective-permute-start(bf16[132,1536]{1,0:T(8,128)(2,1)S(1)} %get-tuple-element.9.refs_3_.refs_4_), channel_id=1, source_target_pairs={{0,128},{128,256},{256,384},{384,0},{1,129},{129,257},{257,385},{3... | collective-permute-start | bytes 1216520 | tf_op jit(solution)/shard_map/ppermute | solution.py:94
  87.3 21.4 %collective-permute-start = (bf16[132,1536]{1,0:T(8,128)(2,1)S(1)}, bf16[132,1536]{1,0:T(8,128)(2,1)S(1)}, u32[]{:S(2)}, u32[]{:S(2)}) collective-permute-start(bf16[132,1536]{1,0:T(8,128)(2,1)S(1)} %get-tuple-element.10.refs_0_), channel_id=1, source_target_pairs={{0,384},{128,0},{256,128},{384,256},{1,385},{129,1},{257,129},{385... | collective-permute-start | bytes 1216520 | tf_op jit(solution)/shard_map/ppermute | solution.py:94
  91.7 17.5 %collective-permute-start.4 = (bf16[132,1536]{1,0:T(8,128)(2,1)S(1)}, bf16[132,1536]{1,0:T(8,128)(2,1)S(1)}, u32[]{:S(2)}, u32[]{:S(2)}) collective-permute-start(bf16[132,1536]{1,0:T(8,128)(2,1)S(1)} %collective-permute-done.3.refs_4_.refs_5_), channel_id=1, source_target_pairs={{0,384},{128,0},{256,128},{384,256},{1,385},{129,1},{257,129},{385... | collective-permute-start | bytes 1216520 | tf_op jit(solution)/shard_map/ppermute | solution.py:94
  95.6 17.6 %collective-permute-start.2 = (bf16[132,1536]{1,0:T(8,128)(2,1)S(1)}, bf16[132,1536]{1,0:T(8,128)(2,1)S(1)}, u32[]{:S(2)}, u32[]{:S(2)}) collective-permute-start(bf16[132,1536]{1,0:T(8,128)(2,1)S(1)} %collective-permute-done.1.refs_2_.refs_3_), channel_id=1, source_target_pairs={{0,128},{128,256},{256,384},{384,0},{1,129},{129,257},{257,385},{3... | collective-permute-start | bytes 1216520 | tf_op jit(solution)/shard_map/ppermute | solution.py:94
Sparse Core Ops, SparseCore 0:
  55.8 49.5 all-gather.3

commit v14 on v12

--- a/solution.py
+++ b/solution.py
@@ -146,10 +146,7 @@
         for k in range(3):
             near[k, :, low:high] = product[SLOT * k : SLOT * k + FOUR, :]
 
-    for copy in copies[0]:
-        copy.wait()
-    multiply_rows(EDGES[0], EDGES[1])
-    for group in range(1, 4):
+    for group in range(4):
         for copy in copies[group]:
             copy.wait()
     for group in range(4):
@@ -164,7 +161,7 @@
             tail[:, 96 * source : 96 * source + 96] = steps[:, :96]
         start = GROUP * group + 256
         block[start : start + 8, :] = tail[...].astype(jnp.bfloat16)
-    for low, high in zip(EDGES[1:-1], EDGES[2:]):
+    for low, high in zip(EDGES[:-1], EDGES[1:]):
         multiply_rows(low, high)
 
 

time: 125 us -> 125 us (level)
  no operation moved by 1% of the time
where the time goes in v14:
time: 125 us
  blocking collectives  70.6 us (56%)
  starting transfers between devices  17.5 us (14%)
  between operations  13.6 us (11%)
  Pallas kernels  12.1 us (10%)
  waiting for transfers between devices  9.48 us (8%)
  local copies, waits for them, and re-layouts  1.49 us (1%)
    all_to_all x1, blocking collectives, on_device(): lax.all_to_all(pack(series), BULK, 0, 0, tiled=True)  38.1 us
    all_gather x1, blocking collectives, on_device(): part = lax.all_gather(own.reshape(SHARE, TIME // 128, 128), 'zl')  22.1 us
    ppermute x6, starting transfers between devices, shift(): lax.ppermute(array, axis, [(i, (i + by) % size) for i in range(size)])  17.5 us
    all_gather x1, blocking collectives, on_device(): gathered = lax.all_gather(lax.all_gather(wide, 'zh'), ('y', 'core'))  10.5 us
    ppermute x6, waiting for transfers between devices, shift(): lax.ppermute(array, axis, [(i, (i + by) % size) for i in range(size)])  9.46 us
    pallas_call x1, Pallas kernels, multiply_near(): pl.pallas_call(near_kernel, out_shape=(jax.ShapeDtypeStruct((ROWS, TIME),...  7.12 us
    pallas_call x1, Pallas kernels, multiply_far(): pl.pallas_call(far_kernel, out_shape=jax.ShapeDtypeStruct((SHARE, 16, ROW...  3.89 us
  transfers between devices with their start and end apart: 7, of which 2 were waited for; matrix products, arithmetic and copies ran while one was open for 0% of the time, Pallas kernels for 6%

profile of v14, /device:TPU:6, one launch (start us, length us, event | category | flops | bytes accessed | tf_op | source)
XLA Modules:
  0.0 124.8 jit_solution(13808357504458567620)
XLA Ops:
  6.5 0.0 all-gather.4.cloned.1.call-start
  6.5 0.0 copy-start
  6.5 1.0 copy-done
  7.6 0.5 shard_map.17
  8.1 38.1 %all_to_all.5.pieces = f32[32,32,128]{2,1,0:T(8,128)S(1)} all-to-all(f32[32,32,128]{2,1,0:T(8,128)S(1)} %shard_map.17), channel_id=1, replica_groups=mesh['x'=4,'zl'=4,'zh'=2,'y'=8,'core'=2] {'zh','y','core'}, dimensions={0} | all-to-all | bytes 1048576 | tf_op jit(solution)/shard_map/all_to_all | solution.py:232
  46.1 0.6 shard_map.18
  46.8 10.5 %all-gather = bf16[64,3200]{1,0:T(8,128)(2,1)} all-gather(bf16[32,3200]{1,0:T(8,128)(2,1)S(1)} %get-tuple-element.10), channel_id=2, replica_groups=mesh['x'=4,'zl'=4,'zh'=2,'y'=8,'core'=2] {'zh'}, dimensions={0}, use_global_device_ids=true | all-gather | bytes 614400 | tf_op jit(solution)/shard_map/all_gather | solution.py:234
  57.2 0.0 all-gather.4.cloned.1.call-update
  57.3 0.1 constant_dynamic-slice_fusion
  57.4 22.1 %all_gather.15 = bf16[4,33,24,128]{3,2,0,1:T(8,128)(2,1)S(1)} all-gather(bf16[1,33,24,128]{3,2,0,1:T(8,128)(2,1)S(1)} %slice_bitcast_fusion), channel_id=1, replica_groups=mesh['x'=4,'zl'=4,'zh'=2,'y'=8,'core'=2] {'zl'}, dimensions={0}, use_global_device_ids=true | all-gather | bytes 1013760 | tf_op jit(solution)/shard_map/all_gather | solution.py:236
  79.5 0.1 pad
  79.6 0.2 copy.3
  79.8 0.1 fusion
  79.9 2.4 %collective-permute-start = (bf16[132,1536]{1,0:T(8,128)(2,1)S(1)}, bf16[132,1536]{1,0:T(8,128)(2,1)S(1)}, u32[]{:S(2)}, u32[]{:S(2)}) collective-permute-start(bf16[132,1536]{1,0:T(8,128)(2,1)S(1)} %get-tuple-element.14.refs_0_), channel_id=1, source_target_pairs={{0,128},{128,256},{256,384},{384,0},{1,129},{129,257},{257,385},{3... | collective-permute-start | bytes 1216520 | tf_op jit(solution)/shard_map/ppermute | solution.py:94
  82.3 3.5 %collective-permute-start.2 = (bf16[132,1536]{1,0:T(8,128)(2,1)S(1)}, bf16[132,1536]{1,0:T(8,128)(2,1)S(1)}, u32[]{:S(2)}, u32[]{:S(2)}) collective-permute-start(bf16[132,1536]{1,0:T(8,128)(2,1)S(1)} %get-tuple-element.13.refs_3_), channel_id=1, source_target_pairs={{0,384},{128,0},{256,128},{384,256},{1,385},{129,1},{257,129},{385... | collective-permute-start | bytes 1216520 | tf_op jit(solution)/shard_map/ppermute | solution.py:94
  85.7 2.7 %collective-permute-start.4 = (bf16[132,1536]{1,0:T(8,128)(2,1)S(1)}, bf16[132,1536]{1,0:T(8,128)(2,1)S(1)}, u32[]{:S(2)}, u32[]{:S(2)}) collective-permute-start(bf16[132,1536]{1,0:T(8,128)(2,1)S(1)} %get-tuple-element.14.refs_0_), channel_id=1, source_target_pairs={{0,384},{128,0},{256,128},{384,256},{1,385},{129,1},{257,129},{385... | collective-permute-start | bytes 1216520 | tf_op jit(solution)/shard_map/ppermute | solution.py:94
  88.5 4.3 %collective-permute-start.5 = (bf16[132,1536]{1,0:T(8,128)(2,1)S(1)}, bf16[132,1536]{1,0:T(8,128)(2,1)S(1)}, u32[]{:S(2)}, u32[]{:S(2)}) collective-permute-start(bf16[132,1536]{1,0:T(8,128)(2,1)S(1)} %get-tuple-element.13.refs_3_), channel_id=1, source_target_pairs={{0,128},{128,256},{256,384},{384,0},{1,129},{129,257},{257,385},{3... | collective-permute-start | bytes 1216520 | tf_op jit(solution)/shard_map/ppermute | solution.py:94
  92.8 0.0 collective-permute-done.refs_2_
  92.8 2.4 %collective-permute-start.1 = (bf16[132,1536]{1,0:T(8,128)(2,1)S(1)}, bf16[132,1536]{1,0:T(8,128)(2,1)S(1)}, u32[]{:S(2)}, u32[]{:S(2)}) collective-permute-start(bf16[132,1536]{1,0:T(8,128)(2,1)S(1)} %collective-permute-done.refs_2_), channel_id=1, source_target_pairs={{0,128},{128,256},{256,384},{384,0},{1,129},{129,257},{257,385},{3... | collective-permute-start | bytes 1216520 | tf_op jit(solution)/shard_map/ppermute | solution.py:94
  95.2 2.7 %collective-permute-done.2.refs_4_ = bf16[132,1536]{1,0:T(8,128)(2,1)S(1)} collective-permute-done((bf16[132,1536]{1,0:T(8,128)(2,1)S(1)}, bf16[132,1536]{1,0:T(8,128)(2,1)S(1)}, u32[]{:S(2)}, u32[]{:S(2)}) %collective-permute-start.2) | collective-permute-done | bytes 405536 | tf_op jit(solution)/shard_map/ppermute | solution.py:94
  97.9 2.2 %collective-permute-start.3 = (bf16[132,1536]{1,0:T(8,128)(2,1)S(1)}, bf16[132,1536]{1,0:T(8,128)(2,1)S(1)}, u32[]{:S(2)}, u32[]{:S(2)}) collective-permute-start(bf16[132,1536]{1,0:T(8,128)(2,1)S(1)} %collective-permute-done.2.refs_4_), channel_id=1, source_target_pairs={{0,384},{128,0},{256,128},{384,256},{1,385},{129,1},{257,129},{385... | collective-permute-start | bytes 1216520 | tf_op jit(solution)/shard_map/ppermute | solution.py:94
  100.2 6.7 %collective-permute-done.4.refs_1_ = bf16[132,1536]{1,0:T(8,128)(2,1)S(1)} collective-permute-done((bf16[132,1536]{1,0:T(8,128)(2,1)S(1)}, bf16[132,1536]{1,0:T(8,128)(2,1)S(1)}, u32[]{:S(2)}, u32[]{:S(2)}) %collective-permute-start.4) | collective-permute-done | bytes 405536 | tf_op jit(solution)/shard_map/ppermute | solution.py:94
  106.9 0.0 collective-permute-done.5.refs_5_
  106.9 0.0 all-gather.4.cloned.1.call-done
  106.9 7.1 %shard_map.19 = (bf16[1056,3072]{1,0:T(8,128)(2,1)S(1)}, f32[3,132,1056]{2,1,0:T(8,128)S(1)}) custom-call(bf16[132,1536]{1,0:T(8,128)(2,1)S(1)} %get-tuple-element.14.refs_0_, bf16[132,1536]{1,0:T(8,128)(2,1)S(1)} %collective-permute-done.4.refs_1_, bf16[132,1536]{1,0:T(8,128)(2,1)S(1)} %collective-permute-done.refs_2_, ...), custom_call_target="tpu_custom_call" | custom-call | flops 2569273344 | bytes 14000000 | tf_op jit(solution)/shard_map/pallas_call | solution.py:188
  114.0 0.0 collective-permute-done.1.first
  114.0 0.0 collective-permute-done.3.second
  114.0 3.9 %shard_map.20 = f32[33,16,1056]{2,1,0:T(8,128)} custom-call(s32[1]{0:T(128)} %bitcast.place, bf16[132,1536]{1,0:T(8,128)(2,1)S(1)} %collective-permute-done.1.first, bf16[132,1536]{1,0:T(8,128)(2,1)S(1)} %collective-permute-done.3.second, bf16[1056,3072]{1,0:T(8,128)(2,1)S(1)} %get-tuple-element.11.block, f32[3,132,1056]{2,1,0:T(8,128)S(1)} %get-tuple-element.12.near), custom_call_target="tpu_custom_call" | custom-call | flops 856424448 | bytes 8000000 | tf_op jit(solution)/shard_map/pallas_call | solution.py:214
  (2 shorter events, 0.1 us)
Async XLA Ops:
  6.5 100.4 %all-gather.4.cloned.1.call-start = ((), (), s32[]{:S(2)}) async-start(), calls=%async_computation.1 | async-start | bytes 6963200 | tf_op jit(solution)/shard_map/all_gather | solution.py:234
  6.5 1.0 copy-start
  79.9 12.9 %collective-permute-start = (bf16[132,1536]{1,0:T(8,128)(2,1)S(1)}, bf16[132,1536]{1,0:T(8,128)(2,1)S(1)}, u32[]{:S(2)}, u32[]{:S(2)}) collective-permute-start(bf16[132,1536]{1,0:T(8,128)(2,1)S(1)} %get-tuple-element.14.refs_0_), channel_id=1, source_target_pairs={{0,128},{128,256},{256,384},{384,0},{1,129},{129,257},{257,385},{3... | collective-permute-start | bytes 1216520 | tf_op jit(solution)/shard_map/ppermute | solution.py:94
  82.3 15.7 %collective-permute-start.2 = (bf16[132,1536]{1,0:T(8,128)(2,1)S(1)}, bf16[132,1536]{1,0:T(8,128)(2,1)S(1)}, u32[]{:S(2)}, u32[]{:S(2)}) collective-permute-start(bf16[132,1536]{1,0:T(8,128)(2,1)S(1)} %get-tuple-element.13.refs_3_), channel_id=1, source_target_pairs={{0,384},{128,0},{256,128},{384,256},{1,385},{129,1},{257,129},{385... | collective-permute-start | bytes 1216520 | tf_op jit(solution)/shard_map/ppermute | solution.py:94
  85.7 21.2 %collective-permute-start.4 = (bf16[132,1536]{1,0:T(8,128)(2,1)S(1)}, bf16[132,1536]{1,0:T(8,128)(2,1)S(1)}, u32[]{:S(2)}, u32[]{:S(2)}) collective-permute-start(bf16[132,1536]{1,0:T(8,128)(2,1)S(1)} %get-tuple-element.14.refs_0_), channel_id=1, source_target_pairs={{0,384},{128,0},{256,128},{384,256},{1,385},{129,1},{257,129},{385... | collective-permute-start | bytes 1216520 | tf_op jit(solution)/shard_map/ppermute | solution.py:94
  88.5 18.4 %collective-permute-start.5 = (bf16[132,1536]{1,0:T(8,128)(2,1)S(1)}, bf16[132,1536]{1,0:T(8,128)(2,1)S(1)}, u32[]{:S(2)}, u32[]{:S(2)}) collective-permute-start(bf16[132,1536]{1,0:T(8,128)(2,1)S(1)} %get-tuple-element.13.refs_3_), channel_id=1, source_target_pairs={{0,128},{128,256},{256,384},{384,0},{1,129},{129,257},{257,385},{3... | collective-permute-start | bytes 1216520 | tf_op jit(solution)/shard_map/ppermute | solution.py:94
  92.8 21.2 %collective-permute-start.1 = (bf16[132,1536]{1,0:T(8,128)(2,1)S(1)}, bf16[132,1536]{1,0:T(8,128)(2,1)S(1)}, u32[]{:S(2)}, u32[]{:S(2)}) collective-permute-start(bf16[132,1536]{1,0:T(8,128)(2,1)S(1)} %collective-permute-done.refs_2_), channel_id=1, source_target_pairs={{0,128},{128,256},{256,384},{384,0},{1,129},{129,257},{257,385},{3... | collective-permute-start | bytes 1216520 | tf_op jit(solution)/shard_map/ppermute | solution.py:94
  97.9 16.1 %collective-permute-start.3 = (bf16[132,1536]{1,0:T(8,128)(2,1)S(1)}, bf16[132,1536]{1,0:T(8,128)(2,1)S(1)}, u32[]{:S(2)}, u32[]{:S(2)}) collective-permute-start(bf16[132,1536]{1,0:T(8,128)(2,1)S(1)} %collective-permute-done.2.refs_4_), channel_id=1, source_target_pairs={{0,384},{128,0},{256,128},{384,256},{1,385},{129,1},{257,129},{385... | collective-permute-start | bytes 1216520 | tf_op jit(solution)/shard_map/ppermute | solution.py:94
Sparse Core Ops, SparseCore 0:
  57.4 48.0 all-gather.3

commit v15 on v14

--- a/solution.py
+++ b/solution.py
@@ -12,7 +12,7 @@
 BULK = ("zh", "y", "core")
 SHARE = 33
 FOUR = 4 * SHARE
-SLOT = 144
+SLOT = 136
 WINDOW = 40
 WIDE = TIME + 128
 ROWS = 1056

time: 125 us -> 125 us (level)
  no operation moved by 1% of the time
where the time goes in v15:
time: 125 us
  blocking collectives  70.6 us (56%)
  starting transfers between devices  17.5 us (14%)
  between operations  13.6 us (11%)
  Pallas kernels  12 us (10%)
  waiting for transfers between devices  9.48 us (8%)
  local copies, waits for them, and re-layouts  1.49 us (1%)
    all_to_all x1, blocking collectives, on_device(): lax.all_to_all(pack(series), BULK, 0, 0, tiled=True)  38.1 us
    all_gather x1, blocking collectives, on_device(): part = lax.all_gather(own.reshape(SHARE, TIME // 128, 128), 'zl')  22.1 us
    ppermute x6, starting transfers between devices, shift(): lax.ppermute(array, axis, [(i, (i + by) % size) for i in range(size)])  17.5 us
    all_gather x1, blocking collectives, on_device(): gathered = lax.all_gather(lax.all_gather(wide, 'zh'), ('y', 'core'))  10.5 us
    ppermute x6, waiting for transfers between devices, shift(): lax.ppermute(array, axis, [(i, (i + by) % size) for i in range(size)])  9.46 us
    pallas_call x1, Pallas kernels, multiply_near(): pl.pallas_call(near_kernel, out_shape=(jax.ShapeDtypeStruct((ROWS, TIME),...  6.99 us
    pallas_call x1, Pallas kernels, multiply_far(): pl.pallas_call(far_kernel, out_shape=jax.ShapeDtypeStruct((SHARE, 16, ROW...  3.89 us
  transfers between devices with their start and end apart: 7, of which 2 were waited for; matrix products, arithmetic and copies ran while one was open for 0% of the time, Pallas kernels for 6%

profile of v15, /device:TPU:6, one launch (start us, length us, event | category | flops | bytes accessed | tf_op | source)
XLA Modules:
  0.0 124.7 jit_solution(2096087230406816183)
XLA Ops:
  6.5 0.0 all-gather.4.cloned.1.call-start
  6.5 0.0 copy-start
  6.5 1.0 copy-done
  7.6 0.5 shard_map.17
  8.1 38.1 %all_to_all.5.pieces = f32[32,32,128]{2,1,0:T(8,128)S(1)} all-to-all(f32[32,32,128]{2,1,0:T(8,128)S(1)} %shard_map.17), channel_id=1, replica_groups=mesh['x'=4,'zl'=4,'zh'=2,'y'=8,'core'=2] {'zh','y','core'}, dimensions={0} | all-to-all | bytes 1048576 | tf_op jit(solution)/shard_map/all_to_all | solution.py:232
  46.1 0.6 shard_map.18
  46.8 10.5 %all-gather = bf16[64,3200]{1,0:T(8,128)(2,1)} all-gather(bf16[32,3200]{1,0:T(8,128)(2,1)S(1)} %get-tuple-element.10), channel_id=2, replica_groups=mesh['x'=4,'zl'=4,'zh'=2,'y'=8,'core'=2] {'zh'}, dimensions={0}, use_global_device_ids=true | all-gather | bytes 614400 | tf_op jit(solution)/shard_map/all_gather | solution.py:234
  57.2 0.0 all-gather.4.cloned.1.call-update
  57.3 0.1 constant_dynamic-slice_fusion
  57.4 22.1 %all_gather.15 = bf16[4,33,24,128]{3,2,0,1:T(8,128)(2,1)S(1)} all-gather(bf16[1,33,24,128]{3,2,0,1:T(8,128)(2,1)S(1)} %slice_bitcast_fusion), channel_id=1, replica_groups=mesh['x'=4,'zl'=4,'zh'=2,'y'=8,'core'=2] {'zl'}, dimensions={0}, use_global_device_ids=true | all-gather | bytes 1013760 | tf_op jit(solution)/shard_map/all_gather | solution.py:236
  79.5 0.1 pad
  79.6 0.2 copy.3
  79.8 0.1 fusion
  79.9 2.4 %collective-permute-start = (bf16[132,1536]{1,0:T(8,128)(2,1)S(1)}, bf16[132,1536]{1,0:T(8,128)(2,1)S(1)}, u32[]{:S(2)}, u32[]{:S(2)}) collective-permute-start(bf16[132,1536]{1,0:T(8,128)(2,1)S(1)} %get-tuple-element.14.refs_0_), channel_id=1, source_target_pairs={{0,128},{128,256},{256,384},{384,0},{1,129},{129,257},{257,385},{3... | collective-permute-start | bytes 1216520 | tf_op jit(solution)/shard_map/ppermute | solution.py:94
  82.3 3.5 %collective-permute-start.2 = (bf16[132,1536]{1,0:T(8,128)(2,1)S(1)}, bf16[132,1536]{1,0:T(8,128)(2,1)S(1)}, u32[]{:S(2)}, u32[]{:S(2)}) collective-permute-start(bf16[132,1536]{1,0:T(8,128)(2,1)S(1)} %get-tuple-element.13.refs_3_), channel_id=1, source_target_pairs={{0,384},{128,0},{256,128},{384,256},{1,385},{129,1},{257,129},{385... | collective-permute-start | bytes 1216520 | tf_op jit(solution)/shard_map/ppermute | solution.py:94
  85.7 2.7 %collective-permute-start.4 = (bf16[132,1536]{1,0:T(8,128)(2,1)S(1)}, bf16[132,1536]{1,0:T(8,128)(2,1)S(1)}, u32[]{:S(2)}, u32[]{:S(2)}) collective-permute-start(bf16[132,1536]{1,0:T(8,128)(2,1)S(1)} %get-tuple-element.14.refs_0_), channel_id=1, source_target_pairs={{0,384},{128,0},{256,128},{384,256},{1,385},{129,1},{257,129},{385... | collective-permute-start | bytes 1216520 | tf_op jit(solution)/shard_map/ppermute | solution.py:94
  88.5 4.3 %collective-permute-start.5 = (bf16[132,1536]{1,0:T(8,128)(2,1)S(1)}, bf16[132,1536]{1,0:T(8,128)(2,1)S(1)}, u32[]{:S(2)}, u32[]{:S(2)}) collective-permute-start(bf16[132,1536]{1,0:T(8,128)(2,1)S(1)} %get-tuple-element.13.refs_3_), channel_id=1, source_target_pairs={{0,128},{128,256},{256,384},{384,0},{1,129},{129,257},{257,385},{3... | collective-permute-start | bytes 1216520 | tf_op jit(solution)/shard_map/ppermute | solution.py:94
  92.8 0.0 collective-permute-done.refs_2_
  92.8 2.4 %collective-permute-start.1 = (bf16[132,1536]{1,0:T(8,128)(2,1)S(1)}, bf16[132,1536]{1,0:T(8,128)(2,1)S(1)}, u32[]{:S(2)}, u32[]{:S(2)}) collective-permute-start(bf16[132,1536]{1,0:T(8,128)(2,1)S(1)} %collective-permute-done.refs_2_), channel_id=1, source_target_pairs={{0,128},{128,256},{256,384},{384,0},{1,129},{129,257},{257,385},{3... | collective-permute-start | bytes 1216520 | tf_op jit(solution)/shard_map/ppermute | solution.py:94
  95.2 2.7 %collective-permute-done.2.refs_4_ = bf16[132,1536]{1,0:T(8,128)(2,1)S(1)} collective-permute-done((bf16[132,1536]{1,0:T(8,128)(2,1)S(1)}, bf16[132,1536]{1,0:T(8,128)(2,1)S(1)}, u32[]{:S(2)}, u32[]{:S(2)}) %collective-permute-start.2) | collective-permute-done | bytes 405536 | tf_op jit(solution)/shard_map/ppermute | solution.py:94
  97.9 2.2 %collective-permute-start.3 = (bf16[132,1536]{1,0:T(8,128)(2,1)S(1)}, bf16[132,1536]{1,0:T(8,128)(2,1)S(1)}, u32[]{:S(2)}, u32[]{:S(2)}) collective-permute-start(bf16[132,1536]{1,0:T(8,128)(2,1)S(1)} %collective-permute-done.2.refs_4_), channel_id=1, source_target_pairs={{0,384},{128,0},{256,128},{384,256},{1,385},{129,1},{257,129},{385... | collective-permute-start | bytes 1216520 | tf_op jit(solution)/shard_map/ppermute | solution.py:94
  100.2 6.7 %collective-permute-done.4.refs_1_ = bf16[132,1536]{1,0:T(8,128)(2,1)S(1)} collective-permute-done((bf16[132,1536]{1,0:T(8,128)(2,1)S(1)}, bf16[132,1536]{1,0:T(8,128)(2,1)S(1)}, u32[]{:S(2)}, u32[]{:S(2)}) %collective-permute-start.4) | collective-permute-done | bytes 405536 | tf_op jit(solution)/shard_map/ppermute | solution.py:94
  106.9 0.0 collective-permute-done.5.refs_5_
  106.9 0.0 all-gather.4.cloned.1.call-done
  106.9 7.0 %shard_map.19 = (bf16[1056,3072]{1,0:T(8,128)(2,1)S(1)}, f32[3,132,1056]{2,1,0:T(8,128)S(1)}) custom-call(bf16[132,1536]{1,0:T(8,128)(2,1)S(1)} %get-tuple-element.14.refs_0_, bf16[132,1536]{1,0:T(8,128)(2,1)S(1)} %collective-permute-done.4.refs_1_, bf16[132,1536]{1,0:T(8,128)(2,1)S(1)} %collective-permute-done.refs_2_, ...), custom_call_target="tpu_custom_call" | custom-call | flops 2569273344 | bytes 14000000 | tf_op jit(solution)/shard_map/pallas_call | solution.py:188
  113.9 0.0 collective-permute-done.1.first
  113.9 0.0 collective-permute-done.3.second
  113.9 3.9 %shard_map.20 = f32[33,16,1056]{2,1,0:T(8,128)} custom-call(s32[1]{0:T(128)} %bitcast.place, bf16[132,1536]{1,0:T(8,128)(2,1)S(1)} %collective-permute-done.1.first, bf16[132,1536]{1,0:T(8,128)(2,1)S(1)} %collective-permute-done.3.second, bf16[1056,3072]{1,0:T(8,128)(2,1)S(1)} %get-tuple-element.11.block, f32[3,132,1056]{2,1,0:T(8,128)S(1)} %get-tuple-element.12.near), custom_call_target="tpu_custom_call" | custom-call | flops 856424448 | bytes 8000000 | tf_op jit(solution)/shard_map/pallas_call | solution.py:214
  (2 shorter events, 0.1 us)
Async XLA Ops:
  6.5 100.4 %all-gather.4.cloned.1.call-start = ((), (), s32[]{:S(2)}) async-start(), calls=%async_computation.1 | async-start | bytes 6963200 | tf_op jit(solution)/shard_map/all_gather | solution.py:234
  6.5 1.0 copy-start
  79.9 12.9 %collective-permute-start = (bf16[132,1536]{1,0:T(8,128)(2,1)S(1)}, bf16[132,1536]{1,0:T(8,128)(2,1)S(1)}, u32[]{:S(2)}, u32[]{:S(2)}) collective-permute-start(bf16[132,1536]{1,0:T(8,128)(2,1)S(1)} %get-tuple-element.14.refs_0_), channel_id=1, source_target_pairs={{0,128},{128,256},{256,384},{384,0},{1,129},{129,257},{257,385},{3... | collective-permute-start | bytes 1216520 | tf_op jit(solution)/shard_map/ppermute | solution.py:94
  82.3 15.7 %collective-permute-start.2 = (bf16[132,1536]{1,0:T(8,128)(2,1)S(1)}, bf16[132,1536]{1,0:T(8,128)(2,1)S(1)}, u32[]{:S(2)}, u32[]{:S(2)}) collective-permute-start(bf16[132,1536]{1,0:T(8,128)(2,1)S(1)} %get-tuple-element.13.refs_3_), channel_id=1, source_target_pairs={{0,384},{128,0},{256,128},{384,256},{1,385},{129,1},{257,129},{385... | collective-permute-start | bytes 1216520 | tf_op jit(solution)/shard_map/ppermute | solution.py:94
  85.7 21.2 %collective-permute-start.4 = (bf16[132,1536]{1,0:T(8,128)(2,1)S(1)}, bf16[132,1536]{1,0:T(8,128)(2,1)S(1)}, u32[]{:S(2)}, u32[]{:S(2)}) collective-permute-start(bf16[132,1536]{1,0:T(8,128)(2,1)S(1)} %get-tuple-element.14.refs_0_), channel_id=1, source_target_pairs={{0,384},{128,0},{256,128},{384,256},{1,385},{129,1},{257,129},{385... | collective-permute-start | bytes 1216520 | tf_op jit(solution)/shard_map/ppermute | solution.py:94
  88.5 18.4 %collective-permute-start.5 = (bf16[132,1536]{1,0:T(8,128)(2,1)S(1)}, bf16[132,1536]{1,0:T(8,128)(2,1)S(1)}, u32[]{:S(2)}, u32[]{:S(2)}) collective-permute-start(bf16[132,1536]{1,0:T(8,128)(2,1)S(1)} %get-tuple-element.13.refs_3_), channel_id=1, source_target_pairs={{0,128},{128,256},{256,384},{384,0},{1,129},{129,257},{257,385},{3... | collective-permute-start | bytes 1216520 | tf_op jit(solution)/shard_map/ppermute | solution.py:94
  92.8 21.1 %collective-permute-start.1 = (bf16[132,1536]{1,0:T(8,128)(2,1)S(1)}, bf16[132,1536]{1,0:T(8,128)(2,1)S(1)}, u32[]{:S(2)}, u32[]{:S(2)}) collective-permute-start(bf16[132,1536]{1,0:T(8,128)(2,1)S(1)} %collective-permute-done.refs_2_), channel_id=1, source_target_pairs={{0,128},{128,256},{256,384},{384,0},{1,129},{129,257},{257,385},{3... | collective-permute-start | bytes 1216520 | tf_op jit(solution)/shard_map/ppermute | solution.py:94
  97.9 16.0 %collective-permute-start.3 = (bf16[132,1536]{1,0:T(8,128)(2,1)S(1)}, bf16[132,1536]{1,0:T(8,128)(2,1)S(1)}, u32[]{:S(2)}, u32[]{:S(2)}) collective-permute-start(bf16[132,1536]{1,0:T(8,128)(2,1)S(1)} %collective-permute-done.2.refs_4_), channel_id=1, source_target_pairs={{0,384},{128,0},{256,128},{384,256},{1,385},{129,1},{257,129},{385... | collective-permute-start | bytes 1216520 | tf_op jit(solution)/shard_map/ppermute | solution.py:94
Sparse Core Ops, SparseCore 0:
  57.4 48.0 all-gather.3

commit v16 on v14

--- a/solution.py
+++ b/solution.py
@@ -17,7 +17,7 @@
 WIDE = TIME + 128
 ROWS = 1056
 GROUP = 8 * SHARE
-EDGES = (0, 256, 512, 768, ROWS)
+EDGES = (0, 512, ROWS)
 
 VMEM = pl.BlockSpec(memory_space=pltpu.VMEM)
 
@@ -217,7 +217,7 @@
         in_specs=[pl.BlockSpec(memory_space=pltpu.SMEM), VMEM, VMEM, VMEM, VMEM],
         out_specs=pl.BlockSpec(memory_space=pl.ANY),
         scratch_shapes=[
-            pltpu.VMEM((4, FOUR, 384), jnp.float32),
+            pltpu.VMEM((4, FOUR, 640), jnp.float32),
             pltpu.VMEM((SHARE, 16, ROWS), jnp.float32),
             pltpu.SemaphoreType.DMA((4,)),
         ],

time: 125 us -> 125 us (level)
  no operation moved by 1% of the time
where the time goes in v16:
time: 125 us
  blocking collectives  70.6 us (56%)
  starting transfers between devices  17.5 us (14%)
  between operations  13.6 us (11%)
  Pallas kernels  11.9 us (10%)
  waiting for transfers between devices  9.48 us (8%)
  local copies, waits for them, and re-layouts  1.49 us (1%)
    all_to_all x1, blocking collectives, on_device(): lax.all_to_all(pack(series), BULK, 0, 0, tiled=True)  38.1 us
    all_gather x1, blocking collectives, on_device(): part = lax.all_gather(own.reshape(SHARE, TIME // 128, 128), 'zl')  22.1 us
    ppermute x6, starting transfers between devices, shift(): lax.ppermute(array, axis, [(i, (i + by) % size) for i in range(size)])  17.5 us
    all_gather x1, blocking collectives, on_device(): gathered = lax.all_gather(lax.all_gather(wide, 'zh'), ('y', 'core'))  10.5 us
    ppermute x6, waiting for transfers between devices, shift(): lax.ppermute(array, axis, [(i, (i + by) % size) for i in range(size)])  9.46 us
    pallas_call x1, Pallas kernels, multiply_near(): pl.pallas_call(near_kernel, out_shape=(jax.ShapeDtypeStruct((ROWS, TIME),...  7.02 us
    pallas_call x1, Pallas kernels, multiply_far(): pl.pallas_call(far_kernel, out_shape=jax.ShapeDtypeStruct((SHARE, 16, ROW...  3.81 us
  transfers between devices with their start and end apart: 7, of which 2 were waited for; matrix products, arithmetic and copies ran while one was open for 0% of the time, Pallas kernels for 6%

profile of v16, /device:TPU:6, one launch (start us, length us, event | category | flops | bytes accessed | tf_op | source)
XLA Modules:
  0.0 124.6 jit_solution(2068005466589672562)
XLA Ops:
  6.5 0.0 all-gather.4.cloned.1.call-start
  6.5 0.0 copy-start
  6.5 1.0 copy-done
  7.6 0.5 shard_map.17
  8.1 38.1 %all_to_all.5.pieces = f32[32,32,128]{2,1,0:T(8,128)S(1)} all-to-all(f32[32,32,128]{2,1,0:T(8,128)S(1)} %shard_map.17), channel_id=1, replica_groups=mesh['x'=4,'zl'=4,'zh'=2,'y'=8,'core'=2] {'zh','y','core'}, dimensions={0} | all-to-all | bytes 1048576 | tf_op jit(solution)/shard_map/all_to_all | solution.py:232
  46.1 0.6 shard_map.18
  46.8 10.5 %all-gather = bf16[64,3200]{1,0:T(8,128)(2,1)} all-gather(bf16[32,3200]{1,0:T(8,128)(2,1)S(1)} %get-tuple-element.10), channel_id=2, replica_groups=mesh['x'=4,'zl'=4,'zh'=2,'y'=8,'core'=2] {'zh'}, dimensions={0}, use_global_device_ids=true | all-gather | bytes 614400 | tf_op jit(solution)/shard_map/all_gather | solution.py:234
  57.2 0.0 all-gather.4.cloned.1.call-update
  57.3 0.1 constant_dynamic-slice_fusion
  57.4 22.1 %all_gather.15 = bf16[4,33,24,128]{3,2,0,1:T(8,128)(2,1)S(1)} all-gather(bf16[1,33,24,128]{3,2,0,1:T(8,128)(2,1)S(1)} %slice_bitcast_fusion), channel_id=1, replica_groups=mesh['x'=4,'zl'=4,'zh'=2,'y'=8,'core'=2] {'zl'}, dimensions={0}, use_global_device_ids=true | all-gather | bytes 1013760 | tf_op jit(solution)/shard_map/all_gather | solution.py:236
  79.5 0.1 pad
  79.6 0.2 copy.3
  79.8 0.1 fusion
  79.9 2.4 %collective-permute-start = (bf16[132,1536]{1,0:T(8,128)(2,1)S(1)}, bf16[132,1536]{1,0:T(8,128)(2,1)S(1)}, u32[]{:S(2)}, u32[]{:S(2)}) collective-permute-start(bf16[132,1536]{1,0:T(8,128)(2,1)S(1)} %get-tuple-element.14.refs_0_), channel_id=1, source_target_pairs={{0,128},{128,256},{256,384},{384,0},{1,129},{129,257},{257,385},{3... | collective-permute-start | bytes 1216520 | tf_op jit(solution)/shard_map/ppermute | solution.py:94
  82.3 3.5 %collective-permute-start.2 = (bf16[132,1536]{1,0:T(8,128)(2,1)S(1)}, bf16[132,1536]{1,0:T(8,128)(2,1)S(1)}, u32[]{:S(2)}, u32[]{:S(2)}) collective-permute-start(bf16[132,1536]{1,0:T(8,128)(2,1)S(1)} %get-tuple-element.13.refs_3_), channel_id=1, source_target_pairs={{0,384},{128,0},{256,128},{384,256},{1,385},{129,1},{257,129},{385... | collective-permute-start | bytes 1216520 | tf_op jit(solution)/shard_map/ppermute | solution.py:94
  85.7 2.7 %collective-permute-start.4 = (bf16[132,1536]{1,0:T(8,128)(2,1)S(1)}, bf16[132,1536]{1,0:T(8,128)(2,1)S(1)}, u32[]{:S(2)}, u32[]{:S(2)}) collective-permute-start(bf16[132,1536]{1,0:T(8,128)(2,1)S(1)} %get-tuple-element.14.refs_0_), channel_id=1, source_target_pairs={{0,384},{128,0},{256,128},{384,256},{1,385},{129,1},{257,129},{385... | collective-permute-start | bytes 1216520 | tf_op jit(solution)/shard_map/ppermute | solution.py:94
  88.5 4.3 %collective-permute-start.5 = (bf16[132,1536]{1,0:T(8,128)(2,1)S(1)}, bf16[132,1536]{1,0:T(8,128)(2,1)S(1)}, u32[]{:S(2)}, u32[]{:S(2)}) collective-permute-start(bf16[132,1536]{1,0:T(8,128)(2,1)S(1)} %get-tuple-element.13.refs_3_), channel_id=1, source_target_pairs={{0,128},{128,256},{256,384},{384,0},{1,129},{129,257},{257,385},{3... | collective-permute-start | bytes 1216520 | tf_op jit(solution)/shard_map/ppermute | solution.py:94
  92.8 0.0 collective-permute-done.refs_2_
  92.8 2.4 %collective-permute-start.1 = (bf16[132,1536]{1,0:T(8,128)(2,1)S(1)}, bf16[132,1536]{1,0:T(8,128)(2,1)S(1)}, u32[]{:S(2)}, u32[]{:S(2)}) collective-permute-start(bf16[132,1536]{1,0:T(8,128)(2,1)S(1)} %collective-permute-done.refs_2_), channel_id=1, source_target_pairs={{0,128},{128,256},{256,384},{384,0},{1,129},{129,257},{257,385},{3... | collective-permute-start | bytes 1216520 | tf_op jit(solution)/shard_map/ppermute | solution.py:94
  95.2 2.7 %collective-permute-done.2.refs_4_ = bf16[132,1536]{1,0:T(8,128)(2,1)S(1)} collective-permute-done((bf16[132,1536]{1,0:T(8,128)(2,1)S(1)}, bf16[132,1536]{1,0:T(8,128)(2,1)S(1)}, u32[]{:S(2)}, u32[]{:S(2)}) %collective-permute-start.2) | collective-permute-done | bytes 405536 | tf_op jit(solution)/shard_map/ppermute | solution.py:94
  97.9 2.2 %collective-permute-start.3 = (bf16[132,1536]{1,0:T(8,128)(2,1)S(1)}, bf16[132,1536]{1,0:T(8,128)(2,1)S(1)}, u32[]{:S(2)}, u32[]{:S(2)}) collective-permute-start(bf16[132,1536]{1,0:T(8,128)(2,1)S(1)} %collective-permute-done.2.refs_4_), channel_id=1, source_target_pairs={{0,384},{128,0},{256,128},{384,256},{1,385},{129,1},{257,129},{385... | collective-permute-start | bytes 1216520 | tf_op jit(solution)/shard_map/ppermute | solution.py:94
  100.2 6.7 %collective-permute-done.4.refs_1_ = bf16[132,1536]{1,0:T(8,128)(2,1)S(1)} collective-permute-done((bf16[132,1536]{1,0:T(8,128)(2,1)S(1)}, bf16[132,1536]{1,0:T(8,128)(2,1)S(1)}, u32[]{:S(2)}, u32[]{:S(2)}) %collective-permute-start.4) | collective-permute-done | bytes 405536 | tf_op jit(solution)/shard_map/ppermute | solution.py:94
  106.9 0.0 collective-permute-done.5.refs_5_
  106.9 0.0 all-gather.4.cloned.1.call-done
  106.9 7.0 %shard_map.19 = (bf16[1056,3072]{1,0:T(8,128)(2,1)S(1)}, f32[3,132,1056]{2,1,0:T(8,128)S(1)}) custom-call(bf16[132,1536]{1,0:T(8,128)(2,1)S(1)} %get-tuple-element.14.refs_0_, bf16[132,1536]{1,0:T(8,128)(2,1)S(1)} %collective-permute-done.4.refs_1_, bf16[132,1536]{1,0:T(8,128)(2,1)S(1)} %collective-permute-done.refs_2_, ...), custom_call_target="tpu_custom_call" | custom-call | flops 2569273344 | bytes 14000000 | tf_op jit(solution)/shard_map/pallas_call | solution.py:188
  113.9 0.0 collective-permute-done.1.first
  113.9 0.0 collective-permute-done.3.second
  114.0 3.8 %shard_map.20 = f32[33,16,1056]{2,1,0:T(8,128)} custom-call(s32[1]{0:T(128)} %bitcast.place, bf16[132,1536]{1,0:T(8,128)(2,1)S(1)} %collective-permute-done.1.first, bf16[132,1536]{1,0:T(8,128)(2,1)S(1)} %collective-permute-done.3.second, bf16[1056,3072]{1,0:T(8,128)(2,1)S(1)} %get-tuple-element.11.block, f32[3,132,1056]{2,1,0:T(8,128)S(1)} %get-tuple-element.12.near), custom_call_target="tpu_custom_call" | custom-call | flops 856424448 | bytes 8000000 | tf_op jit(solution)/shard_map/pallas_call | solution.py:214
  (2 shorter events, 0.1 us)
Async XLA Ops:
  6.5 100.4 %all-gather.4.cloned.1.call-start = ((), (), s32[]{:S(2)}) async-start(), calls=%async_computation.1 | async-start | bytes 6963200 | tf_op jit(solution)/shard_map/all_gather | solution.py:234
  6.5 1.0 copy-start
  79.9 12.9 %collective-permute-start = (bf16[132,1536]{1,0:T(8,128)(2,1)S(1)}, bf16[132,1536]{1,0:T(8,128)(2,1)S(1)}, u32[]{:S(2)}, u32[]{:S(2)}) collective-permute-start(bf16[132,1536]{1,0:T(8,128)(2,1)S(1)} %get-tuple-element.14.refs_0_), channel_id=1, source_target_pairs={{0,128},{128,256},{256,384},{384,0},{1,129},{129,257},{257,385},{3... | collective-permute-start | bytes 1216520 | tf_op jit(solution)/shard_map/ppermute | solution.py:94
  82.3 15.7 %collective-permute-start.2 = (bf16[132,1536]{1,0:T(8,128)(2,1)S(1)}, bf16[132,1536]{1,0:T(8,128)(2,1)S(1)}, u32[]{:S(2)}, u32[]{:S(2)}) collective-permute-start(bf16[132,1536]{1,0:T(8,128)(2,1)S(1)} %get-tuple-element.13.refs_3_), channel_id=1, source_target_pairs={{0,384},{128,0},{256,128},{384,256},{1,385},{129,1},{257,129},{385... | collective-permute-start | bytes 1216520 | tf_op jit(solution)/shard_map/ppermute | solution.py:94
  85.7 21.2 %collective-permute-start.4 = (bf16[132,1536]{1,0:T(8,128)(2,1)S(1)}, bf16[132,1536]{1,0:T(8,128)(2,1)S(1)}, u32[]{:S(2)}, u32[]{:S(2)}) collective-permute-start(bf16[132,1536]{1,0:T(8,128)(2,1)S(1)} %get-tuple-element.14.refs_0_), channel_id=1, source_target_pairs={{0,384},{128,0},{256,128},{384,256},{1,385},{129,1},{257,129},{385... | collective-permute-start | bytes 1216520 | tf_op jit(solution)/shard_map/ppermute | solution.py:94
  88.5 18.4 %collective-permute-start.5 = (bf16[132,1536]{1,0:T(8,128)(2,1)S(1)}, bf16[132,1536]{1,0:T(8,128)(2,1)S(1)}, u32[]{:S(2)}, u32[]{:S(2)}) collective-permute-start(bf16[132,1536]{1,0:T(8,128)(2,1)S(1)} %get-tuple-element.13.refs_3_), channel_id=1, source_target_pairs={{0,128},{128,256},{256,384},{384,0},{1,129},{129,257},{257,385},{3... | collective-permute-start | bytes 1216520 | tf_op jit(solution)/shard_map/ppermute | solution.py:94
  92.8 21.1 %collective-permute-start.1 = (bf16[132,1536]{1,0:T(8,128)(2,1)S(1)}, bf16[132,1536]{1,0:T(8,128)(2,1)S(1)}, u32[]{:S(2)}, u32[]{:S(2)}) collective-permute-start(bf16[132,1536]{1,0:T(8,128)(2,1)S(1)} %collective-permute-done.refs_2_), channel_id=1, source_target_pairs={{0,128},{128,256},{256,384},{384,0},{1,129},{129,257},{257,385},{3... | collective-permute-start | bytes 1216520 | tf_op jit(solution)/shard_map/ppermute | solution.py:94
  97.9 16.0 %collective-permute-start.3 = (bf16[132,1536]{1,0:T(8,128)(2,1)S(1)}, bf16[132,1536]{1,0:T(8,128)(2,1)S(1)}, u32[]{:S(2)}, u32[]{:S(2)}) collective-permute-start(bf16[132,1536]{1,0:T(8,128)(2,1)S(1)} %collective-permute-done.2.refs_4_), channel_id=1, source_target_pairs={{0,384},{128,0},{256,128},{384,256},{1,385},{129,1},{257,129},{385... | collective-permute-start | bytes 1216520 | tf_op jit(solution)/shard_map/ppermute | solution.py:94
Sparse Core Ops, SparseCore 0:
  57.4 48.0 all-gather.3
